TPU v7x, 32 devices: a whole 2x2x4 slice. The times are simulated.
32 devices in a mesh: band: 4 (over y, core), tm: 8 (over z, x).
Axes of the slice: x: 2, y: 2, z: 4, core: 2. Of those that a mesh axis runs over, the one named last changes fastest.
Arguments:
- tod: bfloat16 [4, 64, 65536], P('band', None, 'tm'), may hold values from -6 to 6
- filter_taps: bfloat16 [4, 64, 2049], P('band'), may hold values from -0.125 to 0.125
- det_weights: float32 [4, 64], P('band'), may hold values from -0.75 to 0.75
- owner: int32 [4, 512, 1], P('band', 'tm'), may hold values from 0 to 7; in each aligned block of 64 rows (0 to 63, 64 to 127, ..., all dimensions but the last counted through in order) at most 32 rows name the same one
- tile_row: int32 [4, 512], P('band', 'tm'), may hold values from 0 to 127
- block_counts: int32 [4, 8], P('band', 'tm'), may hold values from 32 to 64, as said below
- beam_rows: float32 [4, 2, 33], P('band'), may hold values from -1 to 1
- beam_cols: float32 [4, 2, 33], P('band'), may hold values from -1 to 1
- mixing: float32 [4, 4, 2], P(None, 'band'), may hold values from -2 to 2
Outputs:
- components: float32 [4, 8, 128, 128], P(None, 'tm', 'band')
Inputs may be any that keep to these rules, and one draw needn't show every extreme that they name: The owner of each scan block; among the 64 scan blocks of one time shard of one band at most 32 share an owner, and in every draw some time shard sends exactly 32 to one owner. A time shard keeps its first block_counts scan blocks, the rest carry nothing; the largest value is reached in every draw.
All inputs are finite; a program needn't handle non-finite values.
Results may differ from a plain program's by a relative error of at most 0.0003.
Values may be sent and summed in bfloat16 or wider, within the bound.
No kernel may reach another device: no remote copies, remote signals or barrier semaphores. Data moves between devices by JAX's collectives and lax.ppermute only.
A program may use at most 128 MiB of HBM per device.

v0:
```python
import math

import jax
import jax.numpy as jnp
from jax import lax
from jax.sharding import PartitionSpec as P

PIX = 128
TROWS = 128


def with_halo(array, sides, width):
    for axis, dim in sides:
        count, length = (lax.axis_size(axis), array.shape[dim])
        up = [(i, (i + 1) % count) for i in range(count - 1)]
        down = [(j, i) for i, j in up]
        last = lax.slice_in_dim(array, length - width, length, axis=dim)
        leading = lax.slice_in_dim(array, 0, width, axis=dim)
        before = lax.ppermute(last, axis, up)
        after = lax.ppermute(leading, axis, down)
        array = jnp.concatenate([before, array, after], axis=dim)
    return array


def toeplitz_rows(tap_row, seg_len):
    taps = tap_row.shape[0]
    width = seg_len + taps - 1
    padded_taps = jnp.concatenate([tap_row, jnp.zeros((seg_len,), tap_row.dtype)])
    tiled = jnp.tile(padded_taps, seg_len)[: seg_len * width]
    return tiled.reshape(seg_len, width)


def filter_group(group_args):
    padded_group, tap_group = group_args
    half_len = (tap_group.shape[1] - 1) // 2
    seg_len = math.gcd(half_len, 128)
    reach_pieces = 2 * half_len // seg_len
    group_size = padded_group.shape[0]
    segments = (padded_group.shape[1] - 2 * half_len) // seg_len
    pieces = padded_group.reshape(group_size, segments + reach_pieces, seg_len)
    windows = jnp.concatenate(
        [pieces[:, shift : shift + segments] for shift in range(reach_pieces + 1)], axis=2
    )
    tables = jax.vmap(lambda tap_row: toeplitz_rows(tap_row, seg_len))(tap_group)
    product = lax.dot_general(
        windows, tables, (((2,), (2,)), ((0,), (0,))), preferred_element_type=jnp.float32
    )
    return product.reshape(group_size, segments * seg_len)


def band_matrix(profiles, out_size, in_size, offset):
    width = profiles.shape[1]
    spread = lax.iota(jnp.int32, in_size)[None, :] - lax.iota(jnp.int32, out_size)[:, None] + offset
    picks = (spread[None, :, :] == lax.iota(jnp.int32, width)[:, None, None]).astype(jnp.float32)
    return jnp.einsum("ka,arq->krq", profiles, picks, precision=lax.Precision.HIGHEST)


def on_device(
    tod, filter_taps, det_weights, owner, tile_row, block_counts, beam_rows, beam_cols, mixing
):
    tap_rows = filter_taps[0]
    half_len = (tap_rows.shape[1] - 1) // 2
    detectors = tod.shape[1]
    samples = tod.shape[2]
    group_size = math.gcd(detectors, 16)
    padded = with_halo(tod, (("tm", 2),), half_len)[0]
    padded = padded.reshape(detectors // group_size, group_size, samples + 2 * half_len)
    grouped_taps = tap_rows.reshape(detectors // group_size, group_size, tap_rows.shape[1])
    filtered = lax.map(filter_group, (padded, grouped_taps))
    filtered = filtered.reshape(detectors, samples)
    weighted = jnp.dot(
        det_weights[0],
        filtered,
        precision=lax.Precision.HIGHEST,
        preferred_element_type=jnp.float32,
    )
    blocks_here = samples // PIX
    block_vals = weighted.reshape(blocks_here, PIX)
    valid_mask = (lax.iota(jnp.int32, blocks_here) < block_counts[0, 0]).astype(jnp.float32)
    block_vals = block_vals * valid_mask[:, None]
    owners = owner[0, :, 0]
    pixel_rows = tile_row[0]
    shards = lax.axis_size("tm")
    capacity = 4 * blocks_here // shards
    owner_hits = (owners[:, None] == lax.iota(jnp.int32, shards)[None, :]).astype(jnp.int32)
    earlier = jnp.cumsum(owner_hits, axis=0) - owner_hits
    ranking = jnp.sum(earlier * owner_hits, axis=1)
    slot_ids = owners * capacity + ranking
    placing = slot_ids[None, :] == lax.iota(jnp.int32, shards * capacity)[:, None]
    send_vals = jnp.dot(
        placing.astype(jnp.float32),
        block_vals,
        precision=lax.Precision.HIGHEST,
        preferred_element_type=jnp.float32,
    )
    send_rows = jnp.sum(placing.astype(jnp.int32) * (pixel_rows + 1)[None, :], axis=1)
    send_vals = send_vals.reshape(shards, capacity, PIX)
    send_rows = send_rows.reshape(shards, capacity)
    recv_vals, recv_rows = (
        lax.all_to_all(send_vals, "tm", split_axis=0, concat_axis=0, tiled=True),
        lax.all_to_all(send_rows, "tm", split_axis=0, concat_axis=0, tiled=True),
    )
    recv_vals = recv_vals.reshape(shards * capacity, PIX)
    recv_rows = recv_rows.reshape(shards * capacity) - 1
    landing = (recv_rows[None, :] == lax.iota(jnp.int32, TROWS)[:, None]).astype(jnp.float32)
    tile = jnp.dot(
        landing, recv_vals, precision=lax.Precision.HIGHEST, preferred_element_type=jnp.float32
    )
    beam_reach = (beam_rows.shape[2] - 1) // 2
    extended = with_halo(tile, (("tm", 0),), beam_reach)
    row_mats = band_matrix(beam_rows[0], TROWS, TROWS + 2 * beam_reach, 0)
    col_mats = band_matrix(beam_cols[0], PIX, PIX, beam_reach)
    rowed = jnp.einsum("krq,qc->krc", row_mats, extended, precision=lax.Precision.HIGHEST)
    beamed = jnp.einsum("krc,kxc->krx", rowed, col_mats, precision=lax.Precision.HIGHEST)
    local_mix = jnp.einsum("ck,krx->crx", mixing[:, 0, :], beamed, precision=lax.Precision.HIGHEST)
    total = lax.psum(local_mix, "band")
    share = TROWS // lax.axis_size("band")
    mine = lax.dynamic_slice_in_dim(total, lax.axis_index("band") * share, share, 1)
    return mine[:, None]


def solution(mesh):
    placed = (
        P("band", None, "tm"),
        P("band", None, None),
        P("band", None),
        P("band", "tm", None),
        P("band", "tm"),
        P("band", "tm"),
        P("band", None, None),
        P("band", None, None),
        P(None, "band", None),
    )
    return jax.shard_map(
        on_device,
        mesh=mesh,
        in_specs=placed,
        out_specs=P(None, "tm", "band", None),
        check_vma=False,
    )
```

profile of v0, /device:TPU:0, one launch (start us, length us, event | category | flops | bytes accessed | tf_op | source)
XLA Modules:
  0.0 315.3 jit_solution(13477389704360329185)
XLA Ops:
  6.5 1.0 fusion.30
  7.5 4.8 %collective-permute-start = (bf16[1,64,1024]{2,1,0:T(8,128)(2,1)S(1)}, bf16[1,64,1024]{2,1,0:T(8,128)(2,1)S(1)}, u32[]{:S(2)}, u32[]{:S(2)}) collective-permute-start(bf16[1,64,1024]{2,1,0:T(8,128)(2,1)S(1)} %get-tuple-element.36), channel_id=1, source_target_pairs={{0,1},{1,2},{2,3},{3,4},{4,5},{5,6},{6,7},{8,9},{9,10},{10,11},{11... | collective-permute-start | bytes 393224 | tf_op jit(solution)/shard_map/ppermute | solution.py:19
  12.4 1.3 collective-permute-start.1
  17.5 7.0 %all-to-all-start = ((s32[8,1,32]{2,1,0:T(1,128)}), s32[8,1,32]{2,1,0:T(1,128)S(1)}, u32[]{:S(2)}, u32[]{:S(2)}) async-start(s32[8,1,32]{2,1,0:T(1,128)} %all_to_all.9), calls=%async_computation | async-start | bytes 8192 | tf_op jit(solution)/shard_map/all_to_all | solution.py:101
  25.1 1.3 pad_maximum_fusion
  26.5 221.9 %while.10 = (s32[]{:T(128)}, f32[4,16,8192]{2,1,0:T(8,128)}, bf16[4,16,10240]{2,1,0:T(8,128)(2,1)S(1)}, bf16[4,16,2049]{2,1,0:T(8,128)(2,1)}, s32[]{:T(128)}, /*index=5*/bf16[]{:T(256)}) while((s32[]{:T(128)}, f32[4,16,8192]{2,1,0:T(8,128)}, bf16[4,16,10240]{2,1,0:T(8,128)(2,1)S(1)}, bf16[4,16,2049]{2,1,0:T(8,128)(2,1)}, s32[]{:T(128)}, ...), condition=%wide.region_4.5_spmd, body=%wide.region_3.4_spmd.sunk | while | flops 570425344 | bytes 106779400 | solution.py:69
  28.5 2.1 copy-done.1
  30.6 0.9 dynamic-slice_bitcast_fusion.6
  31.5 4.2 %tile.11 = bf16[16,128,2177]{2,1,0:T(8,128)(2,1)} broadcast(bf16[16,2177]{1,0:T(8,128)(2,1)S(1)} %concatenate.15), dimensions={0,2} | broadcast | bytes 8986656 | tf_op jit(solution)/shard_map/while/body/eval_jaxpr/vmap()/tile | solution.py:29
  35.7 21.2 %tile.12 = bf16[16,278656]{1,0:T(8,128)(2,1)} reshape(bf16[16,128,2177]{2,1,0:T(8,128)(2,1)} %tile.11) | data formatting | bytes 17833984 | tf_op jit(solution)/shard_map/while/body/eval_jaxpr/vmap()/tile | solution.py:29
  56.9 7.4 %slice.146 = bf16[16,278528]{1,0:T(8,128)(2,1)} slice(bf16[16,278656]{1,0:T(8,128)(2,1)} %tile.12), slice={[0:16], [0:278528]} | slice | bytes 17825792 | tf_op jit(solution)/shard_map/while/body/eval_jaxpr/vmap()/slice | solution.py:29
  64.4 8.5 %copy.30 = bf16[2,8,128,2176]{3,2,1,0:T(8,128)(2,1)} copy(bf16[2,8,128,2176]{3,1,2,0:T(8,128)(2,1)} %bitcast.92) | data formatting | bytes 17825792 | tf_op jit(solution)/shard_map/while
  72.9 8.2 %fusion.43 = f32[16,64,128]{2,1,0:T(8,128)S(1)} fusion(bf16[16,64,2176]{2,1,0:T(8,128)(2,1)} %copy-done.1, bf16[16,128,2176]{2,1,0:T(8,128)(2,1)} %bitcast.93), kind=kOutput, calls=%fused_computation.71.clone.1 | convolution fusion | flops 570425344 | bytes 13893632 | tf_op jit(solution)/shard_map/while/body/eval_jaxpr/dot_general | solution.py:45
  81.1 0.9 constant_dynamic-update-slice_fusion.2
  84.0 2.1 copy-done.1
  86.1 0.9 dynamic-slice_bitcast_fusion.6
  87.0 4.2 %tile.11 = bf16[16,128,2177]{2,1,0:T(8,128)(2,1)} broadcast(bf16[16,2177]{1,0:T(8,128)(2,1)S(1)} %concatenate.15), dimensions={0,2} | broadcast | bytes 8986656 | tf_op jit(solution)/shard_map/while/body/eval_jaxpr/vmap()/tile | solution.py:29
  91.2 21.2 %tile.12 = bf16[16,278656]{1,0:T(8,128)(2,1)} reshape(bf16[16,128,2177]{2,1,0:T(8,128)(2,1)} %tile.11) | data formatting | bytes 17833984 | tf_op jit(solution)/shard_map/while/body/eval_jaxpr/vmap()/tile | solution.py:29
  112.4 7.4 %slice.146 = bf16[16,278528]{1,0:T(8,128)(2,1)} slice(bf16[16,278656]{1,0:T(8,128)(2,1)} %tile.12), slice={[0:16], [0:278528]} | slice | bytes 17825792 | tf_op jit(solution)/shard_map/while/body/eval_jaxpr/vmap()/slice | solution.py:29
  119.9 8.5 %copy.30 = bf16[2,8,128,2176]{3,2,1,0:T(8,128)(2,1)} copy(bf16[2,8,128,2176]{3,1,2,0:T(8,128)(2,1)} %bitcast.92) | data formatting | bytes 17825792 | tf_op jit(solution)/shard_map/while
  128.3 8.2 %fusion.43 = f32[16,64,128]{2,1,0:T(8,128)S(1)} fusion(bf16[16,64,2176]{2,1,0:T(8,128)(2,1)} %copy-done.1, bf16[16,128,2176]{2,1,0:T(8,128)(2,1)} %bitcast.93), kind=kOutput, calls=%fused_computation.71.clone.1 | convolution fusion | flops 570425344 | bytes 13893632 | tf_op jit(solution)/shard_map/while/body/eval_jaxpr/dot_general | solution.py:45
  139.4 2.1 copy-done.1
  141.5 0.9 dynamic-slice_bitcast_fusion.6
  142.4 4.2 %tile.11 = bf16[16,128,2177]{2,1,0:T(8,128)(2,1)} broadcast(bf16[16,2177]{1,0:T(8,128)(2,1)S(1)} %concatenate.15), dimensions={0,2} | broadcast | bytes 8986656 | tf_op jit(solution)/shard_map/while/body/eval_jaxpr/vmap()/tile | solution.py:29
  146.7 21.2 %tile.12 = bf16[16,278656]{1,0:T(8,128)(2,1)} reshape(bf16[16,128,2177]{2,1,0:T(8,128)(2,1)} %tile.11) | data formatting | bytes 17833984 | tf_op jit(solution)/shard_map/while/body/eval_jaxpr/vmap()/tile | solution.py:29
  167.9 7.4 %slice.146 = bf16[16,278528]{1,0:T(8,128)(2,1)} slice(bf16[16,278656]{1,0:T(8,128)(2,1)} %tile.12), slice={[0:16], [0:278528]} | slice | bytes 17825792 | tf_op jit(solution)/shard_map/while/body/eval_jaxpr/vmap()/slice | solution.py:29
  175.3 8.5 %copy.30 = bf16[2,8,128,2176]{3,2,1,0:T(8,128)(2,1)} copy(bf16[2,8,128,2176]{3,1,2,0:T(8,128)(2,1)} %bitcast.92) | data formatting | bytes 17825792 | tf_op jit(solution)/shard_map/while
  183.8 8.2 %fusion.43 = f32[16,64,128]{2,1,0:T(8,128)S(1)} fusion(bf16[16,64,2176]{2,1,0:T(8,128)(2,1)} %copy-done.1, bf16[16,128,2176]{2,1,0:T(8,128)(2,1)} %bitcast.93), kind=kOutput, calls=%fused_computation.71.clone.1 | convolution fusion | flops 570425344 | bytes 13893632 | tf_op jit(solution)/shard_map/while/body/eval_jaxpr/dot_general | solution.py:45
  192.1 0.8 constant_dynamic-update-slice_fusion.2
  194.9 2.1 copy-done.1
  197.0 0.9 dynamic-slice_bitcast_fusion.6
  197.9 4.2 %tile.11 = bf16[16,128,2177]{2,1,0:T(8,128)(2,1)} broadcast(bf16[16,2177]{1,0:T(8,128)(2,1)S(1)} %concatenate.15), dimensions={0,2} | broadcast | bytes 8986656 | tf_op jit(solution)/shard_map/while/body/eval_jaxpr/vmap()/tile | solution.py:29
  202.1 21.2 %tile.12 = bf16[16,278656]{1,0:T(8,128)(2,1)} reshape(bf16[16,128,2177]{2,1,0:T(8,128)(2,1)} %tile.11) | data formatting | bytes 17833984 | tf_op jit(solution)/shard_map/while/body/eval_jaxpr/vmap()/tile | solution.py:29
  223.3 7.4 %slice.146 = bf16[16,278528]{1,0:T(8,128)(2,1)} slice(bf16[16,278656]{1,0:T(8,128)(2,1)} %tile.12), slice={[0:16], [0:278528]} | slice | bytes 17825792 | tf_op jit(solution)/shard_map/while/body/eval_jaxpr/vmap()/slice | solution.py:29
  230.8 8.5 %copy.30 = bf16[2,8,128,2176]{3,2,1,0:T(8,128)(2,1)} copy(bf16[2,8,128,2176]{3,1,2,0:T(8,128)(2,1)} %bitcast.92) | data formatting | bytes 17825792 | tf_op jit(solution)/shard_map/while
  239.3 8.2 %fusion.43 = f32[16,64,128]{2,1,0:T(8,128)S(1)} fusion(bf16[16,64,2176]{2,1,0:T(8,128)(2,1)} %copy-done.1, bf16[16,128,2176]{2,1,0:T(8,128)(2,1)} %bitcast.93), kind=kOutput, calls=%fused_computation.71.clone.1 | convolution fusion | flops 570425344 | bytes 13893632 | tf_op jit(solution)/shard_map/while/body/eval_jaxpr/dot_general | solution.py:45
  248.4 2.8 fusion.27
  251.2 0.9 fusion.12
  252.1 6.0 %all-to-all-start.1 = ((f32[8,32,128]{2,1,0:T(8,128)}), f32[8,32,128]{2,1,0:T(8,128)S(1)}, u32[]{:S(2)}, u32[]{:S(2)}) async-start(f32[8,32,128]{2,1,0:T(8,128)} %fusion.12), calls=%async_computation.1 | async-start | bytes 262144 | tf_op jit(solution)/shard_map/all_to_all | solution.py:100
  258.1 1.9 fusion.4
  260.1 5.3 %all-to-all-done.1 = f32[8,32,128]{2,1,0:T(8,128)S(1)} async-done(((f32[8,32,128]{2,1,0:T(8,128)}), f32[8,32,128]{2,1,0:T(8,128)S(1)}, u32[]{:S(2)}, u32[]{:S(2)}) %all-to-all-start.1) | async-done | bytes 131104 | tf_op jit(solution)/shard_map/all_to_all | solution.py:100
  265.7 2.1 collective-permute-start.2
  267.8 1.3 collective-permute-start.3
  269.1 1.0 fusion.5
  270.1 3.3 %collective-permute-done.3 = f32[16,128]{1,0:T(8,128)S(1)} collective-permute-done((f32[16,128]{1,0:T(8,128)S(1)}, f32[16,128]{1,0:T(8,128)S(1)}, u32[]{:S(2)}, u32[]{:S(2)}) %collective-permute-start.3) | collective-permute-done | bytes 8224 | tf_op jit(solution)/shard_map/ppermute | solution.py:20
  274.1 1.3 convolution_bitcast_fusion
  275.5 31.6 %all-reduce.3.cloned.1.call-done = f32[4,128,128]{2,0,1:T(4,128)} async-done(((f32[4,128,128]{2,0,1:T(4,128)}), f32[4,128,128]{2,0,1:T(4,128)}) %all-reduce.3.cloned.1.call-update) | async-done | bytes 262160 | tf_op jit(solution)/shard_map/psum | solution.py:116
  307.0 0.8 dynamic-slice_bitcast_fusion.2
  (123 shorter events, 15.2 us)
Async XLA Ops:
  6.5 267.6 %copy-start = (f32[4,1,2]{0,2,1:T(2,128)S(1)}, f32[4,1,2]{0,2,1:T(2,128)}, u32[]{:S(2)}) copy-start(f32[4,1,2]{0,2,1:T(2,128)} %param.19) | copy-start | bytes 100
  7.5 17.6 %collective-permute-start = (bf16[1,64,1024]{2,1,0:T(8,128)(2,1)S(1)}, bf16[1,64,1024]{2,1,0:T(8,128)(2,1)S(1)}, u32[]{:S(2)}, u32[]{:S(2)}) collective-permute-start(bf16[1,64,1024]{2,1,0:T(8,128)(2,1)S(1)} %get-tuple-element.36), channel_id=1, source_target_pairs={{0,1},{1,2},{2,3},{3,4},{4,5},{5,6},{6,7},{8,9},{9,10},{10,11},{11... | collective-permute-start | bytes 393224 | tf_op jit(solution)/shard_map/ppermute | solution.py:19
  12.4 12.7 %collective-permute-start.1 = (bf16[1,64,1024]{2,1,0:T(8,128)(2,1)S(1)}, bf16[1,64,1024]{2,1,0:T(8,128)(2,1)S(1)}, u32[]{:S(2)}, u32[]{:S(2)}) collective-permute-start(bf16[1,64,1024]{2,1,0:T(8,128)(2,1)S(1)} %get-tuple-element.37), channel_id=1, source_target_pairs={{1,0},{2,1},{3,2},{4,3},{5,4},{6,5},{7,6},{9,8},{10,9},{11,10},{12... | collective-permute-start | bytes 393224 | tf_op jit(solution)/shard_map/ppermute | solution.py:20
  17.5 234.6 %all-to-all-start = ((s32[8,1,32]{2,1,0:T(1,128)}), s32[8,1,32]{2,1,0:T(1,128)S(1)}, u32[]{:S(2)}, u32[]{:S(2)}) async-start(s32[8,1,32]{2,1,0:T(1,128)} %all_to_all.9), calls=%async_computation | async-start | bytes 8192 | tf_op jit(solution)/shard_map/all_to_all | solution.py:101
  26.5 221.9 %copy-start.2 = (f32[1,64]{1,0:T(1,128)S(1)}, f32[1,64]{1,0:T(1,128)}, u32[]{:S(2)}) copy-start(f32[1,64]{1,0:T(1,128)} %param.13) | copy-start | bytes 772
  26.5 231.6 %copy-start.3 = (f32[1,2,33]{2,1,0:T(2,128)S(1)}, f32[1,2,33]{2,1,0:T(2,128)}, u32[]{:S(2)}) copy-start(f32[1,2,33]{2,1,0:T(2,128)} %param.17) | copy-start | bytes 796
  26.5 242.6 %copy-start.4 = (f32[1,2,33]{2,1,0:T(2,128)S(1)}, f32[1,2,33]{2,1,0:T(2,128)}, u32[]{:S(2)}) copy-start(f32[1,2,33]{2,1,0:T(2,128)} %param.18) | copy-start | bytes 796
  28.5 2.1 copy-start.1
  84.0 2.1 copy-start.1
  139.4 2.1 copy-start.1
  194.9 2.1 copy-start.1
  252.1 13.3 %all-to-all-start.1 = ((f32[8,32,128]{2,1,0:T(8,128)}), f32[8,32,128]{2,1,0:T(8,128)S(1)}, u32[]{:S(2)}, u32[]{:S(2)}) async-start(f32[8,32,128]{2,1,0:T(8,128)} %fusion.12), calls=%async_computation.1 | async-start | bytes 262144 | tf_op jit(solution)/shard_map/all_to_all | solution.py:100
  258.1 48.9 %all-reduce.3.cloned.1.call-start = ((), (), s32[]{:S(2)}) async-start(), calls=%async_computation.2 | async-start | bytes 524288 | tf_op jit(solution)/shard_map/psum | solution.py:116
  265.7 4.4 %collective-permute-start.2 = (f32[16,128]{1,0:T(8,128)S(1)}, f32[16,128]{1,0:T(8,128)S(1)}, u32[]{:S(2)}, u32[]{:S(2)}) collective-permute-start(f32[16,128]{1,0:T(8,128)S(1)} %get-tuple-element.38), channel_id=1, source_target_pairs={{0,1},{1,2},{2,3},{3,4},{4,5},{5,6},{6,7},{8,9},{9,10},{10,11},{11... | collective-permute-start | bytes 24584 | tf_op jit(solution)/shard_map/ppermute | solution.py:19
  267.8 5.5 %collective-permute-start.3 = (f32[16,128]{1,0:T(8,128)S(1)}, f32[16,128]{1,0:T(8,128)S(1)}, u32[]{:S(2)}, u32[]{:S(2)}) collective-permute-start(f32[16,128]{1,0:T(8,128)S(1)} %get-tuple-element.39), channel_id=1, source_target_pairs={{1,0},{2,1},{3,2},{4,3},{5,4},{6,5},{7,6},{9,8},{10,9},{11,10},{12... | collective-permute-start | bytes 24584 | tf_op jit(solution)/shard_map/ppermute | solution.py:20
Sparse Core Ops, SparseCore 0:
  275.6 31.4 all-reduce.2
where the time goes:
time: 317 us; the launch traced here: 315 us
  local copies, waits for them, and re-layouts  192 us (61%)
  matrix products  41.5 us (13%)
  waiting for transfers between devices  40.1 us (13%)
  starting transfers between devices  22.5 us (7%)
  between operations  14.2 us (4%)
  other arithmetic  4.45 us (1%)
    another operation x8, local copies, waits for them, and re-layouts, toeplitz_rows(): tiled = jnp.tile(padded_taps, seg_len)[:seg_len * width]  102 us
    while x84, local copies, waits for them, and re-layouts  49.5 us
    dot_general x4, matrix products, filter_group(): lax.dot_general(windows, tables, (((2,), (2,)), ((0,), (0,))), preferred_...  32.6 us
    psum x1, waiting for transfers between devices, on_device(): total = lax.psum(local_mix, 'band')  31.6 us
    slice x4, local copies, waits for them, and re-layouts, toeplitz_rows(): tiled = jnp.tile(padded_taps, seg_len)[:seg_len * width]  29.8 us
    ppermute x2, starting transfers between devices, with_halo(): before = lax.ppermute(last, axis, up)  6.97 us
    all_to_all x1, starting transfers between devices, on_device(): lax.all_to_all(send_rows, 'tm', split_axis=0, concat_axis=0, tiled=True)  6.96 us
  transfers between devices with their start and end apart: 7, of which 3 were waited for; matrix products, arithmetic and copies ran while one was open for 71% of the time, Pallas kernels for 0%

commit v1 on v0

v1 whole, which is shorter than its diff:
```python
import functools

import jax
import jax.numpy as jnp
from jax import lax
from jax.experimental import pallas as pl
from jax.experimental.pallas import tpu as pltpu
from jax.sharding import PartitionSpec as P

L = 128
TROWS = 128
A = 8
R = 16
STEP = 64
GROUP = 704
UNROLL = 8
MARGIN = 8
VMEM = pl.BlockSpec(memory_space=pltpu.VMEM)
SMEM = pl.BlockSpec(memory_space=pltpu.SMEM)
PARAMS = pltpu.CompilerParams(vmem_limit_bytes=48 * 2**20)
F32, BF16 = jnp.float32, jnp.bfloat16


class Plan:
    def __init__(self, detectors, samples, taps):
        self.detectors, self.taps = detectors, taps
        self.shifts = L // STEP
        self.pieces = -(-(GROUP + STEP - 1) // L)
        self.groups = -(-taps // GROUP)
        self.blocks = samples // L
        self.lead = -(-((GROUP + STEP - 2) // STEP) // self.shifts)
        self.cols = -(-(self.blocks + self.lead) // A)
        self.reads = self.cols + self.pieces - 1
        self.stored = self.cols * (A - 1) + self.reads
        self.reach = (taps - 1) // 2 // L
        self.whole = (taps - 1) // L
        self.rows = self.shifts * self.cols * A
        self.width = STEP * self.groups
        self.lanes = -(-self.width // L)
        self.out = self.blocks + 2 * self.reach


def filter_kernel(
    weights, tod, taps, owner, tile_row, counts, out, shifted, tap_rows, table, acc, unmixed, line, *, plan
):
    nd, nb, lead = plan.detectors, plan.blocks, plan.lead
    lane_d = lax.broadcasted_iota(jnp.int32, (nd, L), 1)
    none = jnp.zeros((nd, L), BF16)

    def tile(g):
        return tod[0, :, g * L : (g + 1) * L] if 0 <= g < nb else none

    for q in range(plan.shifts):
        for i in range(plan.stored):
            g = i - lead
            piece = none
            if 0 <= g < nb or (q > 0 and g == -1):
                piece = tile(g)
                if q > 0:
                    piece = jnp.where(lane_d >= STEP * q, piece, tile(g + 1))
                    piece = pltpu.roll(piece, L - STEP * q, 1)
            shifted[q, i * nd : (i + 1) * nd, :] = piece.astype(F32)
    whole = plan.whole
    for i in range(whole):
        tap_rows[i * nd : (i + 1) * nd, :] = taps[0, :, i * L : (i + 1) * L].astype(F32)
    last = jnp.broadcast_to(taps[0, :, whole * L : whole * L + 1].astype(F32), (nd, L))
    tap_rows[whole * nd : (whole + 1) * nd, :] = jnp.where(lane_d == 0, last, 0.0)
    acc[...] = jnp.zeros_like(acc)
    table[...] = jnp.zeros_like(table)

    row8 = lax.broadcasted_iota(jnp.int32, (8, L), 0)
    lane8 = lax.broadcasted_iota(jnp.int32, (8, L), 1)
    row16 = lax.broadcasted_iota(jnp.int32, (R, L), 0)
    lane16 = lax.broadcasted_iota(jnp.int32, (R, L), 1)
    zero8 = jnp.zeros((8, L), F32)
    zero16 = jnp.zeros((R, L), BF16)

    def make_table(d, slot):
        low, high = [zero8], [zero8]
        for i in range(whole + 1):
            spread = jnp.broadcast_to(tap_rows[pl.ds(i * nd + d, 1), :], (8, L))
            low.append(pltpu.roll(spread, 0, 1, stride=1, stride_axis=0))
            high.append(pltpu.roll(spread, 8, 1, stride=1, stride_axis=0))
        base = {-1: zero16, whole + 1: zero16}
        for i in range(whole + 1):
            base[i] = jnp.concatenate(
                [
                    jnp.where(lane8 >= row8, low[i + 1], low[i]),
                    jnp.where(lane8 >= row8 + 8, high[i + 1], high[i]),
                ],
                axis=0,
            ).astype(BF16)
        for j in range(plan.groups):
            for g in range(STEP // R):
                for k in range(plan.pieces):
                    at = GROUP * j + L * k - R * g
                    i, r = at // L, at % L
                    if i > whole:
                        continue
                    piece = base[i]
                    if r:
                        piece = pltpu.roll(jnp.where(lane16 >= r, piece, base[i + 1]), L - r, 1)
                    if k == 0 and j > 0:
                        piece = jnp.where(lane16 >= row16 + R * g, piece, zero16)
                    if L * k + L + R * g > GROUP and j < plan.groups - 1:
                        piece = jnp.where(lane16 < row16 + (R * g + GROUP - L * k), piece, zero16)
                    table[slot, STEP * j + R * g : STEP * j + R * g + R, k * L : (k + 1) * L] = piece

    def apply_table(d, slot):
        rows = []
        for pair in range(plan.shifts // 2):
            reads = [
                jnp.concatenate(
                    [
                        shifted[2 * pair + side, pl.ds(c * nd + d, A, stride=plan.cols * nd), :]
                        for side in range(2)
                    ],
                    axis=0,
                ).astype(BF16)
                for c in range(plan.reads)
            ]
            for c in range(plan.cols):
                rows.append(jnp.concatenate(reads[c : c + plan.pieces], axis=1))
        windows = jnp.concatenate(rows, axis=0)
        product = lax.dot_general(
            windows, table[slot], (((1,), (1,)), ((), ())), preferred_element_type=F32
        )
        return product * weights[0, d]

    make_table(0, 0)

    def body(step, carry):
        total = None
        for k in range(UNROLL):
            d = UNROLL * step + k
            make_table(jnp.minimum(d + 1, nd - 1), (k + 1) % 2)
            part = apply_table(d, k % 2)
            total = part if total is None else total + part
        acc[...] += total
        return carry

    lax.fori_loop(0, nd // UNROLL, body, 0)

    span = plan.cols * A
    for pair in range(plan.shifts // 2):
        for c in range(plan.cols):
            for side in range(2):
                start = ((pair * plan.cols + c) * 2 + side) * A
                for v in range(plan.lanes):
                    wide = min(L, plan.width - v * L)
                    unmixed[v, pl.ds((2 * pair + side) * span + c, A, stride=plan.cols), 0:wide] = acc[
                        start : start + A, v * L : v * L + wide
                    ]
    line[...] = jnp.zeros_like(line)
    lanes = lax.broadcasted_iota(jnp.int32, (span, L), 1)
    for j in range(plan.groups):
        for q in range(plan.shifts):
            down, slot = divmod(q - (GROUP // STEP) * j, plan.shifts)
            v, start = divmod(STEP * j, L)
            part = unmixed[v, q * span : (q + 1) * span, :]
            turn = (STEP * slot - start) % L
            if turn:
                part = pltpu.roll(part, turn, 1)
            at = down - lead + 2 * plan.reach + MARGIN
            inside = (lanes >= STEP * slot) & (lanes < STEP * slot + STEP)
            line[at : at + span, :] += jnp.where(inside, part, 0.0)
    out[0 : plan.out, :] = line[MARGIN : MARGIN + plan.out, :]

    block = lax.broadcasted_iota(jnp.int32, (nb, L), 0)
    lane = lax.broadcasted_iota(jnp.int32, (nb, L), 1)
    owners = jnp.sum(jnp.where(block == lane, owner[0], 0), axis=0, keepdims=True)
    row = jnp.broadcast_to(jnp.pad(tile_row[...], ((0, 0), (0, L - nb))), (1, L))
    lane1 = lax.broadcasted_iota(jnp.int32, (1, L), 1)
    target = jnp.where(lane1 < counts[0, 0], owners * TROWS + row, -1)
    out[plan.out : plan.out + 8, :] = jnp.broadcast_to(target.astype(F32), (8, L))


def two_terms(x):
    high = x.astype(BF16)
    return high, (x - high.astype(F32)).astype(BF16)


def tile_kernel(
    near, far, beam_rows, beam_cols, mixing, out, marks, tile, *, plan, outer, inner, bands, reach
):
    part_rows = plan.out + 8
    me = lax.axis_index("tm")
    band = lax.axis_index("band")
    halo, nb = plan.reach, plan.blocks
    total = outer * inner
    marks[...] = jnp.full_like(marks, -1.0)
    parts = []
    for flip, ref in enumerate((near, far)[:inner]):
        for k in range(outer):
            t = jnp.bitwise_xor(me, k * inner + flip)
            parts.append((t, ref, k * part_rows))
            marks[pl.ds(8 + t, 1), :] = ref[k * part_rows + plan.out : k * part_rows + plan.out + 1, :]
    here = marks[8 : 8 + total, :]
    before = marks[7 : 7 + total, :]
    after = marks[9 : 9 + total, :]
    lane = lax.broadcasted_iota(jnp.int32, (total, L), 1)
    target = jnp.where(lane < halo, pltpu.roll(before, (halo - nb) % L, 1), pltpu.roll(here, halo, 1))
    target = jnp.where(lane >= halo + nb, pltpu.roll(after, halo + nb, 1), target)
    target = jnp.where(lane < plan.out, target, -1.0)
    marks[8 : 8 + total, :] = target
    ext = TROWS + 2 * reach
    first = (me * TROWS - reach).astype(F32)
    row = lax.broadcasted_iota(jnp.int32, (ext, L), 0).astype(F32) + first
    row = jnp.where(row < 0, -2.0, row)
    result = None
    for t, ref, start in parts:
        picks = (jnp.broadcast_to(marks[pl.ds(8 + t, 1), :], (ext, L)) == row).astype(F32)
        high, low = two_terms(ref[start : start + plan.out, :])
        both = jnp.concatenate([high, low], axis=1)
        got = jnp.dot(picks[:, : plan.out].astype(BF16), both, preferred_element_type=F32)
        result = got if result is None else result + got
    tile[...] = result[:, :L] + result[:, L:]
    share = TROWS // bands
    wide = 2 * share + 2 * reach
    mine = band // 2
    for h in range(bands // 2):
        pair = jnp.bitwise_xor(mine, h)
        start = pl.multiple_of(pair * (2 * share), 8)
        out[h, 0:wide, :] = tile[pl.ds(start, wide), :]
        taps = beam_rows.shape[2]
        for k in range(2):
            out[h, wide + k : wide + k + 1, :] = jnp.zeros((1, L), F32)
        out[h, wide : wide + 8, :] = jnp.zeros((8, L), F32)
        terms = beam_rows.shape[1]
        for k in range(terms):
            out[h, wide + k : wide + k + 1, 0:taps] = beam_rows[0, k : k + 1, :]
            out[h, wide + terms + k : wide + terms + k + 1, 0:taps] = beam_cols[0, k : k + 1, :]
        comps = mixing.shape[0]
        for c in range(comps):
            out[h, wide + 2 * terms + c // 4 : wide + 2 * terms + c // 4 + 1, 32 * (c % 4) : 32 * (c % 4) + terms] = mixing[
                c, 0:1, :
            ]


def dot3(a, b, dims):
    a0, a1 = two_terms(a)
    b0, b1 = two_terms(b)
    ka, kb = dims
    left = jnp.concatenate([a0, a0, a1], axis=ka)
    right = jnp.concatenate([b0, b1, b0], axis=kb)
    return lax.dot_general(left, right, (((ka,), (kb,)), ((), ())), preferred_element_type=F32)


def beam_kernel(*refs, share, reach, terms, comps, taps):
    ins, out = refs[:-1], refs[-1]
    core = lax.rem(lax.axis_index("band"), 2)
    wide = 2 * share + 2 * reach
    need = share + 2 * reach
    x = lax.broadcasted_iota(jnp.int32, (L, L), 0)
    c_in = lax.broadcasted_iota(jnp.int32, (L, L), 1)
    near = jnp.abs(c_in - x) <= reach
    totals = [None] * comps
    for ref in ins:
        for h in range(ref.shape[0]):
            rows = ref[h, pl.ds(pl.multiple_of(core * share, 8), need), :]
            mats = []
            for k in range(terms):
                spread = jnp.broadcast_to(ref[h, wide + k : wide + k + 1, :], (share, L))
                mats.append(pltpu.roll(spread, 0, 1, stride=1, stride_axis=0)[:, :need])
            rowed = dot3(jnp.concatenate(mats, axis=0), rows, (1, 0))
            for k in range(terms):
                at = wide + terms + k
                spread = jnp.broadcast_to(ref[h, at : at + 1, :], (L, L))
                cols = pltpu.roll(spread, L - reach, 1, stride=1, stride_axis=0)
                cols = jnp.where(near, cols, 0.0)
                beamed = dot3(rowed[k * share : (k + 1) * share], cols, (1, 1))
                for c in range(comps):
                    at = wide + 2 * terms + c // 4
                    mix = ref[h, at : at + 1, 32 * (c % 4) + k : 32 * (c % 4) + k + 1]
                    part = beamed * mix
                    totals[c] = part if totals[c] is None else totals[c] + part
    for c in range(comps):
        out[c, 0] = totals[c]


def flip(x, axis, bits):
    count = lax.axis_size(axis)
    return lax.ppermute(x, axis, [(i, i ^ bits) for i in range(count)])


def on_device(
    tod, filter_taps, det_weights, owner, tile_row, block_counts, beam_rows, beam_cols, mixing
):
    detectors, samples = tod.shape[1:]
    taps = filter_taps.shape[2]
    plan = Plan(detectors, samples, taps)
    tms, bands = lax.axis_size("tm"), lax.axis_size("band")
    inner = 2
    outer = tms // inner
    terms, beam = beam_rows.shape[1:]
    reach = (beam - 1) // 2
    comps = mixing.shape[0]
    span = plan.cols * A
    values = pl.pallas_call(
        functools.partial(filter_kernel, plan=plan),
        out_shape=jax.ShapeDtypeStruct((plan.out + 8, L), F32),
        in_specs=[SMEM, VMEM, VMEM, VMEM, VMEM, SMEM],
        out_specs=VMEM,
        scratch_shapes=[
            pltpu.VMEM((plan.shifts, plan.stored * detectors, L), F32),
            pltpu.VMEM(((plan.whole + 1) * detectors, L), F32),
            pltpu.VMEM((2, plan.width, plan.pieces * L), BF16),
            pltpu.VMEM((plan.rows, plan.width), F32),
            pltpu.VMEM((plan.lanes, plan.rows, L), F32),
            pltpu.VMEM((MARGIN + plan.out + plan.lead + 16 + plan.cols, L), F32),
        ],
        compiler_params=PARAMS,
        name="filter_blocks",
    )(det_weights, tod, filter_taps, owner, tile_row, block_counts)
    gathered = [values] + [flip(values, "tm", k * inner) for k in range(1, outer)]
    near = jnp.concatenate(gathered, axis=0)
    far = flip(near, "tm", 1)
    share = TROWS // bands
    wide = 2 * share + 2 * reach
    windows = pl.pallas_call(
        functools.partial(tile_kernel, plan=plan, outer=outer, inner=inner, bands=bands, reach=reach),
        out_shape=jax.ShapeDtypeStruct((bands // 2, wide + 8, L), F32),
        in_specs=[VMEM] * 5,
        out_specs=VMEM,
        scratch_shapes=[pltpu.VMEM((16 + tms, L), F32), pltpu.VMEM((TROWS + 2 * reach, L), F32)],
        compiler_params=PARAMS,
        name="gather_rows",
    )(near, far, beam_rows, beam_cols, mixing)
    own = windows[0:1]
    across = [flip(windows[h : h + 1], "band", 2 * h) for h in range(1, bands // 2)]
    mine = [own] + across
    other = [flip(m, "band", 1) for m in mine]
    return pl.pallas_call(
        functools.partial(beam_kernel, share=share, reach=reach, terms=terms, comps=comps, taps=beam),
        out_shape=jax.ShapeDtypeStruct((comps, 1, share, L), F32),
        in_specs=[VMEM] * (2 * len(mine)),
        out_specs=VMEM,
        compiler_params=PARAMS,
        name="smooth_and_mix",
    )(*mine, *other)


def solution(mesh):
    placed = (
        P("band", None, "tm"),
        P("band", None, None),
        P("band", None),
        P("band", "tm", None),
        P("band", "tm"),
        P("band", "tm"),
        P("band", None, None),
        P("band", None, None),
        P(None, "band", None),
    )
    return jax.shard_map(
        on_device,
        mesh=mesh,
        in_specs=placed,
        out_specs=P(None, "tm", "band", None),
        check_vma=False,
    )
```

time: 317 us -> 41.1 us (0.13)
  local copies, waits for them, and re-layouts: 192 us -> 2.96 us
  matrix products: 41.5 us -> 0 us
  waiting for transfers between devices: 40.1 us -> 12 us
  Pallas kernels: 0 us -> 16.3 us
  starting transfers between devices: 22.5 us -> 8.91 us
  between operations: 14.2 us -> 0.75 us
  other arithmetic: 4.45 us -> 0.01 us
    another operation x8 -> x0, local copies, waits for them, and re-layouts: 102 us -> none  [toeplitz_rows(): tiled = jnp.tile(padded_taps, seg_len)[:seg_len * width]]
    while x84 -> x0, local copies, waits for them, and re-layouts: 49.5 us -> none
    dot_general x12 -> x0, matrix products: 41.5 us -> none  [the longest x4 32.6 us: filter_group(): lax.dot_general(windows, tables, (((2,), (2,)), ((0,), (0,))), preferred_...]
    psum x1 -> x0, waiting for transfers between devices: 31.6 us -> none  [on_device(): total = lax.psum(local_mix, 'band')]
    slice x6 -> x1, local copies, waits for them, and re-layouts: 30.8 us -> 0.01 us  [on_device(): windows[h:h + 1]]
    pallas_call x0 -> x3, Pallas kernels: none -> 16.3 us  [the longest x1 14.2 us: on_device(): pl.pallas_call(functools.partial(filter_kernel, plan=plan), out_shape=jax...]
    all_to_all x2 -> x0, starting transfers between devices: 12.9 us -> none  [the longest x1 6.96 us: on_device(): lax.all_to_all(send_rows, 'tm', split_axis=0, concat_axis=0, tiled=True)]
    ppermute x4 -> x7, waiting for transfers between devices: 3.26 us -> 12 us  [flip(): return lax.ppermute(x, axis, [(i, i ^ bits) for i in range(count)])]
  transfers between devices with their start and end apart: 7 -> 7, of which waited for: 3 -> 5; matrix products, arithmetic and copies ran while one was open for 71% -> 0% of each run, Pallas kernels for 0% -> 0%
where the time goes in v1:
time: 41.1 us; the launch traced here: 40.9 us
  Pallas kernels  16.3 us (40%)
  waiting for transfers between devices  12 us (29%)
  starting transfers between devices  8.91 us (22%)
  local copies, waits for them, and re-layouts  2.96 us (7%)
  between operations  0.75 us (2%)
    pallas_call x1, Pallas kernels, on_device(): pl.pallas_call(functools.partial(filter_kernel, plan=plan), out_shape=jax...  14.2 us
    ppermute x7, waiting for transfers between devices, flip(): return lax.ppermute(x, axis, [(i, i ^ bits) for i in range(count)])  12 us
    ppermute x7, starting transfers between devices, flip(): return lax.ppermute(x, axis, [(i, i ^ bits) for i in range(count)])  8.91 us
    unnamed x18, local copies, waits for them, and re-layouts  2.95 us
    pallas_call x1, Pallas kernels, on_device(): pl.pallas_call(functools.partial(beam_kernel, share=share, reach=reach, t...  1.62 us
  transfers between devices with their start and end apart: 7, of which 5 were waited for; matrix products, arithmetic and copies ran while one was open for 0% of the time, Pallas kernels for 0%

profile of v1, /device:TPU:0, one launch (start us, length us, event | category | flops | bytes accessed | tf_op | source)
XLA Modules:
  0.0 40.9 jit_solution(6211747162463778375)
XLA Ops:
  0.0 0.0 copy-start.7
  0.7 0.0 copy-done.7
  0.7 0.0 copy-start.4
  0.7 0.0 copy-start.5
  0.7 0.1 copy.10.owner
  0.8 0.5 %copy-done.4 = f32[1,64]{1,0:T(1,128)S(1)} copy-done((f32[1,64]{1,0:T(1,128)S(1)}, f32[1,64]{1,0:T(1,128)}, u32[]{:S(2)}) %copy-start.4) | copy-done | bytes 280
  1.3 0.0 copy-done.5
  1.4 0.0 copy-start
  1.4 1.2 %copy-done = bf16[1,64,8192]{2,1,0:T(8,128)(2,1)S(1)} copy-done((bf16[1,64,8192]{2,1,0:T(8,128)(2,1)S(1)}, bf16[1,64,8192]{2,1,0:T(8,128)(2,1)}, u32[]{:S(2)}) %copy-start) | copy-done | bytes 1048600
  2.6 0.0 copy-start.1
  2.6 1.0 %copy-done.1 = bf16[1,64,2049]{2,1,0:T(8,128)(2,1)S(1)} copy-done((bf16[1,64,2049]{2,1,0:T(8,128)(2,1)S(1)}, bf16[1,64,2049]{2,1,0:T(8,128)(2,1)}, u32[]{:S(2)}) %copy-start.1) | copy-done | bytes 262296
  3.5 14.2 %filter_blocks.1 = f32[88,128]{1,0:T(8,128)S(1)} custom-call(f32[1,64]{1,0:T(1,128)S(1)} %copy-done.4, bf16[1,64,8192]{2,1,0:T(8,128)(2,1)S(1)} %copy-done, bf16[1,64,2049]{2,1,0:T(8,128)(2,1)S(1)} %copy-done.1, s32[1,64,1]{2,1,0:T(8,128)S(1)} %copy.10.owner, s32[1,64]{1,0:T(1,128)S(1)} %copy-done.5, s32[1,1]{1,0:T(1,128)S(6)} %copy.12.counts), custom_call_target="tpu_custom_call" | custom-call | tf_op jit(solution)/shard_map/filter_blocks/pallas_call | solution.py:299
  17.8 0.0 copy-start.6
  17.8 5.1 %collective-permute-start.2 = (f32[88,128]{1,0:T(8,128)S(1)}, f32[88,128]{1,0:T(8,128)S(1)}, u32[]{:S(2)}, u32[]{:S(2)}) collective-permute-start(f32[88,128]{1,0:T(8,128)S(1)} %filter_blocks.1), channel_id=1, source_target_pairs={{0,6},{1,7},{2,4},{3,5},{4,2},{5,3},{6,0},{7,1},{8,14},{9,15},{10,... | collective-permute-start | bytes 135176 | tf_op jit(solution)/shard_map/ppermute | solution.py:283
  22.9 0.0 collective-permute-start.1
  22.9 0.6 %collective-permute-start = (f32[88,128]{1,0:T(8,128)S(1)}, f32[88,128]{1,0:T(8,128)S(1)}, u32[]{:S(2)}, u32[]{:S(2)}) collective-permute-start(f32[88,128]{1,0:T(8,128)S(1)} %filter_blocks.1), channel_id=1, source_target_pairs={{0,2},{1,3},{2,0},{3,1},{4,6},{5,7},{6,4},{7,5},{8,10},{9,11},{10,... | collective-permute-start | bytes 135176 | tf_op jit(solution)/shard_map/ppermute | solution.py:283
  23.5 1.4 %collective-permute-done.2 = f32[88,128]{1,0:T(8,128)S(1)} collective-permute-done((f32[88,128]{1,0:T(8,128)S(1)}, f32[88,128]{1,0:T(8,128)S(1)}, u32[]{:S(2)}, u32[]{:S(2)}) %collective-permute-start.2) | collective-permute-done | bytes 45088 | tf_op jit(solution)/shard_map/ppermute | solution.py:283
  25.0 2.9 %collective-permute-done.1 = f32[88,128]{1,0:T(8,128)S(1)} collective-permute-done((f32[88,128]{1,0:T(8,128)S(1)}, f32[88,128]{1,0:T(8,128)S(1)}, u32[]{:S(2)}, u32[]{:S(2)}) %collective-permute-start.1) | collective-permute-done | bytes 45088 | tf_op jit(solution)/shard_map/ppermute | solution.py:283
  27.8 0.0 collective-permute-done
  27.9 0.0 copy-start.2
  27.9 0.0 copy-start.3
  27.9 1.6 %collective-permute-start.3 = (f32[352,128]{1,0:T(8,128)S(1)}, f32[352,128]{1,0:T(8,128)S(1)}, u32[]{:S(2)}, u32[]{:S(2)}) collective-permute-start(f32[352,128]{1,0:T(8,128)S(1)} %pad_maximum_fusion.near), channel_id=1, source_target_pairs={{0,1},{1,0},{2,3},{3,2},{4,5},{5,4},{6,7},{7,6},{8,9},{9,8},{10,11... | collective-permute-start | bytes 540680 | tf_op jit(solution)/shard_map/ppermute | solution.py:283
  29.4 0.0 copy-done.6
  29.4 0.1 copy.11.mixing
  29.5 3.9 %collective-permute-done.3.far = f32[352,128]{1,0:T(8,128)S(1)} collective-permute-done((f32[352,128]{1,0:T(8,128)S(1)}, f32[352,128]{1,0:T(8,128)S(1)}, u32[]{:S(2)}, u32[]{:S(2)}) %collective-permute-start.3) | collective-permute-done | bytes 180256 | tf_op jit(solution)/shard_map/ppermute | solution.py:283
  33.4 0.0 copy-done.2
  33.4 0.0 copy-done.3
  33.4 0.4 gather_rows.1
  33.9 1.6 %collective-permute-start.4 = (f32[1,104,128]{2,1,0:T(8,128)S(1)}, f32[1,104,128]{2,1,0:T(8,128)S(1)}, u32[]{:S(2)}, u32[]{:S(2)}) collective-permute-start(f32[1,104,128]{2,1,0:T(8,128)S(1)} %get-tuple-element.5), channel_id=1, source_target_pairs={{0,16},{8,24},{16,0},{24,8},{1,17},{9,25},{17,1},{25,9},{2,18},{10... | collective-permute-start | bytes 159752 | tf_op jit(solution)/shard_map/ppermute | solution.py:283
  35.5 0.0 collective-permute-start.5
  35.5 2.6 %collective-permute-done.4.refs_1_ = f32[1,104,128]{2,1,0:T(8,128)S(1)} collective-permute-done((f32[1,104,128]{2,1,0:T(8,128)S(1)}, f32[1,104,128]{2,1,0:T(8,128)S(1)}, u32[]{:S(2)}, u32[]{:S(2)}) %collective-permute-start.4) | collective-permute-done | bytes 53280 | tf_op jit(solution)/shard_map/ppermute | solution.py:283
  38.1 0.0 collective-permute-start.6
  38.1 0.0 collective-permute-done.5.refs_2_
  38.1 1.2 %collective-permute-done.6.refs_3_ = f32[1,104,128]{2,1,0:T(8,128)S(1)} collective-permute-done((f32[1,104,128]{2,1,0:T(8,128)S(1)}, f32[1,104,128]{2,1,0:T(8,128)S(1)}, u32[]{:S(2)}, u32[]{:S(2)}) %collective-permute-start.6) | collective-permute-done | bytes 53280 | tf_op jit(solution)/shard_map/ppermute | solution.py:283
  39.3 1.6 %smooth_and_mix.1 = f32[4,1,32,128]{3,2,1,0:T(8,128)} custom-call(f32[1,104,128]{2,1,0:T(8,128)S(1)} %get-tuple-element.6.refs_0_, f32[1,104,128]{2,1,0:T(8,128)S(1)} %collective-permute-done.4.refs_1_, f32[1,104,128]{2,1,0:T(8,128)S(1)} %collective-permute-done.5.refs_2_, f32[1,104,128]{2,1,0:T(8,128)S(1)} %collective-permute-done.6.refs_3_), custom_call_target="tpu_custom_call" | custom-call | tf_op jit(solution)/shard_map/smooth_and_mix/pallas_call | solution.py:333
  (2 shorter events, 0.0 us)
Async XLA Ops:
  0.0 0.7 %copy-start.7 = (s32[1,64,1]{1,2,0:T(1,128)S(1)}, s32[1,64,1]{1,2,0:T(1,128)}, u32[]{:S(2)}) copy-start(s32[1,64,1]{1,2,0:T(1,128)} %param.12) | copy-start | bytes 772
  0.7 0.7 %copy-start.4 = (f32[1,64]{1,0:T(1,128)S(1)}, f32[1,64]{1,0:T(1,128)}, u32[]{:S(2)}) copy-start(f32[1,64]{1,0:T(1,128)} %weights.1) | copy-start | bytes 772
  0.7 0.7 %copy-start.5 = (s32[1,64]{1,0:T(1,128)S(1)}, s32[1,64]{1,0:T(1,128)}, u32[]{:S(2)}) copy-start(s32[1,64]{1,0:T(1,128)} %tile_row.1) | copy-start | bytes 772
  1.4 1.2 %copy-start = (bf16[1,64,8192]{2,1,0:T(8,128)(2,1)S(1)}, bf16[1,64,8192]{2,1,0:T(8,128)(2,1)}, u32[]{:S(2)}) copy-start(bf16[1,64,8192]{2,1,0:T(8,128)(2,1)} %tod.1) | copy-start | bytes 3145732
  2.6 1.0 %copy-start.1 = (bf16[1,64,2049]{2,1,0:T(8,128)(2,1)S(1)}, bf16[1,64,2049]{2,1,0:T(8,128)(2,1)}, u32[]{:S(2)}) copy-start(bf16[1,64,2049]{2,1,0:T(8,128)(2,1)} %taps.1) | copy-start | bytes 786820
  17.8 11.7 %copy-start.6 = (f32[4,1,2]{0,2,1:T(2,128)S(1)}, f32[4,1,2]{0,2,1:T(2,128)}, u32[]{:S(2)}) copy-start(f32[4,1,2]{0,2,1:T(2,128)} %param.17) | copy-start | bytes 100
  17.8 7.2 %collective-permute-start.2 = (f32[88,128]{1,0:T(8,128)S(1)}, f32[88,128]{1,0:T(8,128)S(1)}, u32[]{:S(2)}, u32[]{:S(2)}) collective-permute-start(f32[88,128]{1,0:T(8,128)S(1)} %filter_blocks.1), channel_id=1, source_target_pairs={{0,6},{1,7},{2,4},{3,5},{4,2},{5,3},{6,0},{7,1},{8,14},{9,15},{10,... | collective-permute-start | bytes 135176 | tf_op jit(solution)/shard_map/ppermute | solution.py:283
  22.9 4.9 %collective-permute-start.1 = (f32[88,128]{1,0:T(8,128)S(1)}, f32[88,128]{1,0:T(8,128)S(1)}, u32[]{:S(2)}, u32[]{:S(2)}) collective-permute-start(f32[88,128]{1,0:T(8,128)S(1)} %filter_blocks.1), channel_id=1, source_target_pairs={{0,4},{1,5},{2,6},{3,7},{4,0},{5,1},{6,2},{7,3},{8,12},{9,13},{10,... | collective-permute-start | bytes 135176 | tf_op jit(solution)/shard_map/ppermute | solution.py:283
  22.9 4.9 %collective-permute-start = (f32[88,128]{1,0:T(8,128)S(1)}, f32[88,128]{1,0:T(8,128)S(1)}, u32[]{:S(2)}, u32[]{:S(2)}) collective-permute-start(f32[88,128]{1,0:T(8,128)S(1)} %filter_blocks.1), channel_id=1, source_target_pairs={{0,2},{1,3},{2,0},{3,1},{4,6},{5,7},{6,4},{7,5},{8,10},{9,11},{10,... | collective-permute-start | bytes 135176 | tf_op jit(solution)/shard_map/ppermute | solution.py:283
  27.9 5.6 %copy-start.2 = (f32[1,2,33]{2,1,0:T(2,128)S(1)}, f32[1,2,33]{2,1,0:T(2,128)}, u32[]{:S(2)}) copy-start(f32[1,2,33]{2,1,0:T(2,128)} %beam_rows.1) | copy-start | bytes 796
  27.9 5.6 %copy-start.3 = (f32[1,2,33]{2,1,0:T(2,128)S(1)}, f32[1,2,33]{2,1,0:T(2,128)}, u32[]{:S(2)}) copy-start(f32[1,2,33]{2,1,0:T(2,128)} %beam_cols.1) | copy-start | bytes 796
  27.9 5.6 %collective-permute-start.3 = (f32[352,128]{1,0:T(8,128)S(1)}, f32[352,128]{1,0:T(8,128)S(1)}, u32[]{:S(2)}, u32[]{:S(2)}) collective-permute-start(f32[352,128]{1,0:T(8,128)S(1)} %pad_maximum_fusion.near), channel_id=1, source_target_pairs={{0,1},{1,0},{2,3},{3,2},{4,5},{5,4},{6,7},{7,6},{8,9},{9,8},{10,11... | collective-permute-start | bytes 540680 | tf_op jit(solution)/shard_map/ppermute | solution.py:283
  33.9 4.2 %collective-permute-start.4 = (f32[1,104,128]{2,1,0:T(8,128)S(1)}, f32[1,104,128]{2,1,0:T(8,128)S(1)}, u32[]{:S(2)}, u32[]{:S(2)}) collective-permute-start(f32[1,104,128]{2,1,0:T(8,128)S(1)} %get-tuple-element.5), channel_id=1, source_target_pairs={{0,16},{8,24},{16,0},{24,8},{1,17},{9,25},{17,1},{25,9},{2,18},{10... | collective-permute-start | bytes 159752 | tf_op jit(solution)/shard_map/ppermute | solution.py:283
  35.5 2.6 %collective-permute-start.5 = (f32[1,104,128]{2,1,0:T(8,128)S(1)}, f32[1,104,128]{2,1,0:T(8,128)S(1)}, u32[]{:S(2)}, u32[]{:S(2)}) collective-permute-start(f32[1,104,128]{2,1,0:T(8,128)S(1)} %get-tuple-element.6.refs_0_), channel_id=1, source_target_pairs={{0,8},{8,0},{16,24},{24,16},{1,9},{9,1},{17,25},{25,17},{2,10},{10... | collective-permute-start | bytes 159752 | tf_op jit(solution)/shard_map/ppermute | solution.py:283
  38.1 1.2 %collective-permute-start.6 = (f32[1,104,128]{2,1,0:T(8,128)S(1)}, f32[1,104,128]{2,1,0:T(8,128)S(1)}, u32[]{:S(2)}, u32[]{:S(2)}) collective-permute-start(f32[1,104,128]{2,1,0:T(8,128)S(1)} %collective-permute-done.4.refs_1_), channel_id=1, source_target_pairs={{0,8},{8,0},{16,24},{24,16},{1,9},{9,1},{17,25},{25,17},{2,10},{10... | collective-permute-start | bytes 159752 | tf_op jit(solution)/shard_map/ppermute | solution.py:283

commit v2 on v1

v2 whole, which is shorter than its diff:
```python
import functools

import jax
import jax.numpy as jnp
from jax import lax
from jax.experimental import pallas as pl
from jax.experimental.pallas import tpu as pltpu
from jax.sharding import PartitionSpec as P

L = 128
TROWS = 128
BLOCK = 256
VMEM = pl.BlockSpec(memory_space=pltpu.VMEM)
ANY = pl.BlockSpec(memory_space=pl.ANY)
SMALL = pltpu.CompilerParams(vmem_limit_bytes=32 * 2**20)
WHOLE = pltpu.CompilerParams(vmem_limit_bytes=60 * 2**20)
F32, BF16 = jnp.float32, jnp.bfloat16


class Plan:
    def __init__(self, detectors, samples, taps):
        self.detectors, self.samples, self.taps = detectors, samples, taps
        self.groups = (taps - 1) // BLOCK
        self.steps = samples // BLOCK
        self.lead = self.groups - 1
        self.blocks = samples // L
        self.reach = (taps - 1) // 2 // L
        self.out = self.blocks + 2 * self.reach


def filter_kernel(
    weights_in, tod, taps_in, owner_in, row_in, counts_in,
    out, weights, taps, owner, tile_row, counts, held, table, line, diagonal, sems, *, plan
):
    nd, steps, lead, groups = plan.detectors, plan.steps, plan.lead, plan.groups
    small = [
        pltpu.make_async_copy(src, dst, sems.at[steps + i])
        for i, (src, dst) in enumerate(
            ((taps_in.at[0], taps), (weights_in, weights), (owner_in.at[0], owner), (row_in, tile_row), (counts_in, counts))
        )
    ]
    big = [
        pltpu.make_async_copy(
            tod.at[0, :, b * BLOCK : (b + 1) * BLOCK], held.at[(lead + b) * nd : (lead + b + 1) * nd, :], sems.at[b]
        )
        for b in range(steps)
    ]
    for copy in small + big:
        copy.start()
    held[0 : lead * nd, :] = jnp.zeros((lead * nd, BLOCK), BF16)
    held[(lead + steps) * nd :, :] = jnp.zeros((lead * nd, BLOCK), BF16)
    line[...] = jnp.zeros_like(line)
    row = lax.broadcasted_iota(jnp.int32, (nd, L), 0)
    lane = lax.broadcasted_iota(jnp.int32, (nd, L), 1)
    for copy in small:
        copy.wait()
    spread = jnp.broadcast_to(jnp.pad(weights[...], ((0, 0), (0, L - nd))), (nd, L))
    column = jnp.sum(jnp.where(row == lane, spread, 0.0), axis=1, keepdims=True)
    for pair in range(groups // 2):
        for half in range(2):
            parts = []
            for j in (2 * pair, 2 * pair + 1):
                start = j * BLOCK + half * L
                part = taps[:, start : start + L].astype(F32) * column
                parts.append(jnp.take_along_axis(part, L - 1 - lane, axis=1))
            turned = jnp.concatenate(parts, axis=0).T
            high, low = two_terms(turned)
            at = (1 - half) * L
            table[at : at + L, pair * L : (pair + 1) * L] = high
            table[BLOCK + at : BLOCK + at + L, pair * L : (pair + 1) * L] = low
    last = jnp.broadcast_to(taps[:, groups * BLOCK : groups * BLOCK + 1].astype(F32) * column, (nd, L))
    row8 = lax.broadcasted_iota(jnp.int32, (8, L), 0)
    lane8 = lax.broadcasted_iota(jnp.int32, (8, L), 1)
    for copy in big:
        copy.wait()

    slots = diagonal.shape[0]
    count = steps + lead

    def product(v):
        x = held[v * nd : (v + groups) * nd, :]
        both = jnp.dot(table[...], x, preferred_element_type=F32)
        diagonal[v % slots] = both[:BLOCK] + both[BLOCK:]

    def add_diagonals(tiles, at):
        total = direct = None
        for b in range(0, L, 8):
            part = tiles[0][b : b + 8]
            for other in tiles[1:]:
                part += other[b : b + 8]
            part = pltpu.roll(part, b + 1, 1, stride=1, stride_axis=0)
            kept = jnp.where(lane8 > row8 + b, part, 0.0)
            total = part if total is None else total + part
            direct = kept if direct is None else direct + kept
        line[at] += direct
        line[at + 1] += total - direct

    def corner(v, down, across):
        return diagonal[v % slots, down * L : (down + 1) * L, across * L : (across + 1) * L]

    product(0)
    for v in range(count):
        if v + 1 < count:
            product(v + 1)
        first = [corner(v, 0, 0)] + ([corner(v - 1, 1, 1)] if v else [])
        add_diagonals(first, 2 * v)
        add_diagonals([corner(v, 1, 0), corner(v, 0, 1)], 2 * v + 1)
        if v >= lead:
            for half in range(2):
                x = held[v * nd : (v + 1) * nd, half * L : (half + 1) * L]
                line[2 * (v - lead) + half] += (x.astype(F32) * last).reshape(nd // 8, 8, L).sum(0)
    add_diagonals([corner(count - 1, 1, 1)], 2 * count)
    out[0 : plan.out, :] = jnp.sum(line[0 : plan.out], axis=1)

    nb = plan.blocks
    row = lax.broadcasted_iota(jnp.int32, (nb, L), 0)
    lane = lax.broadcasted_iota(jnp.int32, (nb, L), 1)
    owners = jnp.sum(jnp.where(row == lane, owner[...], 0), axis=0, keepdims=True)
    rows = jnp.pad(tile_row[...], ((0, 0), (0, L - nb)))
    target = jnp.where(lane[:1] < counts[0, 0], owners * TROWS + rows, -1)
    out[plan.out : plan.out + 8, :] = jnp.broadcast_to(target.astype(F32), (8, L))


def two_terms(x):
    high = x.astype(BF16)
    return high, (x - high.astype(F32)).astype(BF16)


def tile_kernel(
    near, far, beam_rows, beam_cols, mixing, out, marks, tile, *, plan, outer, inner, bands, reach
):
    part_rows = plan.out + 8
    me = lax.axis_index("tm")
    band = lax.axis_index("band")
    halo, nb = plan.reach, plan.blocks
    total = outer * inner
    marks[...] = jnp.full_like(marks, -1.0)
    parts = []
    for flip, ref in enumerate((near, far)[:inner]):
        for k in range(outer):
            t = jnp.bitwise_xor(me, k * inner + flip)
            parts.append((t, ref, k * part_rows))
            marks[pl.ds(8 + t, 1), :] = ref[k * part_rows + plan.out : k * part_rows + plan.out + 1, :]
    here = marks[8 : 8 + total, :]
    before = marks[7 : 7 + total, :]
    after = marks[9 : 9 + total, :]
    lane = lax.broadcasted_iota(jnp.int32, (total, L), 1)
    target = jnp.where(lane < halo, pltpu.roll(before, (halo - nb) % L, 1), pltpu.roll(here, halo, 1))
    target = jnp.where(lane >= halo + nb, pltpu.roll(after, halo + nb, 1), target)
    target = jnp.where(lane < plan.out, target, -1.0)
    marks[8 : 8 + total, :] = target
    ext = TROWS + 2 * reach
    first = (me * TROWS - reach).astype(F32)
    row = lax.broadcasted_iota(jnp.int32, (ext, L), 0).astype(F32) + first
    row = jnp.where(row < 0, -2.0, row)
    result = None
    for t, ref, start in parts:
        picks = (jnp.broadcast_to(marks[pl.ds(8 + t, 1), :], (ext, L)) == row).astype(F32)
        high, low = two_terms(ref[start : start + plan.out, :])
        both = jnp.concatenate([high, low], axis=1)
        got = jnp.dot(picks[:, : plan.out].astype(BF16), both, preferred_element_type=F32)
        result = got if result is None else result + got
    tile[...] = result[:, :L] + result[:, L:]
    share = TROWS // bands
    wide = 2 * share + 2 * reach
    mine = band // 2
    for h in range(bands // 2):
        pair = jnp.bitwise_xor(mine, h)
        start = pl.multiple_of(pair * (2 * share), 8)
        out[h, 0:wide, :] = tile[pl.ds(start, wide), :]
        taps = beam_rows.shape[2]
        for k in range(2):
            out[h, wide + k : wide + k + 1, :] = jnp.zeros((1, L), F32)
        out[h, wide : wide + 8, :] = jnp.zeros((8, L), F32)
        terms = beam_rows.shape[1]
        for k in range(terms):
            out[h, wide + k : wide + k + 1, 0:taps] = beam_rows[0, k : k + 1, :]
            out[h, wide + terms + k : wide + terms + k + 1, 0:taps] = beam_cols[0, k : k + 1, :]
        comps = mixing.shape[0]
        for c in range(comps):
            out[h, wide + 2 * terms + c // 4 : wide + 2 * terms + c // 4 + 1, 32 * (c % 4) : 32 * (c % 4) + terms] = mixing[
                c, 0:1, :
            ]


def dot3(a, b, dims):
    a0, a1 = two_terms(a)
    b0, b1 = two_terms(b)
    ka, kb = dims
    left = jnp.concatenate([a0, a0, a1], axis=ka)
    right = jnp.concatenate([b0, b1, b0], axis=kb)
    return lax.dot_general(left, right, (((ka,), (kb,)), ((), ())), preferred_element_type=F32)


def beam_kernel(*refs, share, reach, terms, comps, taps):
    ins, out = refs[:-1], refs[-1]
    core = lax.rem(lax.axis_index("band"), 2)
    wide = 2 * share + 2 * reach
    need = share + 2 * reach
    x = lax.broadcasted_iota(jnp.int32, (L, L), 0)
    c_in = lax.broadcasted_iota(jnp.int32, (L, L), 1)
    near = jnp.abs(c_in - x) <= reach
    totals = [None] * comps
    for ref in ins:
        for h in range(ref.shape[0]):
            rows = ref[h, pl.ds(pl.multiple_of(core * share, 8), need), :]
            mats = []
            for k in range(terms):
                spread = jnp.broadcast_to(ref[h, wide + k : wide + k + 1, :], (share, L))
                mats.append(pltpu.roll(spread, 0, 1, stride=1, stride_axis=0)[:, :need])
            rowed = dot3(jnp.concatenate(mats, axis=0), rows, (1, 0))
            for k in range(terms):
                at = wide + terms + k
                spread = jnp.broadcast_to(ref[h, at : at + 1, :], (L, L))
                cols = pltpu.roll(spread, L - reach, 1, stride=1, stride_axis=0)
                cols = jnp.where(near, cols, 0.0)
                beamed = dot3(rowed[k * share : (k + 1) * share], cols, (1, 1))
                for c in range(comps):
                    at = wide + 2 * terms + c // 4
                    mix = ref[h, at : at + 1, 32 * (c % 4) + k : 32 * (c % 4) + k + 1]
                    part = beamed * mix
                    totals[c] = part if totals[c] is None else totals[c] + part
    for c in range(comps):
        out[c, 0] = totals[c]


def flip(x, axis, bits):
    count = lax.axis_size(axis)
    return lax.ppermute(x, axis, [(i, i ^ bits) for i in range(count)])


def on_device(
    tod, filter_taps, det_weights, owner, tile_row, block_counts, beam_rows, beam_cols, mixing
):
    detectors, samples = tod.shape[1:]
    taps = filter_taps.shape[2]
    plan = Plan(detectors, samples, taps)
    tms, bands = lax.axis_size("tm"), lax.axis_size("band")
    inner = 2
    outer = tms // inner
    terms, beam = beam_rows.shape[1:]
    reach = (beam - 1) // 2
    comps = mixing.shape[0]
    values = pl.pallas_call(
        functools.partial(filter_kernel, plan=plan),
        out_shape=jax.ShapeDtypeStruct((plan.out + 8, L), F32),
        in_specs=[ANY] * 6,
        out_specs=VMEM,
        scratch_shapes=[
            pltpu.VMEM((1, detectors), F32),
            pltpu.VMEM((detectors, taps), BF16),
            pltpu.VMEM((plan.blocks, 1), jnp.int32),
            pltpu.VMEM((1, plan.blocks), jnp.int32),
            pltpu.SMEM((1, 1), jnp.int32),
            pltpu.VMEM(((plan.steps + 2 * plan.lead) * detectors, BLOCK), BF16),
            pltpu.VMEM((2 * BLOCK, plan.groups * detectors), BF16),
            pltpu.VMEM((plan.out + 8, 8, L), F32),
            pltpu.VMEM((3, BLOCK, BLOCK), F32),
            pltpu.SemaphoreType.DMA((plan.steps + 5,)),
        ],
        compiler_params=WHOLE,
        name="filter_blocks",
    )(det_weights, tod, filter_taps, owner, tile_row, block_counts)
    gathered = [values] + [flip(values, "tm", k * inner) for k in range(1, outer)]
    near = jnp.concatenate(gathered, axis=0)
    far = flip(near, "tm", 1)
    share = TROWS // bands
    wide = 2 * share + 2 * reach
    windows = pl.pallas_call(
        functools.partial(tile_kernel, plan=plan, outer=outer, inner=inner, bands=bands, reach=reach),
        out_shape=jax.ShapeDtypeStruct((bands // 2, wide + 8, L), F32),
        in_specs=[VMEM] * 5,
        out_specs=VMEM,
        scratch_shapes=[pltpu.VMEM((16 + tms, L), F32), pltpu.VMEM((TROWS + 2 * reach, L), F32)],
        compiler_params=SMALL,
        name="gather_rows",
    )(near, far, beam_rows, beam_cols, mixing)
    own = windows[0:1]
    across = [flip(windows[h : h + 1], "band", 2 * h) for h in range(1, bands // 2)]
    mine = [own] + across
    other = [flip(m, "band", 1) for m in mine]
    return pl.pallas_call(
        functools.partial(beam_kernel, share=share, reach=reach, terms=terms, comps=comps, taps=beam),
        out_shape=jax.ShapeDtypeStruct((comps, 1, share, L), F32),
        in_specs=[VMEM] * (2 * len(mine)),
        out_specs=VMEM,
        compiler_params=SMALL,
        name="smooth_and_mix",
    )(*mine, *other)


def solution(mesh):
    placed = (
        P("band", None, "tm"),
        P("band", None, None),
        P("band", None),
        P("band", "tm", None),
        P("band", "tm"),
        P("band", "tm"),
        P("band", None, None),
        P("band", None, None),
        P(None, "band", None),
    )
    return jax.shard_map(
        on_device,
        mesh=mesh,
        in_specs=placed,
        out_specs=P(None, "tm", "band", None),
        check_vma=False,
    )
```

time: 41.1 us -> 33.8 us (0.82)
  Pallas kernels: 16.3 us -> 10 us
  local copies, waits for them, and re-layouts: 2.96 us -> 0.82 us
  other arithmetic: 0.01 us -> 0.8 us
    pallas_call x1, Pallas kernels: 14.2 us -> 8.02 us  [on_device(): pl.pallas_call(functools.partial(filter_kernel, plan=plan), out_shape=jax...]
    unnamed x18 -> x10, local copies, waits for them, and re-layouts: 2.95 us -> 0.81 us
    concatenate x1, other arithmetic: 0.01 us -> 0.8 us  [on_device(): near = jnp.concatenate(gathered, axis=0)]
where the time goes in v2:
time: 33.8 us; the launch traced here: 33.6 us
  waiting for transfers between devices  12.3 us (36%)
  Pallas kernels  10 us (30%)
  starting transfers between devices  8.9 us (26%)
  local copies, waits for them, and re-layouts  0.82 us (2%)
  other arithmetic  0.8 us (2%)
  between operations  0.74 us (2%)
    ppermute x7, waiting for transfers between devices, flip(): return lax.ppermute(x, axis, [(i, i ^ bits) for i in range(count)])  12.3 us
    ppermute x7, starting transfers between devices, flip(): return lax.ppermute(x, axis, [(i, i ^ bits) for i in range(count)])  8.9 us
    pallas_call x1, Pallas kernels, on_device(): pl.pallas_call(functools.partial(filter_kernel, plan=plan), out_shape=jax...  8.02 us
    pallas_call x1, Pallas kernels, on_device(): pl.pallas_call(functools.partial(beam_kernel, share=share, reach=reach, t...  1.62 us
    unnamed x10, local copies, waits for them, and re-layouts  0.81 us
    concatenate x1, other arithmetic, on_device(): near = jnp.concatenate(gathered, axis=0)  0.8 us
  transfers between devices with their start and end apart: 7, of which 5 were waited for; matrix products, arithmetic and copies ran while one was open for 0% of the time, Pallas kernels for 0%

profile of v2, /device:TPU:0, one launch (start us, length us, event | category | flops | bytes accessed | tf_op | source)
XLA Modules:
  0.0 33.6 jit_solution(9936793348472746312)
XLA Ops:
  0.0 0.0 copy-start.3
  0.7 0.0 copy-done.3
  0.7 0.7 %copy.10.owner_in = s32[1,64,1]{2,1,0:T(8,128)} copy(s32[1,64,1]{1,2,0:T(1,128)S(1)} %copy-done.3) | data formatting | bytes 512 | tf_op args[3]
  1.4 8.0 %filter_blocks.1 = f32[88,128]{1,0:T(8,128)} custom-call(f32[1,64]{1,0:T(1,128)} %weights_in.1, bf16[1,64,8192]{2,1,0:T(8,128)(2,1)} %tod.1, bf16[1,64,2049]{2,1,0:T(8,128)(2,1)} %taps_in.1, s32[1,64,1]{2,1,0:T(8,128)} %copy.10.owner_in, s32[1,64]{1,0:T(1,128)} %row_in.1, s32[1,1]{1,0:T(1,128)S(6)} %copy.12.counts_in), custom_call_target="tpu_custom_call" | custom-call | tf_op jit(solution)/shard_map/filter_blocks/pallas_call | solution.py:244
  9.4 0.0 copy-start.2
  9.4 5.1 %collective-permute-start.2 = (f32[88,128]{1,0:T(8,128)}, f32[88,128]{1,0:T(8,128)S(1)}, u32[]{:S(2)}, u32[]{:S(2)}) collective-permute-start(f32[88,128]{1,0:T(8,128)} %filter_blocks.1), channel_id=1, source_target_pairs={{0,6},{1,7},{2,4},{3,5},{4,2},{5,3},{6,0},{7,1},{8,14},{9,15},{10,... | collective-permute-start | bytes 135176 | tf_op jit(solution)/shard_map/ppermute | solution.py:229
  14.5 0.0 collective-permute-start.1
  14.5 0.6 %collective-permute-start = (f32[88,128]{1,0:T(8,128)}, f32[88,128]{1,0:T(8,128)S(1)}, u32[]{:S(2)}, u32[]{:S(2)}) collective-permute-start(f32[88,128]{1,0:T(8,128)} %filter_blocks.1), channel_id=1, source_target_pairs={{0,2},{1,3},{2,0},{3,1},{4,6},{5,7},{6,4},{7,5},{8,10},{9,11},{10,... | collective-permute-start | bytes 135176 | tf_op jit(solution)/shard_map/ppermute | solution.py:229
  15.2 1.6 %collective-permute-done.2 = f32[88,128]{1,0:T(8,128)S(1)} collective-permute-done((f32[88,128]{1,0:T(8,128)}, f32[88,128]{1,0:T(8,128)S(1)}, u32[]{:S(2)}, u32[]{:S(2)}) %collective-permute-start.2) | collective-permute-done | bytes 45088 | tf_op jit(solution)/shard_map/ppermute | solution.py:229
  16.8 2.9 %collective-permute-done.1 = f32[88,128]{1,0:T(8,128)S(1)} collective-permute-done((f32[88,128]{1,0:T(8,128)}, f32[88,128]{1,0:T(8,128)S(1)}, u32[]{:S(2)}, u32[]{:S(2)}) %collective-permute-start.1) | collective-permute-done | bytes 45088 | tf_op jit(solution)/shard_map/ppermute | solution.py:229
  19.7 0.0 collective-permute-done
  19.7 0.8 %pad_maximum_fusion.near = f32[352,128]{1,0:T(8,128)S(1)} fusion(f32[88,128]{1,0:T(8,128)S(1)} %collective-permute-done.2, f32[88,128]{1,0:T(8,128)S(1)} %collective-permute-done.1, f32[88,128]{1,0:T(8,128)S(1)} %collective-permute-done, f32[88,128]{1,0:T(8,128)} %filter_blocks.1), kind=kLoop, calls=%fused_computation | loop fusion | flops 135168 | bytes 360448 | tf_op jit(solution)/shard_map/concatenate | solution.py:265
  20.5 0.0 copy-start
  20.5 0.0 copy-start.1
  20.5 1.6 %collective-permute-start.3 = (f32[352,128]{1,0:T(8,128)S(1)}, f32[352,128]{1,0:T(8,128)S(1)}, u32[]{:S(2)}, u32[]{:S(2)}) collective-permute-start(f32[352,128]{1,0:T(8,128)S(1)} %pad_maximum_fusion.near), channel_id=1, source_target_pairs={{0,1},{1,0},{2,3},{3,2},{4,5},{5,4},{6,7},{7,6},{8,9},{9,8},{10,11... | collective-permute-start | bytes 540680 | tf_op jit(solution)/shard_map/ppermute | solution.py:229
  22.1 0.0 copy-done.2
  22.1 0.1 copy.11.mixing
  22.2 3.9 %collective-permute-done.3.far = f32[352,128]{1,0:T(8,128)S(1)} collective-permute-done((f32[352,128]{1,0:T(8,128)S(1)}, f32[352,128]{1,0:T(8,128)S(1)}, u32[]{:S(2)}, u32[]{:S(2)}) %collective-permute-start.3) | collective-permute-done | bytes 180256 | tf_op jit(solution)/shard_map/ppermute | solution.py:229
  26.1 0.0 copy-done
  26.1 0.0 copy-done.1
  26.1 0.4 %gather_rows.1 = f32[2,104,128]{2,1,0:T(8,128)S(1)} custom-call(f32[352,128]{1,0:T(8,128)S(1)} %pad_maximum_fusion.near, f32[352,128]{1,0:T(8,128)S(1)} %collective-permute-done.3.far, f32[1,2,33]{2,1,0:T(2,128)S(1)} %copy-done, f32[1,2,33]{2,1,0:T(2,128)S(1)} %copy-done.1, f32[4,1,2]{2,1,0:T(1,128)S(1)} %copy.11.mixing), custom_call_target="tpu_custom_call" | custom-call | tf_op jit(solution)/shard_map/gather_rows/pallas_call | solution.py:269
  26.5 1.6 %collective-permute-start.4 = (f32[1,104,128]{2,1,0:T(8,128)S(1)}, f32[1,104,128]{2,1,0:T(8,128)S(1)}, u32[]{:S(2)}, u32[]{:S(2)}) collective-permute-start(f32[1,104,128]{2,1,0:T(8,128)S(1)} %get-tuple-element.5), channel_id=1, source_target_pairs={{0,16},{8,24},{16,0},{24,8},{1,17},{9,25},{17,1},{25,9},{2,18},{10... | collective-permute-start | bytes 159752 | tf_op jit(solution)/shard_map/ppermute | solution.py:229
  28.1 0.0 collective-permute-start.5
  28.1 2.6 %collective-permute-done.4.refs_1_ = f32[1,104,128]{2,1,0:T(8,128)S(1)} collective-permute-done((f32[1,104,128]{2,1,0:T(8,128)S(1)}, f32[1,104,128]{2,1,0:T(8,128)S(1)}, u32[]{:S(2)}, u32[]{:S(2)}) %collective-permute-start.4) | collective-permute-done | bytes 53280 | tf_op jit(solution)/shard_map/ppermute | solution.py:229
  30.7 0.0 collective-permute-start.6
  30.7 0.0 collective-permute-done.5.refs_2_
  30.7 1.2 %collective-permute-done.6.refs_3_ = f32[1,104,128]{2,1,0:T(8,128)S(1)} collective-permute-done((f32[1,104,128]{2,1,0:T(8,128)S(1)}, f32[1,104,128]{2,1,0:T(8,128)S(1)}, u32[]{:S(2)}, u32[]{:S(2)}) %collective-permute-start.6) | collective-permute-done | bytes 53280 | tf_op jit(solution)/shard_map/ppermute | solution.py:229
  31.9 1.6 %smooth_and_mix.1 = f32[4,1,32,128]{3,2,1,0:T(8,128)} custom-call(f32[1,104,128]{2,1,0:T(8,128)S(1)} %get-tuple-element.6.refs_0_, f32[1,104,128]{2,1,0:T(8,128)S(1)} %collective-permute-done.4.refs_1_, f32[1,104,128]{2,1,0:T(8,128)S(1)} %collective-permute-done.5.refs_2_, f32[1,104,128]{2,1,0:T(8,128)S(1)} %collective-permute-done.6.refs_3_), custom_call_target="tpu_custom_call" | custom-call | tf_op jit(solution)/shard_map/smooth_and_mix/pallas_call | solution.py:282
  (1 shorter events, 0.0 us)
Async XLA Ops:
  0.0 0.7 %copy-start.3 = (s32[1,64,1]{1,2,0:T(1,128)S(1)}, s32[1,64,1]{1,2,0:T(1,128)}, u32[]{:S(2)}) copy-start(s32[1,64,1]{1,2,0:T(1,128)} %param.12) | copy-start | bytes 772
  9.4 12.7 %copy-start.2 = (f32[4,1,2]{0,2,1:T(2,128)S(1)}, f32[4,1,2]{0,2,1:T(2,128)}, u32[]{:S(2)}) copy-start(f32[4,1,2]{0,2,1:T(2,128)} %param.17) | copy-start | bytes 100
  9.4 7.4 %collective-permute-start.2 = (f32[88,128]{1,0:T(8,128)}, f32[88,128]{1,0:T(8,128)S(1)}, u32[]{:S(2)}, u32[]{:S(2)}) collective-permute-start(f32[88,128]{1,0:T(8,128)} %filter_blocks.1), channel_id=1, source_target_pairs={{0,6},{1,7},{2,4},{3,5},{4,2},{5,3},{6,0},{7,1},{8,14},{9,15},{10,... | collective-permute-start | bytes 135176 | tf_op jit(solution)/shard_map/ppermute | solution.py:229
  14.5 5.2 %collective-permute-start.1 = (f32[88,128]{1,0:T(8,128)}, f32[88,128]{1,0:T(8,128)S(1)}, u32[]{:S(2)}, u32[]{:S(2)}) collective-permute-start(f32[88,128]{1,0:T(8,128)} %filter_blocks.1), channel_id=1, source_target_pairs={{0,4},{1,5},{2,6},{3,7},{4,0},{5,1},{6,2},{7,3},{8,12},{9,13},{10,... | collective-permute-start | bytes 135176 | tf_op jit(solution)/shard_map/ppermute | solution.py:229
  14.5 5.2 %collective-permute-start = (f32[88,128]{1,0:T(8,128)}, f32[88,128]{1,0:T(8,128)S(1)}, u32[]{:S(2)}, u32[]{:S(2)}) collective-permute-start(f32[88,128]{1,0:T(8,128)} %filter_blocks.1), channel_id=1, source_target_pairs={{0,2},{1,3},{2,0},{3,1},{4,6},{5,7},{6,4},{7,5},{8,10},{9,11},{10,... | collective-permute-start | bytes 135176 | tf_op jit(solution)/shard_map/ppermute | solution.py:229
  20.5 5.6 %copy-start = (f32[1,2,33]{2,1,0:T(2,128)S(1)}, f32[1,2,33]{2,1,0:T(2,128)}, u32[]{:S(2)}) copy-start(f32[1,2,33]{2,1,0:T(2,128)} %beam_rows.1) | copy-start | bytes 796
  20.5 5.6 %copy-start.1 = (f32[1,2,33]{2,1,0:T(2,128)S(1)}, f32[1,2,33]{2,1,0:T(2,128)}, u32[]{:S(2)}) copy-start(f32[1,2,33]{2,1,0:T(2,128)} %beam_cols.1) | copy-start | bytes 796
  20.5 5.6 %collective-permute-start.3 = (f32[352,128]{1,0:T(8,128)S(1)}, f32[352,128]{1,0:T(8,128)S(1)}, u32[]{:S(2)}, u32[]{:S(2)}) collective-permute-start(f32[352,128]{1,0:T(8,128)S(1)} %pad_maximum_fusion.near), channel_id=1, source_target_pairs={{0,1},{1,0},{2,3},{3,2},{4,5},{5,4},{6,7},{7,6},{8,9},{9,8},{10,11... | collective-permute-start | bytes 540680 | tf_op jit(solution)/shard_map/ppermute | solution.py:229
  26.5 4.2 %collective-permute-start.4 = (f32[1,104,128]{2,1,0:T(8,128)S(1)}, f32[1,104,128]{2,1,0:T(8,128)S(1)}, u32[]{:S(2)}, u32[]{:S(2)}) collective-permute-start(f32[1,104,128]{2,1,0:T(8,128)S(1)} %get-tuple-element.5), channel_id=1, source_target_pairs={{0,16},{8,24},{16,0},{24,8},{1,17},{9,25},{17,1},{25,9},{2,18},{10... | collective-permute-start | bytes 159752 | tf_op jit(solution)/shard_map/ppermute | solution.py:229
  28.1 2.6 %collective-permute-start.5 = (f32[1,104,128]{2,1,0:T(8,128)S(1)}, f32[1,104,128]{2,1,0:T(8,128)S(1)}, u32[]{:S(2)}, u32[]{:S(2)}) collective-permute-start(f32[1,104,128]{2,1,0:T(8,128)S(1)} %get-tuple-element.6.refs_0_), channel_id=1, source_target_pairs={{0,8},{8,0},{16,24},{24,16},{1,9},{9,1},{17,25},{25,17},{2,10},{10... | collective-permute-start | bytes 159752 | tf_op jit(solution)/shard_map/ppermute | solution.py:229
  30.7 1.2 %collective-permute-start.6 = (f32[1,104,128]{2,1,0:T(8,128)S(1)}, f32[1,104,128]{2,1,0:T(8,128)S(1)}, u32[]{:S(2)}, u32[]{:S(2)}) collective-permute-start(f32[1,104,128]{2,1,0:T(8,128)S(1)} %collective-permute-done.4.refs_1_), channel_id=1, source_target_pairs={{0,8},{8,0},{16,24},{24,16},{1,9},{9,1},{17,25},{25,17},{2,10},{10... | collective-permute-start | bytes 159752 | tf_op jit(solution)/shard_map/ppermute | solution.py:229

commit v3 on v2

--- a/solution.py
+++ b/solution.py
@@ -36,7 +36,7 @@
     small = [
         pltpu.make_async_copy(src, dst, sems.at[steps + i])
         for i, (src, dst) in enumerate(
-            ((taps_in.at[0], taps), (weights_in, weights), (owner_in.at[0], owner), (row_in, tile_row), (counts_in, counts))
+            ((taps_in.at[0], taps), (weights_in, weights), (owner_in, owner), (row_in, tile_row), (counts_in, counts))
         )
     ]
     big = [
@@ -78,8 +78,11 @@
     count = steps + lead
 
     def product(v):
-        x = held[v * nd : (v + groups) * nd, :]
-        both = jnp.dot(table[...], x, preferred_element_type=F32)
+        half = groups // 2
+        low = half if v + half <= lead else 0
+        high = half if v + half >= lead + steps else groups
+        x = held[(v + low) * nd : (v + high) * nd, :]
+        both = jnp.dot(table[:, low * nd : high * nd], x, preferred_element_type=F32)
         diagonal[v % slots] = both[:BLOCK] + both[BLOCK:]
 
     def add_diagonals(tiles, at):
@@ -113,11 +116,10 @@
     out[0 : plan.out, :] = jnp.sum(line[0 : plan.out], axis=1)
 
     nb = plan.blocks
-    row = lax.broadcasted_iota(jnp.int32, (nb, L), 0)
-    lane = lax.broadcasted_iota(jnp.int32, (nb, L), 1)
-    owners = jnp.sum(jnp.where(row == lane, owner[...], 0), axis=0, keepdims=True)
-    rows = jnp.pad(tile_row[...], ((0, 0), (0, L - nb)))
-    target = jnp.where(lane[:1] < counts[0, 0], owners * TROWS + rows, -1)
+    pad = ((0, 0), (0, L - nb))
+    target = jnp.pad(owner[...], pad) * TROWS + jnp.pad(tile_row[...], pad)
+    kept = lax.broadcasted_iota(jnp.int32, (1, L), 1) < counts[0, 0]
+    target = jnp.where(kept, target, -1)
     out[plan.out : plan.out + 8, :] = jnp.broadcast_to(target.astype(F32), (8, L))
 
 
@@ -126,61 +128,86 @@
     return high, (x - high.astype(F32)).astype(BF16)
 
 
-def tile_kernel(
-    near, far, beam_rows, beam_cols, mixing, out, marks, tile, *, plan, outer, inner, bands, reach
-):
-    part_rows = plan.out + 8
+def rows_of(target, first, count):
+    row = lax.broadcasted_iota(jnp.int32, (count, target.shape[1]), 0).astype(F32) + first
+    row = jnp.where(row < 0, -2.0, row)
+    return (jnp.broadcast_to(target, row.shape) == row).astype(BF16)
+
+
+def add_rows(picks, blocks):
+    high, low = two_terms(blocks)
+    both = jnp.dot(picks, jnp.concatenate([high, low], axis=1), preferred_element_type=F32)
+    return both[:, :L] + both[:, L:]
+
+
+def tile_rows_kernel(*refs, plan, reach):
+    parts, (home, away) = refs[:-2], refs[-2:]
+    nb, halo = plan.blocks, plan.reach
     me = lax.axis_index("tm")
-    band = lax.axis_index("band")
-    halo, nb = plan.reach, plan.blocks
-    total = outer * inner
+    ext = TROWS + 2 * reach
+    target = jnp.concatenate([ref[plan.out : plan.out + 1, 0:nb] for ref in parts], axis=1)
+    blocks = jnp.concatenate([ref[halo : halo + nb, :] for ref in parts], axis=0)
+    for out, tile in ((home, me), (away, jnp.bitwise_xor(me, 1))):
+        picks = rows_of(target, (tile * TROWS - reach).astype(F32), ext)
+        out[0:ext, :] = add_rows(picks, blocks)
+    for k, ref in enumerate(parts):
+        at = ext + 2 * halo * k
+        away[at : at + halo, :] = ref[0:halo, :]
+        away[at + halo : at + 2 * halo, :] = ref[halo + nb : plan.out, :]
+    at = ext + 2 * halo * len(parts)
+    away[at:, :] = jnp.full((away.shape[0] - at, L), -1.0, F32)
+    for k, ref in enumerate(parts):
+        away[at + k : at + k + 1, :] = ref[plan.out : plan.out + 1, :]
+
+
+def windows_kernel(*refs, plan, outer, bands, reach):
+    parts = refs[:outer]
+    home, other, beam_rows, beam_cols, mixing, out, marks, tile = refs[outer:]
+    me = lax.axis_index("tm")
+    mine = lax.axis_index("band") // 2
+    nb, halo = plan.blocks, plan.reach
+    ext = TROWS + 2 * reach
+    after_rows = ext + 2 * halo * outer
     marks[...] = jnp.full_like(marks, -1.0)
-    parts = []
-    for flip, ref in enumerate((near, far)[:inner]):
-        for k in range(outer):
-            t = jnp.bitwise_xor(me, k * inner + flip)
-            parts.append((t, ref, k * part_rows))
-            marks[pl.ds(8 + t, 1), :] = ref[k * part_rows + plan.out : k * part_rows + plan.out + 1, :]
-    here = marks[8 : 8 + total, :]
-    before = marks[7 : 7 + total, :]
-    after = marks[9 : 9 + total, :]
-    lane = lax.broadcasted_iota(jnp.int32, (total, L), 1)
-    target = jnp.where(lane < halo, pltpu.roll(before, (halo - nb) % L, 1), pltpu.roll(here, halo, 1))
-    target = jnp.where(lane >= halo + nb, pltpu.roll(after, halo + nb, 1), target)
-    target = jnp.where(lane < plan.out, target, -1.0)
-    marks[8 : 8 + total, :] = target
-    ext = TROWS + 2 * reach
-    first = (me * TROWS - reach).astype(F32)
-    row = lax.broadcasted_iota(jnp.int32, (ext, L), 0).astype(F32) + first
-    row = jnp.where(row < 0, -2.0, row)
-    result = None
-    for t, ref, start in parts:
-        picks = (jnp.broadcast_to(marks[pl.ds(8 + t, 1), :], (ext, L)) == row).astype(F32)
-        high, low = two_terms(ref[start : start + plan.out, :])
-        both = jnp.concatenate([high, low], axis=1)
-        got = jnp.dot(picks[:, : plan.out].astype(BF16), both, preferred_element_type=F32)
-        result = got if result is None else result + got
-    tile[...] = result[:, :L] + result[:, L:]
+    numbers = []
+    for k, ref in enumerate(parts):
+        t = jnp.bitwise_xor(me, 2 * k)
+        marks[pl.ds(8 + t, 1), :] = ref[plan.out : plan.out + 1, :]
+        numbers.append(t)
+    for k in range(outer):
+        t = jnp.bitwise_xor(me, 2 * k + 1)
+        marks[pl.ds(8 + t, 1), :] = other[after_rows + k : after_rows + k + 1, :]
+        numbers.append(t)
+    targets = []
+    for t in numbers:
+        before = marks[pl.ds(7 + t, 1), :]
+        after = marks[pl.ds(9 + t, 1), :]
+        targets += [before[:, nb - halo : nb], after[:, 0:halo]]
+    blocks = []
+    for ref in parts:
+        blocks += [ref[0:halo, :], ref[halo + nb : plan.out, :]]
+    blocks.append(other[ext:after_rows, :])
+    picks = rows_of(jnp.concatenate(targets, axis=1), (me * TROWS - reach).astype(F32), ext)
+    tile[...] = home[...] + other[0:ext, :] + add_rows(picks, jnp.concatenate(blocks, axis=0))
     share = TROWS // bands
     wide = 2 * share + 2 * reach
-    mine = band // 2
+    terms, taps = beam_rows.shape[1:]
+    comps = mixing.shape[0]
+    out[...] = jnp.zeros_like(out)
+    pad = jnp.zeros((8, L - taps), F32)
+    lane = lax.broadcasted_iota(jnp.int32, (8, L), 1)
+    turn = jnp.where(lane < taps, taps - 1 - lane, lane)
     for h in range(bands // 2):
-        pair = jnp.bitwise_xor(mine, h)
-        start = pl.multiple_of(pair * (2 * share), 8)
+        start = pl.multiple_of(jnp.bitwise_xor(mine, h) * (2 * share), 8)
         out[h, 0:wide, :] = tile[pl.ds(start, wide), :]
-        taps = beam_rows.shape[2]
-        for k in range(2):
-            out[h, wide + k : wide + k + 1, :] = jnp.zeros((1, L), F32)
-        out[h, wide : wide + 8, :] = jnp.zeros((8, L), F32)
-        terms = beam_rows.shape[1]
         for k in range(terms):
             out[h, wide + k : wide + k + 1, 0:taps] = beam_rows[0, k : k + 1, :]
-            out[h, wide + terms + k : wide + terms + k + 1, 0:taps] = beam_cols[0, k : k + 1, :]
-        comps = mixing.shape[0]
-        for c in range(comps):
-            out[h, wide + 2 * terms + c // 4 : wide + 2 * terms + c // 4 + 1, 32 * (c % 4) : 32 * (c % 4) + terms] = mixing[
-                c, 0:1, :
-            ]
+            profile = jnp.broadcast_to(beam_cols[0, k : k + 1, :], (8, taps))
+            turned = jnp.take_along_axis(jnp.concatenate([profile, pad], axis=1), turn, axis=1)
+            out[h, wide + terms + k : wide + terms + k + 1, :] = turned[0:1]
+            for c in range(comps):
+                at = wide + 2 * terms + c * terms + k
+                out[h, at : at + 1, :] = jnp.broadcast_to(mixing[c, 0:1, k : k + 1], (1, L))
 
 
 def dot3(a, b, dims):
@@ -214,11 +241,10 @@
                 spread = jnp.broadcast_to(ref[h, at : at + 1, :], (L, L))
                 cols = pltpu.roll(spread, L - reach, 1, stride=1, stride_axis=0)
                 cols = jnp.where(near, cols, 0.0)
-                beamed = dot3(rowed[k * share : (k + 1) * share], cols, (1, 1))
+                beamed = dot3(rowed[k * share : (k + 1) * share], cols, (1, 0))
                 for c in range(comps):
-                    at = wide + 2 * terms + c // 4
-                    mix = ref[h, at : at + 1, 32 * (c % 4) + k : 32 * (c % 4) + k + 1]
-                    part = beamed * mix
+                    at = wide + 2 * terms + c * terms + k
+                    part = beamed * ref[h, at : at + 1, :]
                     totals[c] = part if totals[c] is None else totals[c] + part
     for c in range(comps):
         out[c, 0] = totals[c]
@@ -249,7 +275,7 @@
         scratch_shapes=[
             pltpu.VMEM((1, detectors), F32),
             pltpu.VMEM((detectors, taps), BF16),
-            pltpu.VMEM((plan.blocks, 1), jnp.int32),
+            pltpu.VMEM((1, plan.blocks), jnp.int32),
             pltpu.VMEM((1, plan.blocks), jnp.int32),
             pltpu.SMEM((1, 1), jnp.int32),
             pltpu.VMEM(((plan.steps + 2 * plan.lead) * detectors, BLOCK), BF16),
@@ -260,21 +286,31 @@
         ],
         compiler_params=WHOLE,
         name="filter_blocks",
-    )(det_weights, tod, filter_taps, owner, tile_row, block_counts)
-    gathered = [values] + [flip(values, "tm", k * inner) for k in range(1, outer)]
-    near = jnp.concatenate(gathered, axis=0)
-    far = flip(near, "tm", 1)
+    )(det_weights, tod, filter_taps, owner[:, :, 0], tile_row, block_counts)
+    parts = [values] + [flip(values, "tm", k * inner) for k in range(1, outer)]
+    ext = TROWS + 2 * reach
+    sent = ext + 2 * plan.reach * outer + -(-outer // 8) * 8
+    home, away = pl.pallas_call(
+        functools.partial(tile_rows_kernel, plan=plan, reach=reach),
+        out_shape=(jax.ShapeDtypeStruct((ext, L), F32), jax.ShapeDtypeStruct((sent, L), F32)),
+        in_specs=[VMEM] * outer,
+        out_specs=(VMEM, VMEM),
+        compiler_params=SMALL,
+        name="tile_rows",
+    )(*parts)
+    other = flip(away, "tm", 1)
     share = TROWS // bands
     wide = 2 * share + 2 * reach
+    extra = -(-(2 * terms + comps * terms) // 8) * 8
     windows = pl.pallas_call(
-        functools.partial(tile_kernel, plan=plan, outer=outer, inner=inner, bands=bands, reach=reach),
-        out_shape=jax.ShapeDtypeStruct((bands // 2, wide + 8, L), F32),
-        in_specs=[VMEM] * 5,
+        functools.partial(windows_kernel, plan=plan, outer=outer, bands=bands, reach=reach),
+        out_shape=jax.ShapeDtypeStruct((bands // 2, wide + extra, L), F32),
+        in_specs=[VMEM] * (outer + 5),
         out_specs=VMEM,
-        scratch_shapes=[pltpu.VMEM((16 + tms, L), F32), pltpu.VMEM((TROWS + 2 * reach, L), F32)],
+        scratch_shapes=[pltpu.VMEM((16 + tms, L), F32), pltpu.VMEM((ext, L), F32)],
         compiler_params=SMALL,
-        name="gather_rows",
-    )(near, far, beam_rows, beam_cols, mixing)
+        name="band_windows",
+    )(*parts, home, other, beam_rows, beam_cols, mixing)
     own = windows[0:1]
     across = [flip(windows[h : h + 1], "band", 2 * h) for h in range(1, bands // 2)]
     mine = [own] + across

time: 33.8 us -> 33.3 us (0.985)
  waiting for transfers between devices: 12.3 us -> 13.2 us
  other arithmetic: 0.8 us -> 0 us
  Pallas kernels: 10 us -> 9.48 us
    ppermute x7, waiting for transfers between devices: 12.3 us -> 13.2 us  [flip(): return lax.ppermute(x, axis, [(i, i ^ bits) for i in range(count)])]
    concatenate x1 -> x0, other arithmetic: 0.8 us -> none  [on_device(): near = jnp.concatenate(gathered, axis=0)]
    pallas_call x1, Pallas kernels: 8.02 us -> 7.47 us  [on_device(): pl.pallas_call(functools.partial(filter_kernel, plan=plan), out_shape=jax...]
    unnamed x10 -> x11, local copies, waits for them, and re-layouts: 0.81 us -> 0.9 us
where the time goes in v3:
time: 33.3 us; the launch traced here: 33.1 us
  waiting for transfers between devices  13.2 us (40%)
  Pallas kernels  9.48 us (28%)
  starting transfers between devices  8.83 us (27%)
  local copies, waits for them, and re-layouts  0.91 us (3%)
  between operations  0.7 us (2%)
    ppermute x7, waiting for transfers between devices, flip(): return lax.ppermute(x, axis, [(i, i ^ bits) for i in range(count)])  13.2 us
    ppermute x7, starting transfers between devices, flip(): return lax.ppermute(x, axis, [(i, i ^ bits) for i in range(count)])  8.83 us
    pallas_call x1, Pallas kernels, on_device(): pl.pallas_call(functools.partial(filter_kernel, plan=plan), out_shape=jax...  7.47 us
    pallas_call x1, Pallas kernels, on_device(): pl.pallas_call(functools.partial(beam_kernel, share=share, reach=reach, t...  1.51 us
    unnamed x11, local copies, waits for them, and re-layouts  0.9 us
  transfers between devices with their start and end apart: 7, of which 5 were waited for; matrix products, arithmetic and copies ran while one was open for 0% of the time, Pallas kernels for 0%

profile of v3, /device:TPU:0, one launch (start us, length us, event | category | flops | bytes accessed | tf_op | source)
XLA Modules:
  0.0 33.1 jit_solution(5129533145054228398)
XLA Ops:
  0.7 7.5 %filter_blocks.1.refs_0_ = f32[88,128]{1,0:T(8,128)} custom-call(f32[1,64]{1,0:T(1,128)} %weights_in.1, bf16[1,64,8192]{2,1,0:T(8,128)(2,1)} %tod.1, bf16[1,64,2049]{2,1,0:T(8,128)(2,1)} %taps_in.1, s32[1,64]{1,0:T(1,128)} %bitcast.1, s32[1,64]{1,0:T(1,128)} %row_in.1, s32[1,1]{1,0:T(1,128)S(6)} %copy.11.counts_in), custom_call_target="tpu_custom_call" | custom-call | tf_op jit(solution)/shard_map/filter_blocks/pallas_call | solution.py:270
  8.1 3.1 %collective-permute-start = (f32[88,128]{1,0:T(8,128)}, f32[88,128]{1,0:T(8,128)S(1)}, u32[]{:S(2)}, u32[]{:S(2)}) collective-permute-start(f32[88,128]{1,0:T(8,128)} %filter_blocks.1.refs_0_), channel_id=1, source_target_pairs={{0,2},{1,3},{2,0},{3,1},{4,6},{5,7},{6,4},{7,5},{8,10},{9,11},{10,... | collective-permute-start | bytes 135176 | tf_op jit(solution)/shard_map/ppermute | solution.py:255
  11.2 2.6 %collective-permute-start.1 = (f32[88,128]{1,0:T(8,128)}, f32[88,128]{1,0:T(8,128)S(1)}, u32[]{:S(2)}, u32[]{:S(2)}) collective-permute-start(f32[88,128]{1,0:T(8,128)} %filter_blocks.1.refs_0_), channel_id=1, source_target_pairs={{0,4},{1,5},{2,6},{3,7},{4,0},{5,1},{6,2},{7,3},{8,12},{9,13},{10,... | collective-permute-start | bytes 135176 | tf_op jit(solution)/shard_map/ppermute | solution.py:255
  13.8 0.0 collective-permute-start.2
  13.8 0.0 collective-permute-done.refs_1_
  13.8 3.4 %collective-permute-done.1.refs_2_ = f32[88,128]{1,0:T(8,128)S(1)} collective-permute-done((f32[88,128]{1,0:T(8,128)}, f32[88,128]{1,0:T(8,128)S(1)}, u32[]{:S(2)}, u32[]{:S(2)}) %collective-permute-start.1) | collective-permute-done | bytes 45088 | tf_op jit(solution)/shard_map/ppermute | solution.py:255
  17.2 2.6 %collective-permute-done.2.refs_3_ = f32[88,128]{1,0:T(8,128)S(1)} collective-permute-done((f32[88,128]{1,0:T(8,128)}, f32[88,128]{1,0:T(8,128)S(1)}, u32[]{:S(2)}, u32[]{:S(2)}) %collective-permute-start.2) | collective-permute-done | bytes 45088 | tf_op jit(solution)/shard_map/ppermute | solution.py:255
  19.9 0.0 copy-start
  19.9 0.8 %copy-done = f32[88,128]{1,0:T(8,128)S(1)} copy-done((f32[88,128]{1,0:T(8,128)S(1)}, f32[88,128]{1,0:T(8,128)}, u32[]{:S(2)}) %copy-start) | copy-done | bytes 45080
  20.7 0.0 copy-start.1
  20.7 0.2 tile_rows.1
  20.9 0.0 copy-start.4
  20.9 1.6 %collective-permute-start.3 = (f32[232,128]{1,0:T(8,128)S(1)}, f32[232,128]{1,0:T(8,128)S(1)}, u32[]{:S(2)}, u32[]{:S(2)}) collective-permute-start(f32[232,128]{1,0:T(8,128)S(1)} %get-tuple-element.8), channel_id=1, source_target_pairs={{0,1},{1,0},{2,3},{3,2},{4,5},{5,4},{6,7},{7,6},{8,9},{9,8},{10,11... | collective-permute-start | bytes 356360 | tf_op jit(solution)/shard_map/ppermute | solution.py:255
  22.5 0.0 copy-done.4
  22.5 0.0 copy-start.3
  22.5 0.1 copy.10.refs_8_
  22.6 0.0 copy-start.2
  22.6 3.2 %collective-permute-done.3.refs_5_ = f32[232,128]{1,0:T(8,128)S(1)} collective-permute-done((f32[232,128]{1,0:T(8,128)S(1)}, f32[232,128]{1,0:T(8,128)S(1)}, u32[]{:S(2)}, u32[]{:S(2)}) %collective-permute-start.3) | collective-permute-done | bytes 118816 | tf_op jit(solution)/shard_map/ppermute | solution.py:255
  25.8 0.0 copy-done.1
  25.8 0.0 copy-done.3
  25.8 0.0 copy-done.2
  25.8 0.3 band_windows.1
  26.1 1.6 %collective-permute-start.4 = (f32[1,112,128]{2,1,0:T(8,128)S(1)}, f32[1,112,128]{2,1,0:T(8,128)S(1)}, u32[]{:S(2)}, u32[]{:S(2)}) collective-permute-start(f32[1,112,128]{2,1,0:T(8,128)S(1)} %get-tuple-element.9), channel_id=1, source_target_pairs={{0,16},{8,24},{16,0},{24,8},{1,17},{9,25},{17,1},{25,9},{2,18},{10... | collective-permute-start | bytes 172040 | tf_op jit(solution)/shard_map/ppermute | solution.py:255
  27.7 0.0 collective-permute-start.5
  27.7 2.7 %collective-permute-done.4.refs_1_ = f32[1,112,128]{2,1,0:T(8,128)S(1)} collective-permute-done((f32[1,112,128]{2,1,0:T(8,128)S(1)}, f32[1,112,128]{2,1,0:T(8,128)S(1)}, u32[]{:S(2)}, u32[]{:S(2)}) %collective-permute-start.4) | collective-permute-done | bytes 57376 | tf_op jit(solution)/shard_map/ppermute | solution.py:255
  30.4 0.0 collective-permute-start.6
  30.4 0.0 collective-permute-done.5.refs_2_
  30.4 1.2 %collective-permute-done.6.refs_3_ = f32[1,112,128]{2,1,0:T(8,128)S(1)} collective-permute-done((f32[1,112,128]{2,1,0:T(8,128)S(1)}, f32[1,112,128]{2,1,0:T(8,128)S(1)}, u32[]{:S(2)}, u32[]{:S(2)}) %collective-permute-start.6) | collective-permute-done | bytes 57376 | tf_op jit(solution)/shard_map/ppermute | solution.py:255
  31.6 1.5 %smooth_and_mix.1 = f32[4,1,32,128]{3,2,1,0:T(8,128)} custom-call(f32[1,112,128]{2,1,0:T(8,128)S(1)} %get-tuple-element.10.refs_0_, f32[1,112,128]{2,1,0:T(8,128)S(1)} %collective-permute-done.4.refs_1_, f32[1,112,128]{2,1,0:T(8,128)S(1)} %collective-permute-done.5.refs_2_, f32[1,112,128]{2,1,0:T(8,128)S(1)} %collective-permute-done.6.refs_3_), custom_call_target="tpu_custom_call" | custom-call | tf_op jit(solution)/shard_map/smooth_and_mix/pallas_call | solution.py:318
  (1 shorter events, 0.0 us)
Async XLA Ops:
  8.1 5.7 %collective-permute-start = (f32[88,128]{1,0:T(8,128)}, f32[88,128]{1,0:T(8,128)S(1)}, u32[]{:S(2)}, u32[]{:S(2)}) collective-permute-start(f32[88,128]{1,0:T(8,128)} %filter_blocks.1.refs_0_), channel_id=1, source_target_pairs={{0,2},{1,3},{2,0},{3,1},{4,6},{5,7},{6,4},{7,5},{8,10},{9,11},{10,... | collective-permute-start | bytes 135176 | tf_op jit(solution)/shard_map/ppermute | solution.py:255
  11.2 6.0 %collective-permute-start.1 = (f32[88,128]{1,0:T(8,128)}, f32[88,128]{1,0:T(8,128)S(1)}, u32[]{:S(2)}, u32[]{:S(2)}) collective-permute-start(f32[88,128]{1,0:T(8,128)} %filter_blocks.1.refs_0_), channel_id=1, source_target_pairs={{0,4},{1,5},{2,6},{3,7},{4,0},{5,1},{6,2},{7,3},{8,12},{9,13},{10,... | collective-permute-start | bytes 135176 | tf_op jit(solution)/shard_map/ppermute | solution.py:255
  13.8 6.1 %collective-permute-start.2 = (f32[88,128]{1,0:T(8,128)}, f32[88,128]{1,0:T(8,128)S(1)}, u32[]{:S(2)}, u32[]{:S(2)}) collective-permute-start(f32[88,128]{1,0:T(8,128)} %filter_blocks.1.refs_0_), channel_id=1, source_target_pairs={{0,6},{1,7},{2,4},{3,5},{4,2},{5,3},{6,0},{7,1},{8,14},{9,15},{10,... | collective-permute-start | bytes 135176 | tf_op jit(solution)/shard_map/ppermute | solution.py:255
  19.9 0.8 %copy-start = (f32[88,128]{1,0:T(8,128)S(1)}, f32[88,128]{1,0:T(8,128)}, u32[]{:S(2)}) copy-start(f32[88,128]{1,0:T(8,128)} %filter_blocks.1.refs_0_) | copy-start | bytes 135172
  20.7 5.2 %copy-start.1 = (f32[88,128]{1,0:T(8,128)S(1)}, f32[88,128]{1,0:T(8,128)}, u32[]{:S(2)}) copy-start(f32[88,128]{1,0:T(8,128)} %filter_blocks.1.refs_0_) | copy-start | bytes 135172
  20.9 1.6 %copy-start.4 = (f32[4,1,2]{0,2,1:T(2,128)S(1)}, f32[4,1,2]{0,2,1:T(2,128)}, u32[]{:S(2)}) copy-start(f32[4,1,2]{0,2,1:T(2,128)} %param.17) | copy-start | bytes 100
  20.9 4.9 %collective-permute-start.3 = (f32[232,128]{1,0:T(8,128)S(1)}, f32[232,128]{1,0:T(8,128)S(1)}, u32[]{:S(2)}, u32[]{:S(2)}) collective-permute-start(f32[232,128]{1,0:T(8,128)S(1)} %get-tuple-element.8), channel_id=1, source_target_pairs={{0,1},{1,0},{2,3},{3,2},{4,5},{5,4},{6,7},{7,6},{8,9},{9,8},{10,11... | collective-permute-start | bytes 356360 | tf_op jit(solution)/shard_map/ppermute | solution.py:255
  22.5 3.3 %copy-start.3 = (f32[1,2,33]{2,1,0:T(2,128)S(1)}, f32[1,2,33]{2,1,0:T(2,128)}, u32[]{:S(2)}) copy-start(f32[1,2,33]{2,1,0:T(2,128)} %refs_7_.1) | copy-start | bytes 796
  22.6 3.3 %copy-start.2 = (f32[1,2,33]{2,1,0:T(2,128)S(1)}, f32[1,2,33]{2,1,0:T(2,128)}, u32[]{:S(2)}) copy-start(f32[1,2,33]{2,1,0:T(2,128)} %refs_6_.1) | copy-start | bytes 796
  26.1 4.2 %collective-permute-start.4 = (f32[1,112,128]{2,1,0:T(8,128)S(1)}, f32[1,112,128]{2,1,0:T(8,128)S(1)}, u32[]{:S(2)}, u32[]{:S(2)}) collective-permute-start(f32[1,112,128]{2,1,0:T(8,128)S(1)} %get-tuple-element.9), channel_id=1, source_target_pairs={{0,16},{8,24},{16,0},{24,8},{1,17},{9,25},{17,1},{25,9},{2,18},{10... | collective-permute-start | bytes 172040 | tf_op jit(solution)/shard_map/ppermute | solution.py:255
  27.7 2.7 %collective-permute-start.5 = (f32[1,112,128]{2,1,0:T(8,128)S(1)}, f32[1,112,128]{2,1,0:T(8,128)S(1)}, u32[]{:S(2)}, u32[]{:S(2)}) collective-permute-start(f32[1,112,128]{2,1,0:T(8,128)S(1)} %get-tuple-element.10.refs_0_), channel_id=1, source_target_pairs={{0,8},{8,0},{16,24},{24,16},{1,9},{9,1},{17,25},{25,17},{2,10},{10... | collective-permute-start | bytes 172040 | tf_op jit(solution)/shard_map/ppermute | solution.py:255
  30.4 1.2 %collective-permute-start.6 = (f32[1,112,128]{2,1,0:T(8,128)S(1)}, f32[1,112,128]{2,1,0:T(8,128)S(1)}, u32[]{:S(2)}, u32[]{:S(2)}) collective-permute-start(f32[1,112,128]{2,1,0:T(8,128)S(1)} %collective-permute-done.4.refs_1_), channel_id=1, source_target_pairs={{0,8},{8,0},{16,24},{24,16},{1,9},{9,1},{17,25},{25,17},{2,10},{10... | collective-permute-start | bytes 172040 | tf_op jit(solution)/shard_map/ppermute | solution.py:255

commit v4 on v3

--- a/solution.py
+++ b/solution.py
@@ -13,7 +13,7 @@
 VMEM = pl.BlockSpec(memory_space=pltpu.VMEM)
 ANY = pl.BlockSpec(memory_space=pl.ANY)
 SMALL = pltpu.CompilerParams(vmem_limit_bytes=32 * 2**20)
-WHOLE = pltpu.CompilerParams(vmem_limit_bytes=60 * 2**20)
+WHOLE = pltpu.CompilerParams(vmem_limit_bytes=215 * 2**18)
 F32, BF16 = jnp.float32, jnp.bfloat16
 
 
@@ -141,52 +141,53 @@
 
 
 def tile_rows_kernel(*refs, plan, reach):
-    parts, (home, away) = refs[:-2], refs[-2:]
+    parts, (home, away, own, sem) = list(refs[:-4]), refs[-4:]
+    copy = pltpu.make_async_copy(parts[0], own, sem)
+    copy.start()
     nb, halo = plan.blocks, plan.reach
     me = lax.axis_index("tm")
     ext = TROWS + 2 * reach
-    target = jnp.concatenate([ref[plan.out : plan.out + 1, 0:nb] for ref in parts], axis=1)
-    blocks = jnp.concatenate([ref[halo : halo + nb, :] for ref in parts], axis=0)
-    for out, tile in ((home, me), (away, jnp.bitwise_xor(me, 1))):
-        picks = rows_of(target, (tile * TROWS - reach).astype(F32), ext)
-        out[0:ext, :] = add_rows(picks, blocks)
-    for k, ref in enumerate(parts):
-        at = ext + 2 * halo * k
-        away[at : at + halo, :] = ref[0:halo, :]
-        away[at + halo : at + 2 * halo, :] = ref[halo + nb : plan.out, :]
-    at = ext + 2 * halo * len(parts)
-    away[at:, :] = jnp.full((away.shape[0] - at, L), -1.0, F32)
-    for k, ref in enumerate(parts):
-        away[at + k : at + k + 1, :] = ref[plan.out : plan.out + 1, :]
-
-
-def windows_kernel(*refs, plan, outer, bands, reach):
-    parts = refs[:outer]
-    home, other, beam_rows, beam_cols, mixing, out, marks, tile = refs[outer:]
+    marks_at = ext + 2 * halo * len(parts)
+    away[marks_at:, :] = jnp.full((away.shape[0] - marks_at, L), -1.0, F32)
+
+    def add(some, first):
+        for k, ref in some:
+            at = ext + 2 * halo * k
+            away[at : at + halo, :] = ref[0:halo, :]
+            away[at + halo : at + 2 * halo, :] = ref[halo + nb : plan.out, :]
+            away[marks_at + k : marks_at + k + 1, :] = ref[plan.out : plan.out + 1, :]
+        target = jnp.concatenate([ref[plan.out : plan.out + 1, 0:nb] for _, ref in some], axis=1)
+        blocks = jnp.concatenate([ref[halo : halo + nb, :] for _, ref in some], axis=0)
+        for out, tile in ((home, me), (away, jnp.bitwise_xor(me, 1))):
+            rows = add_rows(rows_of(target, (tile * TROWS - reach).astype(F32), ext), blocks)
+            out[0:ext, :] = rows if first else out[0:ext, :] + rows
+
+    if len(parts) > 1:
+        add(list(enumerate(parts))[1:], True)
+    copy.wait()
+    add([(0, own)], len(parts) == 1)
+
+
+def windows_kernel(*refs, plan, order, bands, reach):
+    home, here, other, beam_rows, beam_cols, mixing, out, marks, tile = refs
     me = lax.axis_index("tm")
     mine = lax.axis_index("band") // 2
     nb, halo = plan.blocks, plan.reach
     ext = TROWS + 2 * reach
-    after_rows = ext + 2 * halo * outer
+    after_rows = ext + 2 * halo * len(order)
     marks[...] = jnp.full_like(marks, -1.0)
     numbers = []
-    for k, ref in enumerate(parts):
-        t = jnp.bitwise_xor(me, 2 * k)
-        marks[pl.ds(8 + t, 1), :] = ref[plan.out : plan.out + 1, :]
-        numbers.append(t)
-    for k in range(outer):
-        t = jnp.bitwise_xor(me, 2 * k + 1)
-        marks[pl.ds(8 + t, 1), :] = other[after_rows + k : after_rows + k + 1, :]
-        numbers.append(t)
+    for side, ref in enumerate((here, other)):
+        for k, z in enumerate(order):
+            t = jnp.bitwise_xor(me, 2 * z + side)
+            marks[pl.ds(8 + t, 1), :] = ref[after_rows + k : after_rows + k + 1, :]
+            numbers.append(t)
     targets = []
     for t in numbers:
         before = marks[pl.ds(7 + t, 1), :]
         after = marks[pl.ds(9 + t, 1), :]
         targets += [before[:, nb - halo : nb], after[:, 0:halo]]
-    blocks = []
-    for ref in parts:
-        blocks += [ref[0:halo, :], ref[halo + nb : plan.out, :]]
-    blocks.append(other[ext:after_rows, :])
+    blocks = [here[ext:after_rows, :], other[ext:after_rows, :]]
     picks = rows_of(jnp.concatenate(targets, axis=1), (me * TROWS - reach).astype(F32), ext)
     tile[...] = home[...] + other[0:ext, :] + add_rows(picks, jnp.concatenate(blocks, axis=0))
     share = TROWS // bands
@@ -287,13 +288,15 @@
         compiler_params=WHOLE,
         name="filter_blocks",
     )(det_weights, tod, filter_taps, owner[:, :, 0], tile_row, block_counts)
-    parts = [values] + [flip(values, "tm", k * inner) for k in range(1, outer)]
+    order = list(range(outer))
+    parts = [flip(values, "tm", k * inner) if k else values for k in order]
     ext = TROWS + 2 * reach
     sent = ext + 2 * plan.reach * outer + -(-outer // 8) * 8
     home, away = pl.pallas_call(
         functools.partial(tile_rows_kernel, plan=plan, reach=reach),
         out_shape=(jax.ShapeDtypeStruct((ext, L), F32), jax.ShapeDtypeStruct((sent, L), F32)),
-        in_specs=[VMEM] * outer,
+        in_specs=[ANY] + [VMEM] * (outer - 1),
+        scratch_shapes=[pltpu.VMEM((plan.out + 8, L), F32), pltpu.SemaphoreType.DMA],
         out_specs=(VMEM, VMEM),
         compiler_params=SMALL,
         name="tile_rows",
@@ -303,14 +306,14 @@
     wide = 2 * share + 2 * reach
     extra = -(-(2 * terms + comps * terms) // 8) * 8
     windows = pl.pallas_call(
-        functools.partial(windows_kernel, plan=plan, outer=outer, bands=bands, reach=reach),
+        functools.partial(windows_kernel, plan=plan, order=order, bands=bands, reach=reach),
         out_shape=jax.ShapeDtypeStruct((bands // 2, wide + extra, L), F32),
-        in_specs=[VMEM] * (outer + 5),
+        in_specs=[VMEM] * 6,
         out_specs=VMEM,
         scratch_shapes=[pltpu.VMEM((16 + tms, L), F32), pltpu.VMEM((ext, L), F32)],
         compiler_params=SMALL,
         name="band_windows",
-    )(*parts, home, other, beam_rows, beam_cols, mixing)
+    )(home, away, other, beam_rows, beam_cols, mixing)
     own = windows[0:1]
     across = [flip(windows[h : h + 1], "band", 2 * h) for h in range(1, bands // 2)]
     mine = [own] + across

time: 33.3 us -> 31.1 us (0.934)
  waiting for transfers between devices: 13.2 us -> 11.4 us
  Pallas kernels: 9.48 us -> 9.08 us
    ppermute x7, waiting for transfers between devices: 13.2 us -> 11.4 us  [flip(): return lax.ppermute(x, axis, [(i, i ^ bits) for i in range(count)])]
    pallas_call x1, Pallas kernels: 7.47 us -> 6.85 us  [on_device(): pl.pallas_call(functools.partial(filter_kernel, plan=plan), out_shape=jax...]
    unnamed x11 -> x13, local copies, waits for them, and re-layouts: 0.9 us -> 0.77 us
where the time goes in v4:
time: 31.1 us; the launch traced here: 30.9 us
  waiting for transfers between devices  11.4 us (37%)
  Pallas kernels  9.08 us (29%)
  starting transfers between devices  8.9 us (29%)
  local copies, waits for them, and re-layouts  0.78 us (3%)
  between operations  0.73 us (2%)
    ppermute x7, waiting for transfers between devices, flip(): return lax.ppermute(x, axis, [(i, i ^ bits) for i in range(count)])  11.4 us
    ppermute x7, starting transfers between devices, flip(): return lax.ppermute(x, axis, [(i, i ^ bits) for i in range(count)])  8.9 us
    pallas_call x1, Pallas kernels, on_device(): pl.pallas_call(functools.partial(filter_kernel, plan=plan), out_shape=jax...  6.85 us
    pallas_call x1, Pallas kernels, on_device(): pl.pallas_call(functools.partial(beam_kernel, share=share, reach=reach, t...  1.51 us
    unnamed x13, local copies, waits for them, and re-layouts  0.77 us
  transfers between devices with their start and end apart: 7, of which 5 were waited for; matrix products, arithmetic and copies ran while one was open for 0% of the time, Pallas kernels for 0%

profile of v4, /device:TPU:0, one launch (start us, length us, event | category | flops | bytes accessed | tf_op | source)
XLA Modules:
  0.0 30.9 jit_solution(16050936467394156867)
XLA Ops:
  0.7 0.0 copy-start.2
  0.7 0.0 copy-start.3
  0.7 0.0 copy-start.4
  0.7 0.6 %copy-done.2 = f32[1,64]{1,0:T(1,128)S(1)} copy-done((f32[1,64]{1,0:T(1,128)S(1)}, f32[1,64]{1,0:T(1,128)}, u32[]{:S(2)}) %copy-start.2) | copy-done | bytes 280
  1.3 0.0 copy-done.3
  1.3 0.0 copy-done.4
  1.3 6.9 %filter_blocks.1.refs_0_ = f32[88,128]{1,0:T(8,128)S(1)} custom-call(f32[1,64]{1,0:T(1,128)S(1)} %copy-done.2, bf16[1,64,8192]{2,1,0:T(8,128)(2,1)} %tod.1, bf16[1,64,2049]{2,1,0:T(8,128)(2,1)} %taps_in.1, s32[1,64]{1,0:T(1,128)S(1)} %bitcast.1, s32[1,64]{1,0:T(1,128)S(1)} %copy-done.4, s32[1,1]{1,0:T(1,128)S(6)} %copy.11.counts_in), custom_call_target="tpu_custom_call" | custom-call | tf_op jit(solution)/shard_map/filter_blocks/pallas_call | solution.py:271
  8.2 5.1 %collective-permute-start.2 = (f32[88,128]{1,0:T(8,128)S(1)}, f32[88,128]{1,0:T(8,128)S(1)}, u32[]{:S(2)}, u32[]{:S(2)}) collective-permute-start(f32[88,128]{1,0:T(8,128)S(1)} %filter_blocks.1.refs_0_), channel_id=1, source_target_pairs={{0,6},{1,7},{2,4},{3,5},{4,2},{5,3},{6,0},{7,1},{8,14},{9,15},{10,... | collective-permute-start | bytes 135176 | tf_op jit(solution)/shard_map/ppermute | solution.py:256
  13.3 0.0 collective-permute-start.1
  13.3 0.6 %collective-permute-start = (f32[88,128]{1,0:T(8,128)S(1)}, f32[88,128]{1,0:T(8,128)S(1)}, u32[]{:S(2)}, u32[]{:S(2)}) collective-permute-start(f32[88,128]{1,0:T(8,128)S(1)} %filter_blocks.1.refs_0_), channel_id=1, source_target_pairs={{0,2},{1,3},{2,0},{3,1},{4,6},{5,7},{6,4},{7,5},{8,10},{9,11},{10,... | collective-permute-start | bytes 135176 | tf_op jit(solution)/shard_map/ppermute | solution.py:256
  14.0 1.4 %collective-permute-done.2.refs_3_ = f32[88,128]{1,0:T(8,128)S(1)} collective-permute-done((f32[88,128]{1,0:T(8,128)S(1)}, f32[88,128]{1,0:T(8,128)S(1)}, u32[]{:S(2)}, u32[]{:S(2)}) %collective-permute-start.2) | collective-permute-done | bytes 45088 | tf_op jit(solution)/shard_map/ppermute | solution.py:256
  15.4 2.9 %collective-permute-done.1.refs_2_ = f32[88,128]{1,0:T(8,128)S(1)} collective-permute-done((f32[88,128]{1,0:T(8,128)S(1)}, f32[88,128]{1,0:T(8,128)S(1)}, u32[]{:S(2)}, u32[]{:S(2)}) %collective-permute-start.1) | collective-permute-done | bytes 45088 | tf_op jit(solution)/shard_map/ppermute | solution.py:256
  18.3 0.0 collective-permute-done.refs_1_
  18.3 0.5 %tile_rows.1 = (f32[160,128]{1,0:T(8,128)S(1)}, f32[232,128]{1,0:T(8,128)S(1)}) custom-call(f32[88,128]{1,0:T(8,128)S(1)} %filter_blocks.1.refs_0_, f32[88,128]{1,0:T(8,128)S(1)} %collective-permute-done.refs_1_, f32[88,128]{1,0:T(8,128)S(1)} %collective-permute-done.1.refs_2_, f32[88,128]{1,0:T(8,128)S(1)} %collective-permute-done.2.refs_3_), custom_call_target="tpu_custom_call" | custom-call | tf_op jit(solution)/shard_map/tile_rows/pallas_call | solution.py:295
  18.7 0.0 copy-start.5
  18.8 1.6 %collective-permute-start.3 = (f32[232,128]{1,0:T(8,128)S(1)}, f32[232,128]{1,0:T(8,128)S(1)}, u32[]{:S(2)}, u32[]{:S(2)}) collective-permute-start(f32[232,128]{1,0:T(8,128)S(1)} %get-tuple-element.8.refs_1_), channel_id=1, source_target_pairs={{0,1},{1,0},{2,3},{3,2},{4,5},{5,4},{6,7},{7,6},{8,9},{9,8},{10,11... | collective-permute-start | bytes 356360 | tf_op jit(solution)/shard_map/ppermute | solution.py:256
  20.3 0.0 copy-done.5
  20.3 0.0 copy-start.1
  20.3 0.1 copy.10.refs_5_
  20.4 0.0 copy-start
  20.4 3.2 %collective-permute-done.3.refs_2_ = f32[232,128]{1,0:T(8,128)S(1)} collective-permute-done((f32[232,128]{1,0:T(8,128)S(1)}, f32[232,128]{1,0:T(8,128)S(1)}, u32[]{:S(2)}, u32[]{:S(2)}) %collective-permute-start.3) | collective-permute-done | bytes 118816 | tf_op jit(solution)/shard_map/ppermute | solution.py:256
  23.7 0.0 copy-done.1
  23.7 0.0 copy-done
  23.7 0.3 band_windows.1
  23.9 1.6 %collective-permute-start.4 = (f32[1,112,128]{2,1,0:T(8,128)S(1)}, f32[1,112,128]{2,1,0:T(8,128)S(1)}, u32[]{:S(2)}, u32[]{:S(2)}) collective-permute-start(f32[1,112,128]{2,1,0:T(8,128)S(1)} %get-tuple-element.9), channel_id=1, source_target_pairs={{0,16},{8,24},{16,0},{24,8},{1,17},{9,25},{17,1},{25,9},{2,18},{10... | collective-permute-start | bytes 172040 | tf_op jit(solution)/shard_map/ppermute | solution.py:256
  25.5 0.0 collective-permute-start.5
  25.5 2.7 %collective-permute-done.4.refs_1_ = f32[1,112,128]{2,1,0:T(8,128)S(1)} collective-permute-done((f32[1,112,128]{2,1,0:T(8,128)S(1)}, f32[1,112,128]{2,1,0:T(8,128)S(1)}, u32[]{:S(2)}, u32[]{:S(2)}) %collective-permute-start.4) | collective-permute-done | bytes 57376 | tf_op jit(solution)/shard_map/ppermute | solution.py:256
  28.2 0.0 collective-permute-start.6
  28.2 0.0 collective-permute-done.5.refs_2_
  28.2 1.2 %collective-permute-done.6.refs_3_ = f32[1,112,128]{2,1,0:T(8,128)S(1)} collective-permute-done((f32[1,112,128]{2,1,0:T(8,128)S(1)}, f32[1,112,128]{2,1,0:T(8,128)S(1)}, u32[]{:S(2)}, u32[]{:S(2)}) %collective-permute-start.6) | collective-permute-done | bytes 57376 | tf_op jit(solution)/shard_map/ppermute | solution.py:256
  29.4 1.5 %smooth_and_mix.1 = f32[4,1,32,128]{3,2,1,0:T(8,128)} custom-call(f32[1,112,128]{2,1,0:T(8,128)S(1)} %get-tuple-element.10.refs_0_, f32[1,112,128]{2,1,0:T(8,128)S(1)} %collective-permute-done.4.refs_1_, f32[1,112,128]{2,1,0:T(8,128)S(1)} %collective-permute-done.5.refs_2_, f32[1,112,128]{2,1,0:T(8,128)S(1)} %collective-permute-done.6.refs_3_), custom_call_target="tpu_custom_call" | custom-call | tf_op jit(solution)/shard_map/smooth_and_mix/pallas_call | solution.py:321
  (1 shorter events, 0.0 us)
Async XLA Ops:
  0.7 0.7 %copy-start.2 = (f32[1,64]{1,0:T(1,128)S(1)}, f32[1,64]{1,0:T(1,128)}, u32[]{:S(2)}) copy-start(f32[1,64]{1,0:T(1,128)} %weights_in.1) | copy-start | bytes 772
  0.7 0.7 %copy-start.3 = (s32[1,64,1]{1,2,0:T(1,128)S(1)}, s32[1,64,1]{1,2,0:T(1,128)}, u32[]{:S(2)}) copy-start(s32[1,64,1]{1,2,0:T(1,128)} %param.12) | copy-start | bytes 772
  0.7 0.7 %copy-start.4 = (s32[1,64]{1,0:T(1,128)S(1)}, s32[1,64]{1,0:T(1,128)}, u32[]{:S(2)}) copy-start(s32[1,64]{1,0:T(1,128)} %row_in.1) | copy-start | bytes 772
  8.2 7.2 %collective-permute-start.2 = (f32[88,128]{1,0:T(8,128)S(1)}, f32[88,128]{1,0:T(8,128)S(1)}, u32[]{:S(2)}, u32[]{:S(2)}) collective-permute-start(f32[88,128]{1,0:T(8,128)S(1)} %filter_blocks.1.refs_0_), channel_id=1, source_target_pairs={{0,6},{1,7},{2,4},{3,5},{4,2},{5,3},{6,0},{7,1},{8,14},{9,15},{10,... | collective-permute-start | bytes 135176 | tf_op jit(solution)/shard_map/ppermute | solution.py:256
  13.3 4.9 %collective-permute-start.1 = (f32[88,128]{1,0:T(8,128)S(1)}, f32[88,128]{1,0:T(8,128)S(1)}, u32[]{:S(2)}, u32[]{:S(2)}) collective-permute-start(f32[88,128]{1,0:T(8,128)S(1)} %filter_blocks.1.refs_0_), channel_id=1, source_target_pairs={{0,4},{1,5},{2,6},{3,7},{4,0},{5,1},{6,2},{7,3},{8,12},{9,13},{10,... | collective-permute-start | bytes 135176 | tf_op jit(solution)/shard_map/ppermute | solution.py:256
  13.3 4.9 %collective-permute-start = (f32[88,128]{1,0:T(8,128)S(1)}, f32[88,128]{1,0:T(8,128)S(1)}, u32[]{:S(2)}, u32[]{:S(2)}) collective-permute-start(f32[88,128]{1,0:T(8,128)S(1)} %filter_blocks.1.refs_0_), channel_id=1, source_target_pairs={{0,2},{1,3},{2,0},{3,1},{4,6},{5,7},{6,4},{7,5},{8,10},{9,11},{10,... | collective-permute-start | bytes 135176 | tf_op jit(solution)/shard_map/ppermute | solution.py:256
  18.7 1.6 %copy-start.5 = (f32[4,1,2]{0,2,1:T(2,128)S(1)}, f32[4,1,2]{0,2,1:T(2,128)}, u32[]{:S(2)}) copy-start(f32[4,1,2]{0,2,1:T(2,128)} %param.17) | copy-start | bytes 100
  18.8 4.9 %collective-permute-start.3 = (f32[232,128]{1,0:T(8,128)S(1)}, f32[232,128]{1,0:T(8,128)S(1)}, u32[]{:S(2)}, u32[]{:S(2)}) collective-permute-start(f32[232,128]{1,0:T(8,128)S(1)} %get-tuple-element.8.refs_1_), channel_id=1, source_target_pairs={{0,1},{1,0},{2,3},{3,2},{4,5},{5,4},{6,7},{7,6},{8,9},{9,8},{10,11... | collective-permute-start | bytes 356360 | tf_op jit(solution)/shard_map/ppermute | solution.py:256
  20.3 3.3 %copy-start.1 = (f32[1,2,33]{2,1,0:T(2,128)S(1)}, f32[1,2,33]{2,1,0:T(2,128)}, u32[]{:S(2)}) copy-start(f32[1,2,33]{2,1,0:T(2,128)} %refs_4_.1) | copy-start | bytes 796
  20.4 3.3 %copy-start = (f32[1,2,33]{2,1,0:T(2,128)S(1)}, f32[1,2,33]{2,1,0:T(2,128)}, u32[]{:S(2)}) copy-start(f32[1,2,33]{2,1,0:T(2,128)} %refs_3_.1) | copy-start | bytes 796
  23.9 4.2 %collective-permute-start.4 = (f32[1,112,128]{2,1,0:T(8,128)S(1)}, f32[1,112,128]{2,1,0:T(8,128)S(1)}, u32[]{:S(2)}, u32[]{:S(2)}) collective-permute-start(f32[1,112,128]{2,1,0:T(8,128)S(1)} %get-tuple-element.9), channel_id=1, source_target_pairs={{0,16},{8,24},{16,0},{24,8},{1,17},{9,25},{17,1},{25,9},{2,18},{10... | collective-permute-start | bytes 172040 | tf_op jit(solution)/shard_map/ppermute | solution.py:256
  25.5 2.7 %collective-permute-start.5 = (f32[1,112,128]{2,1,0:T(8,128)S(1)}, f32[1,112,128]{2,1,0:T(8,128)S(1)}, u32[]{:S(2)}, u32[]{:S(2)}) collective-permute-start(f32[1,112,128]{2,1,0:T(8,128)S(1)} %get-tuple-element.10.refs_0_), channel_id=1, source_target_pairs={{0,8},{8,0},{16,24},{24,16},{1,9},{9,1},{17,25},{25,17},{2,10},{10... | collective-permute-start | bytes 172040 | tf_op jit(solution)/shard_map/ppermute | solution.py:256
  28.2 1.2 %collective-permute-start.6 = (f32[1,112,128]{2,1,0:T(8,128)S(1)}, f32[1,112,128]{2,1,0:T(8,128)S(1)}, u32[]{:S(2)}, u32[]{:S(2)}) collective-permute-start(f32[1,112,128]{2,1,0:T(8,128)S(1)} %collective-permute-done.4.refs_1_), channel_id=1, source_target_pairs={{0,8},{8,0},{16,24},{24,16},{1,9},{9,1},{17,25},{25,17},{2,10},{10... | collective-permute-start | bytes 172040 | tf_op jit(solution)/shard_map/ppermute | solution.py:256

commit v5 on v4

--- a/solution.py
+++ b/solution.py
@@ -140,46 +140,86 @@
     return both[:, :L] + both[:, L:]
 
 
-def tile_rows_kernel(*refs, plan, reach):
-    parts, (home, away, own, sem) = list(refs[:-4]), refs[-4:]
-    copy = pltpu.make_async_copy(parts[0], own, sem)
-    copy.start()
+def gather_rounds(count):
+    if count != 4:
+        return [[(i, i ^ k) for i in range(count)] for k in range(1, count)]
+    last = count - 1
+    ring = [[(i, (i + k) % last) for i in range(last)] for k in range(1, last)]
+    return ring + [[(i, last), (last, i)] for i in range(last)]
+
+
+def slots(rounds, count):
+    found = []
+    seen = [0] * count
+    for r, pairs in enumerate(rounds):
+        for _, target in pairs:
+            if seen[target] == len(found):
+                found.append({})
+            found[seen[target]].setdefault(r, []).append(target)
+            seen[target] += 1
+    return [sorted(slot.items()) for slot in found]
+
+
+def sources(rounds, count):
+    table = [[] for _ in range(count)]
+    for pairs in rounds:
+        for source, target in pairs:
+            table[target].append(source)
+    return [[table[p][k] for p in range(count)] for k in range(count - 1)]
+
+
+def pick(place, values):
+    result = jnp.int32(values[0])
+    for p, value in enumerate(values):
+        result = jnp.where(place == p, value, result)
+    return result
+
+
+def tile_rows_kernel(*refs, plan, reach, rounds, outer):
+    arrived, (home, away, kept) = refs[:-3], refs[-3:]
     nb, halo = plan.blocks, plan.reach
     me = lax.axis_index("tm")
+    parts = [arrived[0]]
+    if rounds:
+        place = me // 2
+        for k, slot in enumerate(slots(rounds, outer)):
+            total = None
+            for r, places in slot:
+                part = arrived[1 + r][...]
+                if len(places) < outer:
+                    hit = functools.reduce(jnp.logical_or, [place == p for p in places])
+                    part = jnp.where(hit, part, 0.0)
+                total = part if total is None else total + part
+            kept[k] = total
+            parts.append(kept.at[k])
     ext = TROWS + 2 * reach
     marks_at = ext + 2 * halo * len(parts)
     away[marks_at:, :] = jnp.full((away.shape[0] - marks_at, L), -1.0, F32)
 
-    def add(some, first):
-        for k, ref in some:
-            at = ext + 2 * halo * k
-            away[at : at + halo, :] = ref[0:halo, :]
-            away[at + halo : at + 2 * halo, :] = ref[halo + nb : plan.out, :]
-            away[marks_at + k : marks_at + k + 1, :] = ref[plan.out : plan.out + 1, :]
-        target = jnp.concatenate([ref[plan.out : plan.out + 1, 0:nb] for _, ref in some], axis=1)
-        blocks = jnp.concatenate([ref[halo : halo + nb, :] for _, ref in some], axis=0)
-        for out, tile in ((home, me), (away, jnp.bitwise_xor(me, 1))):
-            rows = add_rows(rows_of(target, (tile * TROWS - reach).astype(F32), ext), blocks)
-            out[0:ext, :] = rows if first else out[0:ext, :] + rows
-
-    if len(parts) > 1:
-        add(list(enumerate(parts))[1:], True)
-    copy.wait()
-    add([(0, own)], len(parts) == 1)
-
-
-def windows_kernel(*refs, plan, order, bands, reach):
+    for k, ref in enumerate(parts):
+        at = ext + 2 * halo * k
+        away[at : at + halo, :] = ref[0:halo, :]
+        away[at + halo : at + 2 * halo, :] = ref[halo + nb : plan.out, :]
+        away[marks_at + k : marks_at + k + 1, :] = ref[plan.out : plan.out + 1, :]
+    target = jnp.concatenate([ref[plan.out : plan.out + 1, 0:nb] for ref in parts], axis=1)
+    blocks = jnp.concatenate([ref[halo : halo + nb, :] for ref in parts], axis=0)
+    for out, tile in ((home, me), (away, jnp.bitwise_xor(me, 1))):
+        out[0:ext, :] = add_rows(rows_of(target, (tile * TROWS - reach).astype(F32), ext), blocks)
+
+
+def windows_kernel(*refs, plan, origins, outer, bands, reach):
     home, here, other, beam_rows, beam_cols, mixing, out, marks, tile = refs
     me = lax.axis_index("tm")
     mine = lax.axis_index("band") // 2
     nb, halo = plan.blocks, plan.reach
     ext = TROWS + 2 * reach
-    after_rows = ext + 2 * halo * len(order)
+    after_rows = ext + 2 * halo * outer
     marks[...] = jnp.full_like(marks, -1.0)
     numbers = []
     for side, ref in enumerate((here, other)):
-        for k, z in enumerate(order):
-            t = jnp.bitwise_xor(me, 2 * z + side)
+        for k in range(outer):
+            place = pick(me // 2, origins[k - 1]) if k else me // 2
+            t = 2 * place + jnp.bitwise_xor(lax.rem(me, 2), side)
             marks[pl.ds(8 + t, 1), :] = ref[after_rows + k : after_rows + k + 1, :]
             numbers.append(t)
     targets = []
@@ -288,15 +328,16 @@
         compiler_params=WHOLE,
         name="filter_blocks",
     )(det_weights, tod, filter_taps, owner[:, :, 0], tile_row, block_counts)
-    order = list(range(outer))
-    parts = [flip(values, "tm", k * inner) if k else values for k in order]
+    rounds = gather_rounds(outer)
+    pairs = [[(s * inner + i, t * inner + i) for s, t in r for i in range(inner)] for r in rounds]
+    parts = [values] + [lax.ppermute(values, "tm", p) for p in pairs]
     ext = TROWS + 2 * reach
     sent = ext + 2 * plan.reach * outer + -(-outer // 8) * 8
     home, away = pl.pallas_call(
-        functools.partial(tile_rows_kernel, plan=plan, reach=reach),
+        functools.partial(tile_rows_kernel, plan=plan, reach=reach, rounds=rounds, outer=outer),
         out_shape=(jax.ShapeDtypeStruct((ext, L), F32), jax.ShapeDtypeStruct((sent, L), F32)),
-        in_specs=[ANY] + [VMEM] * (outer - 1),
-        scratch_shapes=[pltpu.VMEM((plan.out + 8, L), F32), pltpu.SemaphoreType.DMA],
+        in_specs=[VMEM] * len(parts),
+        scratch_shapes=[pltpu.VMEM((max(outer - 1, 1), plan.out + 8, L), F32)],
         out_specs=(VMEM, VMEM),
         compiler_params=SMALL,
         name="tile_rows",
@@ -306,7 +347,7 @@
     wide = 2 * share + 2 * reach
     extra = -(-(2 * terms + comps * terms) // 8) * 8
     windows = pl.pallas_call(
-        functools.partial(windows_kernel, plan=plan, order=order, bands=bands, reach=reach),
+        functools.partial(windows_kernel, plan=plan, origins=sources(rounds, outer), outer=outer, bands=bands, reach=reach),
         out_shape=jax.ShapeDtypeStruct((bands // 2, wide + extra, L), F32),
         in_specs=[VMEM] * 6,
         out_specs=VMEM,

time: 31.1 us -> 38 us (1.22)
  the two profiles are of different devices: /device:TPU:0 before, /device:TPU:29 now
where the time goes in v5:
time: 38 us; the launch traced here: 37.8 us
  starting transfers between devices  21.2 us (56%)
  Pallas kernels  8.89 us (23%)
  waiting for transfers between devices  6.11 us (16%)
  local copies, waits for them, and re-layouts  0.78 us (2%)
  between operations  0.78 us (2%)
    ppermute x5, starting transfers between devices, on_device(): parts = [values] + [lax.ppermute(values, 'tm', p) for p in pairs]  11.9 us
    ppermute x4, starting transfers between devices, flip(): return lax.ppermute(x, axis, [(i, i ^ bits) for i in range(count)])  9.33 us
    pallas_call x1, Pallas kernels, on_device(): pl.pallas_call(functools.partial(filter_kernel, plan=plan), out_shape=jax...  6.85 us
    ppermute x4, waiting for transfers between devices, flip(): return lax.ppermute(x, axis, [(i, i ^ bits) for i in range(count)])  3.27 us
    ppermute x5, waiting for transfers between devices, on_device(): parts = [values] + [lax.ppermute(values, 'tm', p) for p in pairs]  2.84 us
    pallas_call x1, Pallas kernels, on_device(): pl.pallas_call(functools.partial(beam_kernel, share=share, reach=reach, t...  1.51 us
    unnamed x13, local copies, waits for them, and re-layouts  0.77 us
  transfers between devices with their start and end apart: 9, of which 4 were waited for; matrix products, arithmetic and copies ran while one was open for 0% of the time, Pallas kernels for 0%

profile of v5, /device:TPU:29, one launch (start us, length us, event | category | flops | bytes accessed | tf_op | source)
XLA Modules:
  0.0 37.8 jit_solution(7730547590218692233)
XLA Ops:
  0.7 0.0 copy-start.2
  0.7 0.0 copy-start.3
  0.7 0.0 copy-start.4
  0.7 0.6 %copy-done.2 = f32[1,64]{1,0:T(1,128)S(1)} copy-done((f32[1,64]{1,0:T(1,128)S(1)}, f32[1,64]{1,0:T(1,128)}, u32[]{:S(2)}) %copy-start.2) | copy-done | bytes 280
  1.3 0.0 copy-done.3
  1.3 0.0 copy-done.4
  1.3 6.9 %filter_blocks.1.refs_0_ = f32[88,128]{1,0:T(8,128)S(1)} custom-call(f32[1,64]{1,0:T(1,128)S(1)} %copy-done.2, bf16[1,64,8192]{2,1,0:T(8,128)(2,1)} %tod.1, bf16[1,64,2049]{2,1,0:T(8,128)(2,1)} %taps_in.1, s32[1,64]{1,0:T(1,128)S(1)} %bitcast.1, s32[1,64]{1,0:T(1,128)S(1)} %copy-done.4, s32[1,1]{1,0:T(1,128)S(6)} %copy.11.counts_in), custom_call_target="tpu_custom_call" | custom-call | tf_op jit(solution)/shard_map/filter_blocks/pallas_call | solution.py:311
  8.2 0.7 %collective-permute-start = (f32[88,128]{1,0:T(8,128)S(1)}, f32[88,128]{1,0:T(8,128)S(1)}, u32[]{:S(2)}, u32[]{:S(2)}) collective-permute-start(f32[88,128]{1,0:T(8,128)S(1)} %filter_blocks.1.refs_0_), channel_id=1, source_target_pairs={{0,2},{1,3},{2,4},{3,5},{4,0},{5,1},{8,10},{9,11},{10,12},{11,13},... | collective-permute-start | bytes 135176 | tf_op jit(solution)/shard_map/ppermute | solution.py:333
  8.9 0.7 %collective-permute-start.1 = (f32[88,128]{1,0:T(8,128)S(1)}, f32[88,128]{1,0:T(8,128)S(1)}, u32[]{:S(2)}, u32[]{:S(2)}) collective-permute-start(f32[88,128]{1,0:T(8,128)S(1)} %filter_blocks.1.refs_0_), channel_id=1, source_target_pairs={{0,4},{1,5},{2,0},{3,1},{4,2},{5,3},{8,12},{9,13},{10,8},{11,9},{1... | collective-permute-start | bytes 135176 | tf_op jit(solution)/shard_map/ppermute | solution.py:333
  9.5 6.7 %collective-permute-start.2 = (f32[88,128]{1,0:T(8,128)S(1)}, f32[88,128]{1,0:T(8,128)S(1)}, u32[]{:S(2)}, u32[]{:S(2)}) collective-permute-start(f32[88,128]{1,0:T(8,128)S(1)} %filter_blocks.1.refs_0_), channel_id=1, source_target_pairs={{0,6},{1,7},{6,0},{7,1},{8,14},{9,15},{14,8},{15,9},{16,22},{17,23... | collective-permute-start | bytes 135176 | tf_op jit(solution)/shard_map/ppermute | solution.py:333
  16.3 1.9 %collective-permute-start.3 = (f32[88,128]{1,0:T(8,128)S(1)}, f32[88,128]{1,0:T(8,128)S(1)}, u32[]{:S(2)}, u32[]{:S(2)}) collective-permute-start(f32[88,128]{1,0:T(8,128)S(1)} %filter_blocks.1.refs_0_), channel_id=1, source_target_pairs={{2,6},{3,7},{6,2},{7,3},{10,14},{11,15},{14,10},{15,11},{18,22},{1... | collective-permute-start | bytes 135176 | tf_op jit(solution)/shard_map/ppermute | solution.py:333
  18.2 1.9 %collective-permute-start.4 = (f32[88,128]{1,0:T(8,128)S(1)}, f32[88,128]{1,0:T(8,128)S(1)}, u32[]{:S(2)}, u32[]{:S(2)}) collective-permute-start(f32[88,128]{1,0:T(8,128)S(1)} %filter_blocks.1.refs_0_), channel_id=1, source_target_pairs={{4,6},{5,7},{6,4},{7,5},{12,14},{13,15},{14,12},{15,13},{20,22},{2... | collective-permute-start | bytes 135176 | tf_op jit(solution)/shard_map/ppermute | solution.py:333
  20.1 0.0 collective-permute-done.refs_1_
  20.1 0.0 collective-permute-done.1.refs_2_
  20.1 0.0 collective-permute-done.2.refs_3_
  20.1 1.8 %collective-permute-done.3.refs_4_ = f32[88,128]{1,0:T(8,128)S(1)} collective-permute-done((f32[88,128]{1,0:T(8,128)S(1)}, f32[88,128]{1,0:T(8,128)S(1)}, u32[]{:S(2)}, u32[]{:S(2)}) %collective-permute-start.3) | collective-permute-done | bytes 45088 | tf_op jit(solution)/shard_map/ppermute | solution.py:333
  21.9 1.0 %collective-permute-done.4.refs_5_ = f32[88,128]{1,0:T(8,128)S(1)} collective-permute-done((f32[88,128]{1,0:T(8,128)S(1)}, f32[88,128]{1,0:T(8,128)S(1)}, u32[]{:S(2)}, u32[]{:S(2)}) %collective-permute-start.4) | collective-permute-done | bytes 45088 | tf_op jit(solution)/shard_map/ppermute | solution.py:333
  23.0 0.3 tile_rows.1
  23.2 0.0 copy-start.5
  23.3 1.3 %collective-permute-start.5 = (f32[232,128]{1,0:T(8,128)S(1)}, f32[232,128]{1,0:T(8,128)S(1)}, u32[]{:S(2)}, u32[]{:S(2)}) collective-permute-start(f32[232,128]{1,0:T(8,128)S(1)} %get-tuple-element.8.refs_1_), channel_id=1, source_target_pairs={{0,1},{1,0},{2,3},{3,2},{4,5},{5,4},{6,7},{7,6},{8,9},{9,8},{10,11... | collective-permute-start | bytes 356360 | tf_op jit(solution)/shard_map/ppermute | solution.py:296
  24.5 0.0 copy-done.5
  24.5 0.0 copy-start.1
  24.5 0.1 copy.10.refs_5_
  24.6 0.0 copy-start
  24.6 2.4 %collective-permute-done.5.refs_2_ = f32[232,128]{1,0:T(8,128)S(1)} collective-permute-done((f32[232,128]{1,0:T(8,128)S(1)}, f32[232,128]{1,0:T(8,128)S(1)}, u32[]{:S(2)}, u32[]{:S(2)}) %collective-permute-start.5) | collective-permute-done | bytes 118816 | tf_op jit(solution)/shard_map/ppermute | solution.py:296
  27.0 0.0 copy-done.1
  27.0 0.0 copy-done
  27.0 0.3 band_windows.1
  27.3 0.2 collective-permute-start.6
  27.6 3.8 %collective-permute-start.7 = (f32[1,112,128]{2,1,0:T(8,128)S(1)}, f32[1,112,128]{2,1,0:T(8,128)S(1)}, u32[]{:S(2)}, u32[]{:S(2)}) collective-permute-start(f32[1,112,128]{2,1,0:T(8,128)S(1)} %get-tuple-element.10.refs_0_), channel_id=1, source_target_pairs={{0,8},{8,0},{16,24},{24,16},{1,9},{9,1},{17,25},{25,17},{2,10},{10... | collective-permute-start | bytes 172040 | tf_op jit(solution)/shard_map/ppermute | solution.py:296
  31.4 0.0 collective-permute-done.6.refs_1_
  31.4 4.0 %collective-permute-start.8 = (f32[1,112,128]{2,1,0:T(8,128)S(1)}, f32[1,112,128]{2,1,0:T(8,128)S(1)}, u32[]{:S(2)}, u32[]{:S(2)}) collective-permute-start(f32[1,112,128]{2,1,0:T(8,128)S(1)} %collective-permute-done.6.refs_1_), channel_id=1, source_target_pairs={{0,8},{8,0},{16,24},{24,16},{1,9},{9,1},{17,25},{25,17},{2,10},{10... | collective-permute-start | bytes 172040 | tf_op jit(solution)/shard_map/ppermute | solution.py:296
  35.4 0.0 collective-permute-done.7.refs_2_
  35.4 0.9 %collective-permute-done.8.refs_3_ = f32[1,112,128]{2,1,0:T(8,128)S(1)} collective-permute-done((f32[1,112,128]{2,1,0:T(8,128)S(1)}, f32[1,112,128]{2,1,0:T(8,128)S(1)}, u32[]{:S(2)}, u32[]{:S(2)}) %collective-permute-start.8) | collective-permute-done | bytes 57376 | tf_op jit(solution)/shard_map/ppermute | solution.py:296
  36.3 1.5 %smooth_and_mix.1 = f32[4,1,32,128]{3,2,1,0:T(8,128)} custom-call(f32[1,112,128]{2,1,0:T(8,128)S(1)} %get-tuple-element.10.refs_0_, f32[1,112,128]{2,1,0:T(8,128)S(1)} %collective-permute-done.6.refs_1_, f32[1,112,128]{2,1,0:T(8,128)S(1)} %collective-permute-done.7.refs_2_, f32[1,112,128]{2,1,0:T(8,128)S(1)} %collective-permute-done.8.refs_3_), custom_call_target="tpu_custom_call" | custom-call | tf_op jit(solution)/shard_map/smooth_and_mix/pallas_call | solution.py:362
  (1 shorter events, 0.0 us)
Async XLA Ops:
  0.7 0.7 %copy-start.2 = (f32[1,64]{1,0:T(1,128)S(1)}, f32[1,64]{1,0:T(1,128)}, u32[]{:S(2)}) copy-start(f32[1,64]{1,0:T(1,128)} %weights_in.1) | copy-start | bytes 772
  0.7 0.7 %copy-start.3 = (s32[1,64,1]{1,2,0:T(1,128)S(1)}, s32[1,64,1]{1,2,0:T(1,128)}, u32[]{:S(2)}) copy-start(s32[1,64,1]{1,2,0:T(1,128)} %param.12) | copy-start | bytes 772
  0.7 0.7 %copy-start.4 = (s32[1,64]{1,0:T(1,128)S(1)}, s32[1,64]{1,0:T(1,128)}, u32[]{:S(2)}) copy-start(s32[1,64]{1,0:T(1,128)} %row_in.1) | copy-start | bytes 772
  8.2 11.9 %collective-permute-start = (f32[88,128]{1,0:T(8,128)S(1)}, f32[88,128]{1,0:T(8,128)S(1)}, u32[]{:S(2)}, u32[]{:S(2)}) collective-permute-start(f32[88,128]{1,0:T(8,128)S(1)} %filter_blocks.1.refs_0_), channel_id=1, source_target_pairs={{0,2},{1,3},{2,4},{3,5},{4,0},{5,1},{8,10},{9,11},{10,12},{11,13},... | collective-permute-start | bytes 135176 | tf_op jit(solution)/shard_map/ppermute | solution.py:333
  8.9 11.3 %collective-permute-start.1 = (f32[88,128]{1,0:T(8,128)S(1)}, f32[88,128]{1,0:T(8,128)S(1)}, u32[]{:S(2)}, u32[]{:S(2)}) collective-permute-start(f32[88,128]{1,0:T(8,128)S(1)} %filter_blocks.1.refs_0_), channel_id=1, source_target_pairs={{0,4},{1,5},{2,0},{3,1},{4,2},{5,3},{8,12},{9,13},{10,8},{11,9},{1... | collective-permute-start | bytes 135176 | tf_op jit(solution)/shard_map/ppermute | solution.py:333
  9.5 10.6 %collective-permute-start.2 = (f32[88,128]{1,0:T(8,128)S(1)}, f32[88,128]{1,0:T(8,128)S(1)}, u32[]{:S(2)}, u32[]{:S(2)}) collective-permute-start(f32[88,128]{1,0:T(8,128)S(1)} %filter_blocks.1.refs_0_), channel_id=1, source_target_pairs={{0,6},{1,7},{6,0},{7,1},{8,14},{9,15},{14,8},{15,9},{16,22},{17,23... | collective-permute-start | bytes 135176 | tf_op jit(solution)/shard_map/ppermute | solution.py:333
  16.3 5.7 %collective-permute-start.3 = (f32[88,128]{1,0:T(8,128)S(1)}, f32[88,128]{1,0:T(8,128)S(1)}, u32[]{:S(2)}, u32[]{:S(2)}) collective-permute-start(f32[88,128]{1,0:T(8,128)S(1)} %filter_blocks.1.refs_0_), channel_id=1, source_target_pairs={{2,6},{3,7},{6,2},{7,3},{10,14},{11,15},{14,10},{15,11},{18,22},{1... | collective-permute-start | bytes 135176 | tf_op jit(solution)/shard_map/ppermute | solution.py:333
  18.2 4.8 %collective-permute-start.4 = (f32[88,128]{1,0:T(8,128)S(1)}, f32[88,128]{1,0:T(8,128)S(1)}, u32[]{:S(2)}, u32[]{:S(2)}) collective-permute-start(f32[88,128]{1,0:T(8,128)S(1)} %filter_blocks.1.refs_0_), channel_id=1, source_target_pairs={{4,6},{5,7},{6,4},{7,5},{12,14},{13,15},{14,12},{15,13},{20,22},{2... | collective-permute-start | bytes 135176 | tf_op jit(solution)/shard_map/ppermute | solution.py:333
  23.2 1.3 %copy-start.5 = (f32[4,1,2]{0,2,1:T(2,128)S(1)}, f32[4,1,2]{0,2,1:T(2,128)}, u32[]{:S(2)}) copy-start(f32[4,1,2]{0,2,1:T(2,128)} %param.17) | copy-start | bytes 100
  23.3 3.8 %collective-permute-start.5 = (f32[232,128]{1,0:T(8,128)S(1)}, f32[232,128]{1,0:T(8,128)S(1)}, u32[]{:S(2)}, u32[]{:S(2)}) collective-permute-start(f32[232,128]{1,0:T(8,128)S(1)} %get-tuple-element.8.refs_1_), channel_id=1, source_target_pairs={{0,1},{1,0},{2,3},{3,2},{4,5},{5,4},{6,7},{7,6},{8,9},{9,8},{10,11... | collective-permute-start | bytes 356360 | tf_op jit(solution)/shard_map/ppermute | solution.py:296
  24.5 2.5 %copy-start.1 = (f32[1,2,33]{2,1,0:T(2,128)S(1)}, f32[1,2,33]{2,1,0:T(2,128)}, u32[]{:S(2)}) copy-start(f32[1,2,33]{2,1,0:T(2,128)} %refs_4_.1) | copy-start | bytes 796
  24.6 2.4 %copy-start = (f32[1,2,33]{2,1,0:T(2,128)S(1)}, f32[1,2,33]{2,1,0:T(2,128)}, u32[]{:S(2)}) copy-start(f32[1,2,33]{2,1,0:T(2,128)} %refs_3_.1) | copy-start | bytes 796
  27.3 4.1 %collective-permute-start.6 = (f32[1,112,128]{2,1,0:T(8,128)S(1)}, f32[1,112,128]{2,1,0:T(8,128)S(1)}, u32[]{:S(2)}, u32[]{:S(2)}) collective-permute-start(f32[1,112,128]{2,1,0:T(8,128)S(1)} %get-tuple-element.9), channel_id=1, source_target_pairs={{0,16},{8,24},{16,0},{24,8},{1,17},{9,25},{17,1},{25,9},{2,18},{10... | collective-permute-start | bytes 172040 | tf_op jit(solution)/shard_map/ppermute | solution.py:296
  27.6 7.8 %collective-permute-start.7 = (f32[1,112,128]{2,1,0:T(8,128)S(1)}, f32[1,112,128]{2,1,0:T(8,128)S(1)}, u32[]{:S(2)}, u32[]{:S(2)}) collective-permute-start(f32[1,112,128]{2,1,0:T(8,128)S(1)} %get-tuple-element.10.refs_0_), channel_id=1, source_target_pairs={{0,8},{8,0},{16,24},{24,16},{1,9},{9,1},{17,25},{25,17},{2,10},{10... | collective-permute-start | bytes 172040 | tf_op jit(solution)/shard_map/ppermute | solution.py:296
  31.4 4.9 %collective-permute-start.8 = (f32[1,112,128]{2,1,0:T(8,128)S(1)}, f32[1,112,128]{2,1,0:T(8,128)S(1)}, u32[]{:S(2)}, u32[]{:S(2)}) collective-permute-start(f32[1,112,128]{2,1,0:T(8,128)S(1)} %collective-permute-done.6.refs_1_), channel_id=1, source_target_pairs={{0,8},{8,0},{16,24},{24,16},{1,9},{9,1},{17,25},{25,17},{2,10},{10... | collective-permute-start | bytes 172040 | tf_op jit(solution)/shard_map/ppermute | solution.py:296

commit v6 on v4

--- a/solution.py
+++ b/solution.py
@@ -13,7 +13,7 @@
 VMEM = pl.BlockSpec(memory_space=pltpu.VMEM)
 ANY = pl.BlockSpec(memory_space=pl.ANY)
 SMALL = pltpu.CompilerParams(vmem_limit_bytes=32 * 2**20)
-WHOLE = pltpu.CompilerParams(vmem_limit_bytes=215 * 2**18)
+WHOLE = pltpu.CompilerParams(vmem_limit_bytes=48 * 2**20)
 F32, BF16 = jnp.float32, jnp.bfloat16
 
 
@@ -220,15 +220,15 @@
     return lax.dot_general(left, right, (((ka,), (kb,)), ((), ())), preferred_element_type=F32)
 
 
-def beam_kernel(*refs, share, reach, terms, comps, taps):
-    ins, out = refs[:-1], refs[-1]
+def beam_kernel(*refs, windows, share, reach, terms, comps):
+    ins, sofar, out = refs[:windows], refs[windows:-1], refs[-1]
     core = lax.rem(lax.axis_index("band"), 2)
     wide = 2 * share + 2 * reach
     need = share + 2 * reach
     x = lax.broadcasted_iota(jnp.int32, (L, L), 0)
     c_in = lax.broadcasted_iota(jnp.int32, (L, L), 1)
     near = jnp.abs(c_in - x) <= reach
-    totals = [None] * comps
+    totals = [sofar[0][c, 0] if sofar else None for c in range(comps)]
     for ref in ins:
         for h in range(ref.shape[0]):
             rows = ref[h, pl.ds(pl.multiple_of(core * share, 8), need), :]
@@ -268,6 +268,7 @@
     terms, beam = beam_rows.shape[1:]
     reach = (beam - 1) // 2
     comps = mixing.shape[0]
+    inputs = (det_weights, tod, filter_taps, owner[:, :, 0], tile_row)
     values = pl.pallas_call(
         functools.partial(filter_kernel, plan=plan),
         out_shape=jax.ShapeDtypeStruct((plan.out + 8, L), F32),
@@ -287,7 +288,7 @@
         ],
         compiler_params=WHOLE,
         name="filter_blocks",
-    )(det_weights, tod, filter_taps, owner[:, :, 0], tile_row, block_counts)
+    )(*[pltpu.with_memory_space_constraint(v, pltpu.HBM) for v in inputs], block_counts)
     order = list(range(outer))
     parts = [flip(values, "tm", k * inner) if k else values for k in order]
     ext = TROWS + 2 * reach
@@ -316,16 +317,22 @@
     )(home, away, other, beam_rows, beam_cols, mixing)
     own = windows[0:1]
     across = [flip(windows[h : h + 1], "band", 2 * h) for h in range(1, bands // 2)]
-    mine = [own] + across
-    other = [flip(m, "band", 1) for m in mine]
-    return pl.pallas_call(
-        functools.partial(beam_kernel, share=share, reach=reach, terms=terms, comps=comps, taps=beam),
-        out_shape=jax.ShapeDtypeStruct((comps, 1, share, L), F32),
-        in_specs=[VMEM] * (2 * len(mine)),
-        out_specs=VMEM,
-        compiler_params=SMALL,
-        name="smooth_and_mix",
-    )(*mine, *other)
+    smooth = functools.partial(beam_kernel, share=share, reach=reach, terms=terms, comps=comps)
+
+    def add_beams(windows, *sofar):
+        return pl.pallas_call(
+            functools.partial(smooth, windows=len(windows)),
+            out_shape=jax.ShapeDtypeStruct((comps, 1, share, L), F32),
+            in_specs=[VMEM] * (len(windows) + len(sofar)),
+            out_specs=VMEM,
+            compiler_params=SMALL,
+            cost_estimate=pl.CostEstimate(flops=10**9, bytes_accessed=10**6, transcendentals=0),
+            name="smooth_and_mix",
+        )(*windows, *sofar)
+
+    result = add_beams([own])
+    result = add_beams([flip(own, "band", 1)] + across, result)
+    return add_beams([flip(window, "band", 1) for window in across], result)
 
 
 def solution(mesh):

time: 31.1 us -> 29.9 us (0.961)
  waiting for transfers between devices: 11.4 us -> 10.5 us
  local copies, waits for them, and re-layouts: 0.78 us -> 0.12 us
  Pallas kernels: 9.08 us -> 9.59 us
    ppermute x7, waiting for transfers between devices: 11.4 us -> 10.5 us  [flip(): return lax.ppermute(x, axis, [(i, i ^ bits) for i in range(count)])]
    unnamed x13 -> x7, local copies, waits for them, and re-layouts: 0.77 us -> 0.11 us
    pallas_call x1 -> x3, Pallas kernels: 1.51 us -> 2.01 us  [add_beams(): pl.pallas_call(functools.partial(smooth, windows=len(windows)), out_shape...]
  transfers between devices with their start and end apart: 7 -> 7, of which waited for: 5 -> 5; matrix products, arithmetic and copies ran while one was open for 0% -> 0% of each run, Pallas kernels for 0% -> 3%
where the time goes in v6:
time: 29.9 us; the launch traced here: 29.8 us
  waiting for transfers between devices  10.5 us (35%)
  Pallas kernels  9.59 us (32%)
  starting transfers between devices  8.89 us (30%)
  between operations  0.71 us (2%)
    ppermute x7, waiting for transfers between devices, flip(): return lax.ppermute(x, axis, [(i, i ^ bits) for i in range(count)])  10.5 us
    ppermute x7, starting transfers between devices, flip(): return lax.ppermute(x, axis, [(i, i ^ bits) for i in range(count)])  8.89 us
    pallas_call x1, Pallas kernels, on_device(): pl.pallas_call(functools.partial(filter_kernel, plan=plan), out_shape=jax...  6.85 us
    pallas_call x3, Pallas kernels, add_beams(): pl.pallas_call(functools.partial(smooth, windows=len(windows)), out_shape...  2.01 us
  transfers between devices with their start and end apart: 7, of which 5 were waited for; matrix products, arithmetic and copies ran while one was open for 0% of the time, Pallas kernels for 3%

profile of v6, /device:TPU:0, one launch (start us, length us, event | category | flops | bytes accessed | tf_op | source)
XLA Modules:
  0.0 29.8 jit_solution(7697809176684003599)
XLA Ops:
  0.7 6.9 %filter_blocks.1.refs_0_ = f32[88,128]{1,0:T(8,128)S(1)} custom-call(f32[1,64]{1,0:T(1,128)} %weights_in.1, bf16[1,64,8192]{2,1,0:T(8,128)(2,1)} %tod.1, bf16[1,64,2049]{2,1,0:T(8,128)(2,1)} %taps_in.1, s32[1,64]{1,0:T(1,128)} %bitcast.1, s32[1,64]{1,0:T(1,128)} %row_in.1, s32[1,1]{1,0:T(1,128)S(6)} %copy.11.counts_in), custom_call_target="tpu_custom_call" | custom-call | tf_op jit(solution)/shard_map/filter_blocks/pallas_call | solution.py:272
  7.5 5.1 %collective-permute-start.2 = (f32[88,128]{1,0:T(8,128)S(1)}, f32[88,128]{1,0:T(8,128)S(1)}, u32[]{:S(2)}, u32[]{:S(2)}) collective-permute-start(f32[88,128]{1,0:T(8,128)S(1)} %filter_blocks.1.refs_0_), channel_id=1, source_target_pairs={{0,6},{1,7},{2,4},{3,5},{4,2},{5,3},{6,0},{7,1},{8,14},{9,15},{10,... | collective-permute-start | bytes 135176 | tf_op jit(solution)/shard_map/ppermute | solution.py:256
  12.6 0.0 collective-permute-start.1
  12.6 0.6 %collective-permute-start = (f32[88,128]{1,0:T(8,128)S(1)}, f32[88,128]{1,0:T(8,128)S(1)}, u32[]{:S(2)}, u32[]{:S(2)}) collective-permute-start(f32[88,128]{1,0:T(8,128)S(1)} %filter_blocks.1.refs_0_), channel_id=1, source_target_pairs={{0,2},{1,3},{2,0},{3,1},{4,6},{5,7},{6,4},{7,5},{8,10},{9,11},{10,... | collective-permute-start | bytes 135176 | tf_op jit(solution)/shard_map/ppermute | solution.py:256
  13.3 1.4 %collective-permute-done.2.refs_3_ = f32[88,128]{1,0:T(8,128)S(1)} collective-permute-done((f32[88,128]{1,0:T(8,128)S(1)}, f32[88,128]{1,0:T(8,128)S(1)}, u32[]{:S(2)}, u32[]{:S(2)}) %collective-permute-start.2) | collective-permute-done | bytes 45088 | tf_op jit(solution)/shard_map/ppermute | solution.py:256
  14.7 2.9 %collective-permute-done.1.refs_2_ = f32[88,128]{1,0:T(8,128)S(1)} collective-permute-done((f32[88,128]{1,0:T(8,128)S(1)}, f32[88,128]{1,0:T(8,128)S(1)}, u32[]{:S(2)}, u32[]{:S(2)}) %collective-permute-start.1) | collective-permute-done | bytes 45088 | tf_op jit(solution)/shard_map/ppermute | solution.py:256
  17.6 0.0 collective-permute-done.refs_1_
  17.6 0.5 %tile_rows.1 = (f32[160,128]{1,0:T(8,128)S(1)}, f32[232,128]{1,0:T(8,128)S(1)}) custom-call(f32[88,128]{1,0:T(8,128)S(1)} %filter_blocks.1.refs_0_, f32[88,128]{1,0:T(8,128)S(1)} %collective-permute-done.refs_1_, f32[88,128]{1,0:T(8,128)S(1)} %collective-permute-done.1.refs_2_, f32[88,128]{1,0:T(8,128)S(1)} %collective-permute-done.2.refs_3_), custom_call_target="tpu_custom_call" | custom-call | tf_op jit(solution)/shard_map/tile_rows/pallas_call | solution.py:296
  18.1 0.0 copy-start.2
  18.1 1.5 %collective-permute-start.3 = (f32[232,128]{1,0:T(8,128)S(1)}, f32[232,128]{1,0:T(8,128)S(1)}, u32[]{:S(2)}, u32[]{:S(2)}) collective-permute-start(f32[232,128]{1,0:T(8,128)S(1)} %get-tuple-element.8.refs_1_), channel_id=1, source_target_pairs={{0,1},{1,0},{2,3},{3,2},{4,5},{5,4},{6,7},{7,6},{8,9},{9,8},{10,11... | collective-permute-start | bytes 356360 | tf_op jit(solution)/shard_map/ppermute | solution.py:256
  19.6 0.0 copy-done.2
  19.6 0.0 copy-start.1
  19.6 0.1 copy.10.refs_5_
  19.7 0.0 copy-start
  19.7 3.3 %collective-permute-done.3.refs_2_ = f32[232,128]{1,0:T(8,128)S(1)} collective-permute-done((f32[232,128]{1,0:T(8,128)S(1)}, f32[232,128]{1,0:T(8,128)S(1)}, u32[]{:S(2)}, u32[]{:S(2)}) %collective-permute-start.3) | collective-permute-done | bytes 118816 | tf_op jit(solution)/shard_map/ppermute | solution.py:256
  23.0 0.0 copy-done.1
  23.0 0.0 copy-done
  23.0 0.3 band_windows.1
  23.3 1.6 %collective-permute-start.4 = (f32[1,112,128]{2,1,0:T(8,128)S(1)}, f32[1,112,128]{2,1,0:T(8,128)S(1)}, u32[]{:S(2)}, u32[]{:S(2)}) collective-permute-start(f32[1,112,128]{2,1,0:T(8,128)S(1)} %get-tuple-element.10), channel_id=1, source_target_pairs={{0,16},{8,24},{16,0},{24,8},{1,17},{9,25},{17,1},{25,9},{2,18},{10... | collective-permute-start | bytes 172040 | tf_op jit(solution)/shard_map/ppermute | solution.py:256
  24.8 0.0 collective-permute-start.6
  24.8 0.4 %smooth_and_mix.3.refs_2_ = f32[4,1,32,128]{3,2,1,0:T(8,128)S(1)} custom-call(f32[1,112,128]{2,1,0:T(8,128)S(1)} %get-tuple-element.9.refs_0_), custom_call_target="tpu_custom_call" | custom-call | flops 1000000000 | bytes 1000000 | tf_op jit(solution)/shard_map/smooth_and_mix/pallas_call | solution.py:323
  25.2 2.2 %collective-permute-done.4.refs_1_ = f32[1,112,128]{2,1,0:T(8,128)S(1)} collective-permute-done((f32[1,112,128]{2,1,0:T(8,128)S(1)}, f32[1,112,128]{2,1,0:T(8,128)S(1)}, u32[]{:S(2)}, u32[]{:S(2)}) %collective-permute-start.4) | collective-permute-done | bytes 57376 | tf_op jit(solution)/shard_map/ppermute | solution.py:256
  27.5 0.0 collective-permute-start.5
  27.5 0.0 collective-permute-done.6.refs_0_
  27.5 0.6 %smooth_and_mix.4.refs_1_ = f32[4,1,32,128]{3,2,1,0:T(8,128)S(1)} custom-call(f32[1,112,128]{2,1,0:T(8,128)S(1)} %collective-permute-done.6.refs_0_, f32[1,112,128]{2,1,0:T(8,128)S(1)} %collective-permute-done.4.refs_1_, f32[4,1,32,128]{3,2,1,0:T(8,128)S(1)} %smooth_and_mix.3.refs_2_), custom_call_target="tpu_custom_call" | custom-call | flops 1000000000 | bytes 1000000 | tf_op jit(solution)/shard_map/smooth_and_mix/pallas_call | solution.py:323
  28.1 0.7 %collective-permute-done.5.refs_0_ = f32[1,112,128]{2,1,0:T(8,128)S(1)} collective-permute-done((f32[1,112,128]{2,1,0:T(8,128)S(1)}, f32[1,112,128]{2,1,0:T(8,128)S(1)}, u32[]{:S(2)}, u32[]{:S(2)}) %collective-permute-start.5) | collective-permute-done | bytes 57376 | tf_op jit(solution)/shard_map/ppermute | solution.py:256
  28.7 1.0 %smooth_and_mix.5 = f32[4,1,32,128]{3,2,1,0:T(8,128)} custom-call(f32[1,112,128]{2,1,0:T(8,128)S(1)} %collective-permute-done.5.refs_0_, f32[4,1,32,128]{3,2,1,0:T(8,128)S(1)} %smooth_and_mix.4.refs_1_), custom_call_target="tpu_custom_call" | custom-call | flops 1000000000 | bytes 1000000 | tf_op jit(solution)/shard_map/smooth_and_mix/pallas_call | solution.py:323
  (1 shorter events, 0.0 us)
Async XLA Ops:
  7.5 7.2 %collective-permute-start.2 = (f32[88,128]{1,0:T(8,128)S(1)}, f32[88,128]{1,0:T(8,128)S(1)}, u32[]{:S(2)}, u32[]{:S(2)}) collective-permute-start(f32[88,128]{1,0:T(8,128)S(1)} %filter_blocks.1.refs_0_), channel_id=1, source_target_pairs={{0,6},{1,7},{2,4},{3,5},{4,2},{5,3},{6,0},{7,1},{8,14},{9,15},{10,... | collective-permute-start | bytes 135176 | tf_op jit(solution)/shard_map/ppermute | solution.py:256
  12.6 4.9 %collective-permute-start.1 = (f32[88,128]{1,0:T(8,128)S(1)}, f32[88,128]{1,0:T(8,128)S(1)}, u32[]{:S(2)}, u32[]{:S(2)}) collective-permute-start(f32[88,128]{1,0:T(8,128)S(1)} %filter_blocks.1.refs_0_), channel_id=1, source_target_pairs={{0,4},{1,5},{2,6},{3,7},{4,0},{5,1},{6,2},{7,3},{8,12},{9,13},{10,... | collective-permute-start | bytes 135176 | tf_op jit(solution)/shard_map/ppermute | solution.py:256
  12.6 4.9 %collective-permute-start = (f32[88,128]{1,0:T(8,128)S(1)}, f32[88,128]{1,0:T(8,128)S(1)}, u32[]{:S(2)}, u32[]{:S(2)}) collective-permute-start(f32[88,128]{1,0:T(8,128)S(1)} %filter_blocks.1.refs_0_), channel_id=1, source_target_pairs={{0,2},{1,3},{2,0},{3,1},{4,6},{5,7},{6,4},{7,5},{8,10},{9,11},{10,... | collective-permute-start | bytes 135176 | tf_op jit(solution)/shard_map/ppermute | solution.py:256
  18.1 1.6 %copy-start.2 = (f32[4,1,2]{0,2,1:T(2,128)S(1)}, f32[4,1,2]{0,2,1:T(2,128)}, u32[]{:S(2)}) copy-start(f32[4,1,2]{0,2,1:T(2,128)} %param.17) | copy-start | bytes 100
  18.1 4.9 %collective-permute-start.3 = (f32[232,128]{1,0:T(8,128)S(1)}, f32[232,128]{1,0:T(8,128)S(1)}, u32[]{:S(2)}, u32[]{:S(2)}) collective-permute-start(f32[232,128]{1,0:T(8,128)S(1)} %get-tuple-element.8.refs_1_), channel_id=1, source_target_pairs={{0,1},{1,0},{2,3},{3,2},{4,5},{5,4},{6,7},{7,6},{8,9},{9,8},{10,11... | collective-permute-start | bytes 356360 | tf_op jit(solution)/shard_map/ppermute | solution.py:256
  19.6 3.4 %copy-start.1 = (f32[1,2,33]{2,1,0:T(2,128)S(1)}, f32[1,2,33]{2,1,0:T(2,128)}, u32[]{:S(2)}) copy-start(f32[1,2,33]{2,1,0:T(2,128)} %refs_4_.1) | copy-start | bytes 796
  19.7 3.3 %copy-start = (f32[1,2,33]{2,1,0:T(2,128)S(1)}, f32[1,2,33]{2,1,0:T(2,128)}, u32[]{:S(2)}) copy-start(f32[1,2,33]{2,1,0:T(2,128)} %refs_3_.1) | copy-start | bytes 796
  23.3 4.2 %collective-permute-start.4 = (f32[1,112,128]{2,1,0:T(8,128)S(1)}, f32[1,112,128]{2,1,0:T(8,128)S(1)}, u32[]{:S(2)}, u32[]{:S(2)}) collective-permute-start(f32[1,112,128]{2,1,0:T(8,128)S(1)} %get-tuple-element.10), channel_id=1, source_target_pairs={{0,16},{8,24},{16,0},{24,8},{1,17},{9,25},{17,1},{25,9},{2,18},{10... | collective-permute-start | bytes 172040 | tf_op jit(solution)/shard_map/ppermute | solution.py:256
  24.8 2.7 %collective-permute-start.6 = (f32[1,112,128]{2,1,0:T(8,128)S(1)}, f32[1,112,128]{2,1,0:T(8,128)S(1)}, u32[]{:S(2)}, u32[]{:S(2)}) collective-permute-start(f32[1,112,128]{2,1,0:T(8,128)S(1)} %get-tuple-element.9.refs_0_), channel_id=1, source_target_pairs={{0,8},{8,0},{16,24},{24,16},{1,9},{9,1},{17,25},{25,17},{2,10},{10... | collective-permute-start | bytes 172040 | tf_op jit(solution)/shard_map/ppermute | solution.py:256
  27.5 1.2 %collective-permute-start.5 = (f32[1,112,128]{2,1,0:T(8,128)S(1)}, f32[1,112,128]{2,1,0:T(8,128)S(1)}, u32[]{:S(2)}, u32[]{:S(2)}) collective-permute-start(f32[1,112,128]{2,1,0:T(8,128)S(1)} %collective-permute-done.4.refs_1_), channel_id=1, source_target_pairs={{0,8},{8,0},{16,24},{24,16},{1,9},{9,1},{17,25},{25,17},{2,10},{10... | collective-permute-start | bytes 172040 | tf_op jit(solution)/shard_map/ppermute | solution.py:256

commit v7 on v6

--- a/solution.py
+++ b/solution.py
@@ -14,7 +14,9 @@
 ANY = pl.BlockSpec(memory_space=pl.ANY)
 SMALL = pltpu.CompilerParams(vmem_limit_bytes=32 * 2**20)
 WHOLE = pltpu.CompilerParams(vmem_limit_bytes=48 * 2**20)
-F32, BF16 = jnp.float32, jnp.bfloat16
+F32, BF16, FP8 = jnp.float32, jnp.bfloat16, jnp.float8_e4m3fn
+TOP = 256.0
+TINY = 1e-30
 
 
 class Plan:
@@ -30,7 +32,7 @@
 
 def filter_kernel(
     weights_in, tod, taps_in, owner_in, row_in, counts_in,
-    out, weights, taps, owner, tile_row, counts, held, table, line, diagonal, sems, *, plan
+    out, weights, taps, owner, tile_row, counts, held, held8, table, rest, table8, line, diagonal, sems, *, plan
 ):
     nd, steps, lead, groups = plan.detectors, plan.steps, plan.lead, plan.groups
     small = [
@@ -49,6 +51,8 @@
         copy.start()
     held[0 : lead * nd, :] = jnp.zeros((lead * nd, BLOCK), BF16)
     held[(lead + steps) * nd :, :] = jnp.zeros((lead * nd, BLOCK), BF16)
+    held8[0 : lead * nd, :] = jnp.zeros((lead * nd, BLOCK), FP8)
+    held8[(lead + steps) * nd :, :] = jnp.zeros((lead * nd, BLOCK), FP8)
     line[...] = jnp.zeros_like(line)
     row = lax.broadcasted_iota(jnp.int32, (nd, L), 0)
     lane = lax.broadcasted_iota(jnp.int32, (nd, L), 1)
@@ -64,16 +68,34 @@
                 part = taps[:, start : start + L].astype(F32) * column
                 parts.append(jnp.take_along_axis(part, L - 1 - lane, axis=1))
             turned = jnp.concatenate(parts, axis=0).T
-            high, low = two_terms(turned)
+            high = turned.astype(BF16)
             at = (1 - half) * L
             table[at : at + L, pair * L : (pair + 1) * L] = high
-            table[BLOCK + at : BLOCK + at + L, pair * L : (pair + 1) * L] = low
+            rest[at : at + L, pair * L : (pair + 1) * L] = turned - high.astype(F32)
     last = jnp.broadcast_to(taps[:, groups * BLOCK : groups * BLOCK + 1].astype(F32) * column, (nd, L))
     row8 = lax.broadcasted_iota(jnp.int32, (8, L), 0)
     lane8 = lax.broadcasted_iota(jnp.int32, (8, L), 1)
     for copy in big:
         copy.wait()
 
+    loud = jnp.zeros((nd, BLOCK), BF16)
+    for b in range(steps):
+        loud = jnp.maximum(loud, jnp.abs(held[(lead + b) * nd : (lead + b + 1) * nd, :]))
+    loud = jnp.maximum(jnp.max(loud.astype(F32), axis=1, keepdims=True), TINY)
+    quiet = jnp.broadcast_to(TOP / loud, (nd, BLOCK))
+    across = jnp.sum(jnp.where(row == lane, jnp.broadcast_to(loud, (nd, L)), 0.0), axis=0, keepdims=True)
+    across = jnp.concatenate([across[:, :nd]] * groups, axis=1)
+    scaled = rest[...] * across
+    largest = jnp.max(jnp.max(jnp.abs(scaled), axis=0, keepdims=True), axis=1, keepdims=True)
+    largest = jnp.maximum(largest, TINY)
+    table8[...] = (scaled * (TOP / largest)).astype(FP8)
+    back = largest * (1.0 / (TOP * TOP))
+
+    def shrink(b):
+        if b < steps:
+            at = (lead + b) * nd
+            held8[at : at + nd, :] = (held[at : at + nd, :].astype(F32) * quiet).astype(FP8)
+
     slots = diagonal.shape[0]
     count = steps + lead
 
@@ -81,9 +103,10 @@
         half = groups // 2
         low = half if v + half <= lead else 0
         high = half if v + half >= lead + steps else groups
-        x = held[(v + low) * nd : (v + high) * nd, :]
-        both = jnp.dot(table[:, low * nd : high * nd], x, preferred_element_type=F32)
-        diagonal[v % slots] = both[:BLOCK] + both[BLOCK:]
+        rows, cols = slice((v + low) * nd, (v + high) * nd), slice(low * nd, high * nd)
+        main = jnp.dot(table[:, cols], held[rows, :], preferred_element_type=F32)
+        small = jnp.dot(table8[:, cols], held8[rows, :], preferred_element_type=F32)
+        diagonal[v % slots] = main + small * back
 
     def add_diagonals(tiles, at):
         total = direct = None
@@ -101,8 +124,11 @@
     def corner(v, down, across):
         return diagonal[v % slots, down * L : (down + 1) * L, across * L : (across + 1) * L]
 
+    shrink(0)
+    shrink(1)
     product(0)
     for v in range(count):
+        shrink(v + 2)
         if v + 1 < count:
             product(v + 1)
         first = [corner(v, 0, 0)] + ([corner(v - 1, 1, 1)] if v else [])
@@ -141,31 +167,22 @@
 
 
 def tile_rows_kernel(*refs, plan, reach):
-    parts, (home, away, own, sem) = list(refs[:-4]), refs[-4:]
-    copy = pltpu.make_async_copy(parts[0], own, sem)
-    copy.start()
+    parts, (home, away) = refs[:-2], refs[-2:]
     nb, halo = plan.blocks, plan.reach
     me = lax.axis_index("tm")
     ext = TROWS + 2 * reach
     marks_at = ext + 2 * halo * len(parts)
     away[marks_at:, :] = jnp.full((away.shape[0] - marks_at, L), -1.0, F32)
 
-    def add(some, first):
-        for k, ref in some:
-            at = ext + 2 * halo * k
-            away[at : at + halo, :] = ref[0:halo, :]
-            away[at + halo : at + 2 * halo, :] = ref[halo + nb : plan.out, :]
-            away[marks_at + k : marks_at + k + 1, :] = ref[plan.out : plan.out + 1, :]
-        target = jnp.concatenate([ref[plan.out : plan.out + 1, 0:nb] for _, ref in some], axis=1)
-        blocks = jnp.concatenate([ref[halo : halo + nb, :] for _, ref in some], axis=0)
-        for out, tile in ((home, me), (away, jnp.bitwise_xor(me, 1))):
-            rows = add_rows(rows_of(target, (tile * TROWS - reach).astype(F32), ext), blocks)
-            out[0:ext, :] = rows if first else out[0:ext, :] + rows
-
-    if len(parts) > 1:
-        add(list(enumerate(parts))[1:], True)
-    copy.wait()
-    add([(0, own)], len(parts) == 1)
+    for k, ref in enumerate(parts):
+        at = ext + 2 * halo * k
+        away[at : at + halo, :] = ref[0:halo, :]
+        away[at + halo : at + 2 * halo, :] = ref[halo + nb : plan.out, :]
+        away[marks_at + k : marks_at + k + 1, :] = ref[plan.out : plan.out + 1, :]
+    target = jnp.concatenate([ref[plan.out : plan.out + 1, 0:nb] for ref in parts], axis=1)
+    blocks = jnp.concatenate([ref[halo : halo + nb, :] for ref in parts], axis=0)
+    for out, tile in ((home, me), (away, jnp.bitwise_xor(me, 1))):
+        out[0:ext, :] = add_rows(rows_of(target, (tile * TROWS - reach).astype(F32), ext), blocks)
 
 
 def windows_kernel(*refs, plan, order, bands, reach):
@@ -281,7 +298,10 @@
             pltpu.VMEM((1, plan.blocks), jnp.int32),
             pltpu.SMEM((1, 1), jnp.int32),
             pltpu.VMEM(((plan.steps + 2 * plan.lead) * detectors, BLOCK), BF16),
-            pltpu.VMEM((2 * BLOCK, plan.groups * detectors), BF16),
+            pltpu.VMEM(((plan.steps + 2 * plan.lead) * detectors, BLOCK), FP8),
+            pltpu.VMEM((BLOCK, plan.groups * detectors), BF16),
+            pltpu.VMEM((BLOCK, plan.groups * detectors), F32),
+            pltpu.VMEM((BLOCK, plan.groups * detectors), FP8),
             pltpu.VMEM((plan.out + 8, 8, L), F32),
             pltpu.VMEM((3, BLOCK, BLOCK), F32),
             pltpu.SemaphoreType.DMA((plan.steps + 5,)),
@@ -296,8 +316,7 @@
     home, away = pl.pallas_call(
         functools.partial(tile_rows_kernel, plan=plan, reach=reach),
         out_shape=(jax.ShapeDtypeStruct((ext, L), F32), jax.ShapeDtypeStruct((sent, L), F32)),
-        in_specs=[ANY] + [VMEM] * (outer - 1),
-        scratch_shapes=[pltpu.VMEM((plan.out + 8, L), F32), pltpu.SemaphoreType.DMA],
+        in_specs=[VMEM] * outer,
         out_specs=(VMEM, VMEM),
         compiler_params=SMALL,
         name="tile_rows",

time: 29.9 us -> 29.2 us (0.977)
  Pallas kernels: 9.59 us -> 8.86 us
    pallas_call x1, Pallas kernels: 6.85 us -> 6.36 us  [on_device(): pl.pallas_call(functools.partial(filter_kernel, plan=plan), out_shape=jax...]
where the time goes in v7:
time: 29.2 us; the launch traced here: 29.1 us
  waiting for transfers between devices  10.5 us (36%)
  starting transfers between devices  8.9 us (30%)
  Pallas kernels  8.86 us (30%)
  between operations  0.71 us (2%)
    ppermute x7, waiting for transfers between devices, flip(): return lax.ppermute(x, axis, [(i, i ^ bits) for i in range(count)])  10.5 us
    ppermute x7, starting transfers between devices, flip(): return lax.ppermute(x, axis, [(i, i ^ bits) for i in range(count)])  8.9 us
    pallas_call x1, Pallas kernels, on_device(): pl.pallas_call(functools.partial(filter_kernel, plan=plan), out_shape=jax...  6.36 us
    pallas_call x3, Pallas kernels, add_beams(): pl.pallas_call(functools.partial(smooth, windows=len(windows)), out_shape...  2.01 us
  transfers between devices with their start and end apart: 7, of which 5 were waited for; matrix products, arithmetic and copies ran while one was open for 0% of the time, Pallas kernels for 3%

profile of v7, /device:TPU:0, one launch (start us, length us, event | category | flops | bytes accessed | tf_op | source)
XLA Modules:
  0.0 29.1 jit_solution(8240473808350476829)
XLA Ops:
  0.7 6.4 %filter_blocks.1.refs_0_ = f32[88,128]{1,0:T(8,128)S(1)} custom-call(f32[1,64]{1,0:T(1,128)} %weights_in.1, bf16[1,64,8192]{2,1,0:T(8,128)(2,1)} %tod.1, bf16[1,64,2049]{2,1,0:T(8,128)(2,1)} %taps_in.1, s32[1,64]{1,0:T(1,128)} %bitcast.1, s32[1,64]{1,0:T(1,128)} %row_in.1, s32[1,1]{1,0:T(1,128)S(6)} %copy.11.counts_in), custom_call_target="tpu_custom_call" | custom-call | tf_op jit(solution)/shard_map/filter_blocks/pallas_call | solution.py:289
  7.0 5.1 %collective-permute-start.2 = (f32[88,128]{1,0:T(8,128)S(1)}, f32[88,128]{1,0:T(8,128)S(1)}, u32[]{:S(2)}, u32[]{:S(2)}) collective-permute-start(f32[88,128]{1,0:T(8,128)S(1)} %filter_blocks.1.refs_0_), channel_id=1, source_target_pairs={{0,6},{1,7},{2,4},{3,5},{4,2},{5,3},{6,0},{7,1},{8,14},{9,15},{10,... | collective-permute-start | bytes 135176 | tf_op jit(solution)/shard_map/ppermute | solution.py:273
  12.1 0.0 collective-permute-start.1
  12.1 0.6 %collective-permute-start = (f32[88,128]{1,0:T(8,128)S(1)}, f32[88,128]{1,0:T(8,128)S(1)}, u32[]{:S(2)}, u32[]{:S(2)}) collective-permute-start(f32[88,128]{1,0:T(8,128)S(1)} %filter_blocks.1.refs_0_), channel_id=1, source_target_pairs={{0,2},{1,3},{2,0},{3,1},{4,6},{5,7},{6,4},{7,5},{8,10},{9,11},{10,... | collective-permute-start | bytes 135176 | tf_op jit(solution)/shard_map/ppermute | solution.py:273
  12.8 1.4 %collective-permute-done.2.refs_3_ = f32[88,128]{1,0:T(8,128)S(1)} collective-permute-done((f32[88,128]{1,0:T(8,128)S(1)}, f32[88,128]{1,0:T(8,128)S(1)}, u32[]{:S(2)}, u32[]{:S(2)}) %collective-permute-start.2) | collective-permute-done | bytes 45088 | tf_op jit(solution)/shard_map/ppermute | solution.py:273
  14.2 2.9 %collective-permute-done.1.refs_2_ = f32[88,128]{1,0:T(8,128)S(1)} collective-permute-done((f32[88,128]{1,0:T(8,128)S(1)}, f32[88,128]{1,0:T(8,128)S(1)}, u32[]{:S(2)}, u32[]{:S(2)}) %collective-permute-start.1) | collective-permute-done | bytes 45088 | tf_op jit(solution)/shard_map/ppermute | solution.py:273
  17.1 0.0 collective-permute-done.refs_1_
  17.1 0.2 tile_rows.1
  17.3 0.0 copy-start.2
  17.3 1.6 %collective-permute-start.3 = (f32[232,128]{1,0:T(8,128)S(1)}, f32[232,128]{1,0:T(8,128)S(1)}, u32[]{:S(2)}, u32[]{:S(2)}) collective-permute-start(f32[232,128]{1,0:T(8,128)S(1)} %get-tuple-element.8.refs_1_), channel_id=1, source_target_pairs={{0,1},{1,0},{2,3},{3,2},{4,5},{5,4},{6,7},{7,6},{8,9},{9,8},{10,11... | collective-permute-start | bytes 356360 | tf_op jit(solution)/shard_map/ppermute | solution.py:273
  18.9 0.0 copy-done.2
  18.9 0.0 copy-start.1
  18.9 0.1 copy.10.refs_5_
  19.0 0.0 copy-start
  19.0 3.2 %collective-permute-done.3.refs_2_ = f32[232,128]{1,0:T(8,128)S(1)} collective-permute-done((f32[232,128]{1,0:T(8,128)S(1)}, f32[232,128]{1,0:T(8,128)S(1)}, u32[]{:S(2)}, u32[]{:S(2)}) %collective-permute-start.3) | collective-permute-done | bytes 118816 | tf_op jit(solution)/shard_map/ppermute | solution.py:273
  22.2 0.0 copy-done.1
  22.2 0.0 copy-done
  22.2 0.3 band_windows.1
  22.5 1.6 %collective-permute-start.4 = (f32[1,112,128]{2,1,0:T(8,128)S(1)}, f32[1,112,128]{2,1,0:T(8,128)S(1)}, u32[]{:S(2)}, u32[]{:S(2)}) collective-permute-start(f32[1,112,128]{2,1,0:T(8,128)S(1)} %get-tuple-element.10), channel_id=1, source_target_pairs={{0,16},{8,24},{16,0},{24,8},{1,17},{9,25},{17,1},{25,9},{2,18},{10... | collective-permute-start | bytes 172040 | tf_op jit(solution)/shard_map/ppermute | solution.py:273
  24.1 0.0 collective-permute-start.6
  24.1 0.4 %smooth_and_mix.3.refs_2_ = f32[4,1,32,128]{3,2,1,0:T(8,128)S(1)} custom-call(f32[1,112,128]{2,1,0:T(8,128)S(1)} %get-tuple-element.9.refs_0_), custom_call_target="tpu_custom_call" | custom-call | flops 1000000000 | bytes 1000000 | tf_op jit(solution)/shard_map/smooth_and_mix/pallas_call | solution.py:342
  24.5 2.2 %collective-permute-done.4.refs_1_ = f32[1,112,128]{2,1,0:T(8,128)S(1)} collective-permute-done((f32[1,112,128]{2,1,0:T(8,128)S(1)}, f32[1,112,128]{2,1,0:T(8,128)S(1)}, u32[]{:S(2)}, u32[]{:S(2)}) %collective-permute-start.4) | collective-permute-done | bytes 57376 | tf_op jit(solution)/shard_map/ppermute | solution.py:273
  26.8 0.0 collective-permute-start.5
  26.8 0.0 collective-permute-done.6.refs_0_
  26.8 0.6 %smooth_and_mix.4.refs_1_ = f32[4,1,32,128]{3,2,1,0:T(8,128)S(1)} custom-call(f32[1,112,128]{2,1,0:T(8,128)S(1)} %collective-permute-done.6.refs_0_, f32[1,112,128]{2,1,0:T(8,128)S(1)} %collective-permute-done.4.refs_1_, f32[4,1,32,128]{3,2,1,0:T(8,128)S(1)} %smooth_and_mix.3.refs_2_), custom_call_target="tpu_custom_call" | custom-call | flops 1000000000 | bytes 1000000 | tf_op jit(solution)/shard_map/smooth_and_mix/pallas_call | solution.py:342
  27.3 0.7 %collective-permute-done.5.refs_0_ = f32[1,112,128]{2,1,0:T(8,128)S(1)} collective-permute-done((f32[1,112,128]{2,1,0:T(8,128)S(1)}, f32[1,112,128]{2,1,0:T(8,128)S(1)}, u32[]{:S(2)}, u32[]{:S(2)}) %collective-permute-start.5) | collective-permute-done | bytes 57376 | tf_op jit(solution)/shard_map/ppermute | solution.py:273
  28.0 1.0 %smooth_and_mix.5 = f32[4,1,32,128]{3,2,1,0:T(8,128)} custom-call(f32[1,112,128]{2,1,0:T(8,128)S(1)} %collective-permute-done.5.refs_0_, f32[4,1,32,128]{3,2,1,0:T(8,128)S(1)} %smooth_and_mix.4.refs_1_), custom_call_target="tpu_custom_call" | custom-call | flops 1000000000 | bytes 1000000 | tf_op jit(solution)/shard_map/smooth_and_mix/pallas_call | solution.py:342
  (1 shorter events, 0.0 us)
Async XLA Ops:
  7.0 7.2 %collective-permute-start.2 = (f32[88,128]{1,0:T(8,128)S(1)}, f32[88,128]{1,0:T(8,128)S(1)}, u32[]{:S(2)}, u32[]{:S(2)}) collective-permute-start(f32[88,128]{1,0:T(8,128)S(1)} %filter_blocks.1.refs_0_), channel_id=1, source_target_pairs={{0,6},{1,7},{2,4},{3,5},{4,2},{5,3},{6,0},{7,1},{8,14},{9,15},{10,... | collective-permute-start | bytes 135176 | tf_op jit(solution)/shard_map/ppermute | solution.py:273
  12.1 4.9 %collective-permute-start.1 = (f32[88,128]{1,0:T(8,128)S(1)}, f32[88,128]{1,0:T(8,128)S(1)}, u32[]{:S(2)}, u32[]{:S(2)}) collective-permute-start(f32[88,128]{1,0:T(8,128)S(1)} %filter_blocks.1.refs_0_), channel_id=1, source_target_pairs={{0,4},{1,5},{2,6},{3,7},{4,0},{5,1},{6,2},{7,3},{8,12},{9,13},{10,... | collective-permute-start | bytes 135176 | tf_op jit(solution)/shard_map/ppermute | solution.py:273
  12.1 4.9 %collective-permute-start = (f32[88,128]{1,0:T(8,128)S(1)}, f32[88,128]{1,0:T(8,128)S(1)}, u32[]{:S(2)}, u32[]{:S(2)}) collective-permute-start(f32[88,128]{1,0:T(8,128)S(1)} %filter_blocks.1.refs_0_), channel_id=1, source_target_pairs={{0,2},{1,3},{2,0},{3,1},{4,6},{5,7},{6,4},{7,5},{8,10},{9,11},{10,... | collective-permute-start | bytes 135176 | tf_op jit(solution)/shard_map/ppermute | solution.py:273
  17.3 1.6 %copy-start.2 = (f32[4,1,2]{0,2,1:T(2,128)S(1)}, f32[4,1,2]{0,2,1:T(2,128)}, u32[]{:S(2)}) copy-start(f32[4,1,2]{0,2,1:T(2,128)} %param.17) | copy-start | bytes 100
  17.3 4.9 %collective-permute-start.3 = (f32[232,128]{1,0:T(8,128)S(1)}, f32[232,128]{1,0:T(8,128)S(1)}, u32[]{:S(2)}, u32[]{:S(2)}) collective-permute-start(f32[232,128]{1,0:T(8,128)S(1)} %get-tuple-element.8.refs_1_), channel_id=1, source_target_pairs={{0,1},{1,0},{2,3},{3,2},{4,5},{5,4},{6,7},{7,6},{8,9},{9,8},{10,11... | collective-permute-start | bytes 356360 | tf_op jit(solution)/shard_map/ppermute | solution.py:273
  18.9 3.3 %copy-start.1 = (f32[1,2,33]{2,1,0:T(2,128)S(1)}, f32[1,2,33]{2,1,0:T(2,128)}, u32[]{:S(2)}) copy-start(f32[1,2,33]{2,1,0:T(2,128)} %refs_4_.1) | copy-start | bytes 796
  19.0 3.3 %copy-start = (f32[1,2,33]{2,1,0:T(2,128)S(1)}, f32[1,2,33]{2,1,0:T(2,128)}, u32[]{:S(2)}) copy-start(f32[1,2,33]{2,1,0:T(2,128)} %refs_3_.1) | copy-start | bytes 796
  22.5 4.2 %collective-permute-start.4 = (f32[1,112,128]{2,1,0:T(8,128)S(1)}, f32[1,112,128]{2,1,0:T(8,128)S(1)}, u32[]{:S(2)}, u32[]{:S(2)}) collective-permute-start(f32[1,112,128]{2,1,0:T(8,128)S(1)} %get-tuple-element.10), channel_id=1, source_target_pairs={{0,16},{8,24},{16,0},{24,8},{1,17},{9,25},{17,1},{25,9},{2,18},{10... | collective-permute-start | bytes 172040 | tf_op jit(solution)/shard_map/ppermute | solution.py:273
  24.1 2.7 %collective-permute-start.6 = (f32[1,112,128]{2,1,0:T(8,128)S(1)}, f32[1,112,128]{2,1,0:T(8,128)S(1)}, u32[]{:S(2)}, u32[]{:S(2)}) collective-permute-start(f32[1,112,128]{2,1,0:T(8,128)S(1)} %get-tuple-element.9.refs_0_), channel_id=1, source_target_pairs={{0,8},{8,0},{16,24},{24,16},{1,9},{9,1},{17,25},{25,17},{2,10},{10... | collective-permute-start | bytes 172040 | tf_op jit(solution)/shard_map/ppermute | solution.py:273
  26.8 1.2 %collective-permute-start.5 = (f32[1,112,128]{2,1,0:T(8,128)S(1)}, f32[1,112,128]{2,1,0:T(8,128)S(1)}, u32[]{:S(2)}, u32[]{:S(2)}) collective-permute-start(f32[1,112,128]{2,1,0:T(8,128)S(1)} %collective-permute-done.4.refs_1_), channel_id=1, source_target_pairs={{0,8},{8,0},{16,24},{24,16},{1,9},{9,1},{17,25},{25,17},{2,10},{10... | collective-permute-start | bytes 172040 | tf_op jit(solution)/shard_map/ppermute | solution.py:273

commit v8 on v7

--- a/solution.py
+++ b/solution.py
@@ -188,7 +188,7 @@
 def windows_kernel(*refs, plan, order, bands, reach):
     home, here, other, beam_rows, beam_cols, mixing, out, marks, tile = refs
     me = lax.axis_index("tm")
-    mine = lax.axis_index("band") // 2
+    mine = lax.axis_index("band")
     nb, halo = plan.blocks, plan.reach
     ext = TROWS + 2 * reach
     after_rows = ext + 2 * halo * len(order)
@@ -208,15 +208,15 @@
     picks = rows_of(jnp.concatenate(targets, axis=1), (me * TROWS - reach).astype(F32), ext)
     tile[...] = home[...] + other[0:ext, :] + add_rows(picks, jnp.concatenate(blocks, axis=0))
     share = TROWS // bands
-    wide = 2 * share + 2 * reach
+    wide = share + 2 * reach
     terms, taps = beam_rows.shape[1:]
     comps = mixing.shape[0]
     out[...] = jnp.zeros_like(out)
     pad = jnp.zeros((8, L - taps), F32)
     lane = lax.broadcasted_iota(jnp.int32, (8, L), 1)
     turn = jnp.where(lane < taps, taps - 1 - lane, lane)
-    for h in range(bands // 2):
-        start = pl.multiple_of(jnp.bitwise_xor(mine, h) * (2 * share), 8)
+    for h in range(bands):
+        start = pl.multiple_of(jnp.bitwise_xor(mine, h) * share, 8)
         out[h, 0:wide, :] = tile[pl.ds(start, wide), :]
         for k in range(terms):
             out[h, wide + k : wide + k + 1, 0:taps] = beam_rows[0, k : k + 1, :]
@@ -239,20 +239,18 @@
 
 def beam_kernel(*refs, windows, share, reach, terms, comps):
     ins, sofar, out = refs[:windows], refs[windows:-1], refs[-1]
-    core = lax.rem(lax.axis_index("band"), 2)
-    wide = 2 * share + 2 * reach
-    need = share + 2 * reach
+    wide = share + 2 * reach
     x = lax.broadcasted_iota(jnp.int32, (L, L), 0)
     c_in = lax.broadcasted_iota(jnp.int32, (L, L), 1)
     near = jnp.abs(c_in - x) <= reach
     totals = [sofar[0][c, 0] if sofar else None for c in range(comps)]
     for ref in ins:
         for h in range(ref.shape[0]):
-            rows = ref[h, pl.ds(pl.multiple_of(core * share, 8), need), :]
+            rows = ref[h, 0:wide, :]
             mats = []
             for k in range(terms):
                 spread = jnp.broadcast_to(ref[h, wide + k : wide + k + 1, :], (share, L))
-                mats.append(pltpu.roll(spread, 0, 1, stride=1, stride_axis=0)[:, :need])
+                mats.append(pltpu.roll(spread, 0, 1, stride=1, stride_axis=0)[:, :wide])
             rowed = dot3(jnp.concatenate(mats, axis=0), rows, (1, 0))
             for k in range(terms):
                 at = wide + terms + k
@@ -323,19 +321,19 @@
     )(*parts)
     other = flip(away, "tm", 1)
     share = TROWS // bands
-    wide = 2 * share + 2 * reach
+    wide = share + 2 * reach
     extra = -(-(2 * terms + comps * terms) // 8) * 8
     windows = pl.pallas_call(
         functools.partial(windows_kernel, plan=plan, order=order, bands=bands, reach=reach),
-        out_shape=jax.ShapeDtypeStruct((bands // 2, wide + extra, L), F32),
+        out_shape=jax.ShapeDtypeStruct((bands, wide + extra, L), F32),
         in_specs=[VMEM] * 6,
         out_specs=VMEM,
         scratch_shapes=[pltpu.VMEM((16 + tms, L), F32), pltpu.VMEM((ext, L), F32)],
         compiler_params=SMALL,
         name="band_windows",
     )(home, away, other, beam_rows, beam_cols, mixing)
-    own = windows[0:1]
-    across = [flip(windows[h : h + 1], "band", 2 * h) for h in range(1, bands // 2)]
+    half = bands // 2
+    sent = {h: flip(windows[h : h + 1], "band", h) for h in list(range(half, bands)) + list(range(1, half))}
     smooth = functools.partial(beam_kernel, share=share, reach=reach, terms=terms, comps=comps)
 
     def add_beams(windows, *sofar):
@@ -349,9 +347,9 @@
             name="smooth_and_mix",
         )(*windows, *sofar)
 
-    result = add_beams([own])
-    result = add_beams([flip(own, "band", 1)] + across, result)
-    return add_beams([flip(window, "band", 1) for window in across], result)
+    result = add_beams([windows[0:1]] + [sent[h] for h in range(1, half)])
+    result = add_beams([sent[half]], result)
+    return add_beams([sent[h] for h in range(half + 1, bands)], result)
 
 
 def solution(mesh):

time: 29.2 us -> 28.9 us (0.990)
  waiting for transfers between devices: 10.5 us -> 9.82 us
  starting transfers between devices: 8.9 us -> 9.24 us
    ppermute x7, waiting for transfers between devices: 10.5 us -> 9.82 us  [flip(): return lax.ppermute(x, axis, [(i, i ^ bits) for i in range(count)])]
    ppermute x7, starting transfers between devices: 8.9 us -> 9.24 us  [flip(): return lax.ppermute(x, axis, [(i, i ^ bits) for i in range(count)])]
where the time goes in v8:
time: 28.9 us; the launch traced here: 28.8 us
  waiting for transfers between devices  9.82 us (34%)
  starting transfers between devices  9.24 us (32%)
  Pallas kernels  8.87 us (31%)
  between operations  0.71 us (2%)
    ppermute x7, waiting for transfers between devices, flip(): return lax.ppermute(x, axis, [(i, i ^ bits) for i in range(count)])  9.82 us
    ppermute x7, starting transfers between devices, flip(): return lax.ppermute(x, axis, [(i, i ^ bits) for i in range(count)])  9.24 us
    pallas_call x1, Pallas kernels, on_device(): pl.pallas_call(functools.partial(filter_kernel, plan=plan), out_shape=jax...  6.36 us
    pallas_call x3, Pallas kernels, add_beams(): pl.pallas_call(functools.partial(smooth, windows=len(windows)), out_shape...  2.01 us
  transfers between devices with their start and end apart: 7, of which 5 were waited for; matrix products, arithmetic and copies ran while one was open for 0% of the time, Pallas kernels for 3%

profile of v8, /device:TPU:0, one launch (start us, length us, event | category | flops | bytes accessed | tf_op | source)
XLA Modules:
  0.0 28.8 jit_solution(16086343144415923147)
XLA Ops:
  0.7 6.4 %filter_blocks.1.refs_0_ = f32[88,128]{1,0:T(8,128)S(1)} custom-call(f32[1,64]{1,0:T(1,128)} %weights_in.1, bf16[1,64,8192]{2,1,0:T(8,128)(2,1)} %tod.1, bf16[1,64,2049]{2,1,0:T(8,128)(2,1)} %taps_in.1, s32[1,64]{1,0:T(1,128)} %bitcast.1, s32[1,64]{1,0:T(1,128)} %row_in.1, s32[1,1]{1,0:T(1,128)S(6)} %copy.11.counts_in), custom_call_target="tpu_custom_call" | custom-call | tf_op jit(solution)/shard_map/filter_blocks/pallas_call | solution.py:287
  7.0 5.1 %collective-permute-start.2 = (f32[88,128]{1,0:T(8,128)S(1)}, f32[88,128]{1,0:T(8,128)S(1)}, u32[]{:S(2)}, u32[]{:S(2)}) collective-permute-start(f32[88,128]{1,0:T(8,128)S(1)} %filter_blocks.1.refs_0_), channel_id=1, source_target_pairs={{0,6},{1,7},{2,4},{3,5},{4,2},{5,3},{6,0},{7,1},{8,14},{9,15},{10,... | collective-permute-start | bytes 135176 | tf_op jit(solution)/shard_map/ppermute | solution.py:271
  12.1 0.0 collective-permute-start.1
  12.1 0.6 %collective-permute-start = (f32[88,128]{1,0:T(8,128)S(1)}, f32[88,128]{1,0:T(8,128)S(1)}, u32[]{:S(2)}, u32[]{:S(2)}) collective-permute-start(f32[88,128]{1,0:T(8,128)S(1)} %filter_blocks.1.refs_0_), channel_id=1, source_target_pairs={{0,2},{1,3},{2,0},{3,1},{4,6},{5,7},{6,4},{7,5},{8,10},{9,11},{10,... | collective-permute-start | bytes 135176 | tf_op jit(solution)/shard_map/ppermute | solution.py:271
  12.8 1.4 %collective-permute-done.2.refs_3_ = f32[88,128]{1,0:T(8,128)S(1)} collective-permute-done((f32[88,128]{1,0:T(8,128)S(1)}, f32[88,128]{1,0:T(8,128)S(1)}, u32[]{:S(2)}, u32[]{:S(2)}) %collective-permute-start.2) | collective-permute-done | bytes 45088 | tf_op jit(solution)/shard_map/ppermute | solution.py:271
  14.2 2.9 %collective-permute-done.1.refs_2_ = f32[88,128]{1,0:T(8,128)S(1)} collective-permute-done((f32[88,128]{1,0:T(8,128)S(1)}, f32[88,128]{1,0:T(8,128)S(1)}, u32[]{:S(2)}, u32[]{:S(2)}) %collective-permute-start.1) | collective-permute-done | bytes 45088 | tf_op jit(solution)/shard_map/ppermute | solution.py:271
  17.1 0.0 collective-permute-done.refs_1_
  17.1 0.2 tile_rows.1
  17.3 0.0 copy-start.2
  17.3 1.6 %collective-permute-start.3 = (f32[232,128]{1,0:T(8,128)S(1)}, f32[232,128]{1,0:T(8,128)S(1)}, u32[]{:S(2)}, u32[]{:S(2)}) collective-permute-start(f32[232,128]{1,0:T(8,128)S(1)} %get-tuple-element.8.refs_1_), channel_id=1, source_target_pairs={{0,1},{1,0},{2,3},{3,2},{4,5},{5,4},{6,7},{7,6},{8,9},{9,8},{10,11... | collective-permute-start | bytes 356360 | tf_op jit(solution)/shard_map/ppermute | solution.py:271
  18.9 0.0 copy-done.2
  18.9 0.0 copy-start.1
  18.9 0.1 copy.10.refs_5_
  19.0 0.0 copy-start
  19.0 3.2 %collective-permute-done.3.refs_2_ = f32[232,128]{1,0:T(8,128)S(1)} collective-permute-done((f32[232,128]{1,0:T(8,128)S(1)}, f32[232,128]{1,0:T(8,128)S(1)}, u32[]{:S(2)}, u32[]{:S(2)}) %collective-permute-start.3) | collective-permute-done | bytes 118816 | tf_op jit(solution)/shard_map/ppermute | solution.py:271
  22.2 0.0 copy-done.1
  22.2 0.0 copy-done
  22.2 0.3 band_windows.1
  22.5 0.1 collective-permute-start.6
  22.6 1.6 %collective-permute-start.5 = (f32[1,80,128]{2,1,0:T(8,128)S(1)}, f32[1,80,128]{2,1,0:T(8,128)S(1)}, u32[]{:S(2)}, u32[]{:S(2)}) collective-permute-start(f32[1,80,128]{2,1,0:T(8,128)S(1)} %get-tuple-element.11), channel_id=1, source_target_pairs={{0,16},{8,24},{16,0},{24,8},{1,17},{9,25},{17,1},{25,9},{2,18},{10... | collective-permute-start | bytes 122888 | tf_op jit(solution)/shard_map/ppermute | solution.py:271
  24.2 0.3 collective-permute-start.4
  24.5 0.0 collective-permute-done.6.refs_1_
  24.5 0.6 %smooth_and_mix.3.refs_1_ = f32[4,1,32,128]{3,2,1,0:T(8,128)S(1)} custom-call(f32[1,80,128]{2,1,0:T(8,128)S(1)} %get-tuple-element.10.refs_0_, f32[1,80,128]{2,1,0:T(8,128)S(1)} %collective-permute-done.6.refs_1_), custom_call_target="tpu_custom_call" | custom-call | flops 1000000000 | bytes 1000000 | tf_op jit(solution)/shard_map/smooth_and_mix/pallas_call | solution.py:340
  25.0 1.6 %collective-permute-done.5.refs_0_ = f32[1,80,128]{2,1,0:T(8,128)S(1)} collective-permute-done((f32[1,80,128]{2,1,0:T(8,128)S(1)}, f32[1,80,128]{2,1,0:T(8,128)S(1)}, u32[]{:S(2)}, u32[]{:S(2)}) %collective-permute-start.5) | collective-permute-done | bytes 40992 | tf_op jit(solution)/shard_map/ppermute | solution.py:271
  26.7 0.4 %smooth_and_mix.4.refs_1_ = f32[4,1,32,128]{3,2,1,0:T(8,128)S(1)} custom-call(f32[1,80,128]{2,1,0:T(8,128)S(1)} %collective-permute-done.5.refs_0_, f32[4,1,32,128]{3,2,1,0:T(8,128)S(1)} %smooth_and_mix.3.refs_1_), custom_call_target="tpu_custom_call" | custom-call | flops 1000000000 | bytes 1000000 | tf_op jit(solution)/shard_map/smooth_and_mix/pallas_call | solution.py:340
  27.1 0.6 %collective-permute-done.4.refs_0_ = f32[1,80,128]{2,1,0:T(8,128)S(1)} collective-permute-done((f32[1,80,128]{2,1,0:T(8,128)S(1)}, f32[1,80,128]{2,1,0:T(8,128)S(1)}, u32[]{:S(2)}, u32[]{:S(2)}) %collective-permute-start.4) | collective-permute-done | bytes 40992 | tf_op jit(solution)/shard_map/ppermute | solution.py:271
  27.7 1.0 %smooth_and_mix.5 = f32[4,1,32,128]{3,2,1,0:T(8,128)} custom-call(f32[1,80,128]{2,1,0:T(8,128)S(1)} %collective-permute-done.4.refs_0_, f32[4,1,32,128]{3,2,1,0:T(8,128)S(1)} %smooth_and_mix.4.refs_1_), custom_call_target="tpu_custom_call" | custom-call | flops 1000000000 | bytes 1000000 | tf_op jit(solution)/shard_map/smooth_and_mix/pallas_call | solution.py:340
  (1 shorter events, 0.0 us)
Async XLA Ops:
  7.0 7.2 %collective-permute-start.2 = (f32[88,128]{1,0:T(8,128)S(1)}, f32[88,128]{1,0:T(8,128)S(1)}, u32[]{:S(2)}, u32[]{:S(2)}) collective-permute-start(f32[88,128]{1,0:T(8,128)S(1)} %filter_blocks.1.refs_0_), channel_id=1, source_target_pairs={{0,6},{1,7},{2,4},{3,5},{4,2},{5,3},{6,0},{7,1},{8,14},{9,15},{10,... | collective-permute-start | bytes 135176 | tf_op jit(solution)/shard_map/ppermute | solution.py:271
  12.1 4.9 %collective-permute-start.1 = (f32[88,128]{1,0:T(8,128)S(1)}, f32[88,128]{1,0:T(8,128)S(1)}, u32[]{:S(2)}, u32[]{:S(2)}) collective-permute-start(f32[88,128]{1,0:T(8,128)S(1)} %filter_blocks.1.refs_0_), channel_id=1, source_target_pairs={{0,4},{1,5},{2,6},{3,7},{4,0},{5,1},{6,2},{7,3},{8,12},{9,13},{10,... | collective-permute-start | bytes 135176 | tf_op jit(solution)/shard_map/ppermute | solution.py:271
  12.1 4.9 %collective-permute-start = (f32[88,128]{1,0:T(8,128)S(1)}, f32[88,128]{1,0:T(8,128)S(1)}, u32[]{:S(2)}, u32[]{:S(2)}) collective-permute-start(f32[88,128]{1,0:T(8,128)S(1)} %filter_blocks.1.refs_0_), channel_id=1, source_target_pairs={{0,2},{1,3},{2,0},{3,1},{4,6},{5,7},{6,4},{7,5},{8,10},{9,11},{10,... | collective-permute-start | bytes 135176 | tf_op jit(solution)/shard_map/ppermute | solution.py:271
  17.3 1.6 %copy-start.2 = (f32[4,1,2]{0,2,1:T(2,128)S(1)}, f32[4,1,2]{0,2,1:T(2,128)}, u32[]{:S(2)}) copy-start(f32[4,1,2]{0,2,1:T(2,128)} %param.17) | copy-start | bytes 100
  17.3 4.9 %collective-permute-start.3 = (f32[232,128]{1,0:T(8,128)S(1)}, f32[232,128]{1,0:T(8,128)S(1)}, u32[]{:S(2)}, u32[]{:S(2)}) collective-permute-start(f32[232,128]{1,0:T(8,128)S(1)} %get-tuple-element.8.refs_1_), channel_id=1, source_target_pairs={{0,1},{1,0},{2,3},{3,2},{4,5},{5,4},{6,7},{7,6},{8,9},{9,8},{10,11... | collective-permute-start | bytes 356360 | tf_op jit(solution)/shard_map/ppermute | solution.py:271
  18.9 3.3 %copy-start.1 = (f32[1,2,33]{2,1,0:T(2,128)S(1)}, f32[1,2,33]{2,1,0:T(2,128)}, u32[]{:S(2)}) copy-start(f32[1,2,33]{2,1,0:T(2,128)} %refs_4_.1) | copy-start | bytes 796
  19.0 3.3 %copy-start = (f32[1,2,33]{2,1,0:T(2,128)S(1)}, f32[1,2,33]{2,1,0:T(2,128)}, u32[]{:S(2)}) copy-start(f32[1,2,33]{2,1,0:T(2,128)} %refs_3_.1) | copy-start | bytes 796
  22.5 1.9 %collective-permute-start.6 = (f32[1,80,128]{2,1,0:T(8,128)S(1)}, f32[1,80,128]{2,1,0:T(8,128)S(1)}, u32[]{:S(2)}, u32[]{:S(2)}) collective-permute-start(f32[1,80,128]{2,1,0:T(8,128)S(1)} %get-tuple-element.9), channel_id=1, source_target_pairs={{0,8},{8,0},{16,24},{24,16},{1,9},{9,1},{17,25},{25,17},{2,10},{10... | collective-permute-start | bytes 122888 | tf_op jit(solution)/shard_map/ppermute | solution.py:271
  22.6 4.1 %collective-permute-start.5 = (f32[1,80,128]{2,1,0:T(8,128)S(1)}, f32[1,80,128]{2,1,0:T(8,128)S(1)}, u32[]{:S(2)}, u32[]{:S(2)}) collective-permute-start(f32[1,80,128]{2,1,0:T(8,128)S(1)} %get-tuple-element.11), channel_id=1, source_target_pairs={{0,16},{8,24},{16,0},{24,8},{1,17},{9,25},{17,1},{25,9},{2,18},{10... | collective-permute-start | bytes 122888 | tf_op jit(solution)/shard_map/ppermute | solution.py:271
  24.2 3.5 %collective-permute-start.4 = (f32[1,80,128]{2,1,0:T(8,128)S(1)}, f32[1,80,128]{2,1,0:T(8,128)S(1)}, u32[]{:S(2)}, u32[]{:S(2)}) collective-permute-start(f32[1,80,128]{2,1,0:T(8,128)S(1)} %get-tuple-element.12), channel_id=1, source_target_pairs={{0,24},{8,16},{16,8},{24,0},{1,25},{9,17},{17,9},{25,1},{2,26},{10... | collective-permute-start | bytes 122888 | tf_op jit(solution)/shard_map/ppermute | solution.py:271

commit v9 on v8

--- a/solution.py
+++ b/solution.py
@@ -72,6 +72,13 @@
             at = (1 - half) * L
             table[at : at + L, pair * L : (pair + 1) * L] = high
             rest[at : at + L, pair * L : (pair + 1) * L] = turned - high.astype(F32)
+    left = jnp.maximum(jnp.max(jnp.abs(rest[...]), axis=0, keepdims=True), TINY)
+    most = left[:, :nd]
+    for j in range(1, groups):
+        most = jnp.maximum(most, left[:, j * nd : (j + 1) * nd])
+    table8[...] = (rest[...] * jnp.concatenate([TOP / most] * groups, axis=1)).astype(FP8)
+    most = jnp.broadcast_to(jnp.pad(most, ((0, 0), (0, L - nd))), (nd, L))
+    most = jnp.sum(jnp.where(row == lane, most, 0.0), axis=1, keepdims=True)
     last = jnp.broadcast_to(taps[:, groups * BLOCK : groups * BLOCK + 1].astype(F32) * column, (nd, L))
     row8 = lax.broadcasted_iota(jnp.int32, (8, L), 0)
     lane8 = lax.broadcasted_iota(jnp.int32, (8, L), 1)
@@ -81,14 +88,9 @@
     loud = jnp.zeros((nd, BLOCK), BF16)
     for b in range(steps):
         loud = jnp.maximum(loud, jnp.abs(held[(lead + b) * nd : (lead + b + 1) * nd, :]))
-    loud = jnp.maximum(jnp.max(loud.astype(F32), axis=1, keepdims=True), TINY)
-    quiet = jnp.broadcast_to(TOP / loud, (nd, BLOCK))
-    across = jnp.sum(jnp.where(row == lane, jnp.broadcast_to(loud, (nd, L)), 0.0), axis=0, keepdims=True)
-    across = jnp.concatenate([across[:, :nd]] * groups, axis=1)
-    scaled = rest[...] * across
-    largest = jnp.max(jnp.max(jnp.abs(scaled), axis=0, keepdims=True), axis=1, keepdims=True)
-    largest = jnp.maximum(largest, TINY)
-    table8[...] = (scaled * (TOP / largest)).astype(FP8)
+    loud = jnp.max(loud.astype(F32), axis=1, keepdims=True) * most
+    largest = jnp.maximum(jnp.max(loud, axis=0, keepdims=True), TINY)
+    quiet = jnp.broadcast_to(most * (TOP / largest), (nd, BLOCK))
     back = largest * (1.0 / (TOP * TOP))
 
     def shrink(b):
@@ -223,9 +225,9 @@
             profile = jnp.broadcast_to(beam_cols[0, k : k + 1, :], (8, taps))
             turned = jnp.take_along_axis(jnp.concatenate([profile, pad], axis=1), turn, axis=1)
             out[h, wide + terms + k : wide + terms + k + 1, :] = turned[0:1]
-            for c in range(comps):
-                at = wide + 2 * terms + c * terms + k
-                out[h, at : at + 1, :] = jnp.broadcast_to(mixing[c, 0:1, k : k + 1], (1, L))
+        for c in range(comps):
+            at = wide + 2 * terms
+            out[h, at : at + 1, c * terms : (c + 1) * terms] = mixing[c, 0:1, :]
 
 
 def dot3(a, b, dims):
@@ -237,7 +239,9 @@
     return lax.dot_general(left, right, (((ka,), (kb,)), ((), ())), preferred_element_type=F32)
 
 
-def beam_kernel(*refs, windows, share, reach, terms, comps):
+def beam_kernel(*refs, windows, share, reach, terms, comps, last):
+    if last:
+        refs, (stage, sems) = refs[:-2], refs[-2:]
     ins, sofar, out = refs[:windows], refs[windows:-1], refs[-1]
     wide = share + 2 * reach
     x = lax.broadcasted_iota(jnp.int32, (L, L), 0)
@@ -259,11 +263,19 @@
                 cols = jnp.where(near, cols, 0.0)
                 beamed = dot3(rowed[k * share : (k + 1) * share], cols, (1, 0))
                 for c in range(comps):
-                    at = wide + 2 * terms + c * terms + k
-                    part = beamed * ref[h, at : at + 1, :]
+                    at, lane = wide + 2 * terms, c * terms + k
+                    part = beamed * ref[h, at : at + 1, lane : lane + 1]
                     totals[c] = part if totals[c] is None else totals[c] + part
+    if not last:
+        for c in range(comps):
+            out[c, 0] = totals[c]
+        return
+    copies = [pltpu.make_async_copy(stage.at[c], out.at[c, 0], sems.at[c]) for c in range(comps)]
     for c in range(comps):
-        out[c, 0] = totals[c]
+        stage[c] = totals[c]
+        copies[c].start()
+    for copy in copies:
+        copy.wait()
 
 
 def flip(x, axis, bits):
@@ -322,7 +334,7 @@
     other = flip(away, "tm", 1)
     share = TROWS // bands
     wide = share + 2 * reach
-    extra = -(-(2 * terms + comps * terms) // 8) * 8
+    extra = -(-(2 * terms + 1) // 8) * 8
     windows = pl.pallas_call(
         functools.partial(windows_kernel, plan=plan, order=order, bands=bands, reach=reach),
         out_shape=jax.ShapeDtypeStruct((bands, wide + extra, L), F32),
@@ -336,12 +348,13 @@
     sent = {h: flip(windows[h : h + 1], "band", h) for h in list(range(half, bands)) + list(range(1, half))}
     smooth = functools.partial(beam_kernel, share=share, reach=reach, terms=terms, comps=comps)
 
-    def add_beams(windows, *sofar):
+    def add_beams(windows, *sofar, last=False):
         return pl.pallas_call(
-            functools.partial(smooth, windows=len(windows)),
+            functools.partial(smooth, windows=len(windows), last=last),
             out_shape=jax.ShapeDtypeStruct((comps, 1, share, L), F32),
             in_specs=[VMEM] * (len(windows) + len(sofar)),
-            out_specs=VMEM,
+            out_specs=ANY if last else VMEM,
+            scratch_shapes=[pltpu.VMEM((comps, share, L), F32), pltpu.SemaphoreType.DMA((comps,))] if last else [],
             compiler_params=SMALL,
             cost_estimate=pl.CostEstimate(flops=10**9, bytes_accessed=10**6, transcendentals=0),
             name="smooth_and_mix",
@@ -349,7 +362,7 @@
 
     result = add_beams([windows[0:1]] + [sent[h] for h in range(1, half)])
     result = add_beams([sent[half]], result)
-    return add_beams([sent[h] for h in range(half + 1, bands)], result)
+    return add_beams([sent[h] for h in range(half + 1, bands)], result, last=True)
 
 
 def solution(mesh):

time: 28.9 us -> 28.9 us (level)
  no operation moved by 1% of the time
where the time goes in v9:
time: 28.9 us; the launch traced here: 28.7 us
  waiting for transfers between devices  9.71 us (34%)
  starting transfers between devices  9.24 us (32%)
  Pallas kernels  8.93 us (31%)
  between operations  0.71 us (2%)
    ppermute x7, waiting for transfers between devices, flip(): return lax.ppermute(x, axis, [(i, i ^ bits) for i in range(count)])  9.71 us
    ppermute x7, starting transfers between devices, flip(): return lax.ppermute(x, axis, [(i, i ^ bits) for i in range(count)])  9.24 us
    pallas_call x1, Pallas kernels, on_device(): pl.pallas_call(functools.partial(filter_kernel, plan=plan), out_shape=jax...  6.36 us
    pallas_call x3, Pallas kernels, add_beams(): pl.pallas_call(functools.partial(smooth, windows=len(windows), last=last)...  2.06 us
  transfers between devices with their start and end apart: 7, of which 5 were waited for; matrix products, arithmetic and copies ran while one was open for 0% of the time, Pallas kernels for 3%

profile of v9, /device:TPU:0, one launch (start us, length us, event | category | flops | bytes accessed | tf_op | source)
XLA Modules:
  0.0 28.7 jit_solution(17571074936584802832)
XLA Ops:
  0.7 6.4 %filter_blocks.1.refs_0_ = f32[88,128]{1,0:T(8,128)S(1)} custom-call(f32[1,64]{1,0:T(1,128)} %weights_in.1, bf16[1,64,8192]{2,1,0:T(8,128)(2,1)} %tod.1, bf16[1,64,2049]{2,1,0:T(8,128)(2,1)} %taps_in.1, s32[1,64]{1,0:T(1,128)} %bitcast.1, s32[1,64]{1,0:T(1,128)} %row_in.1, s32[1,1]{1,0:T(1,128)S(6)} %copy.11.counts_in), custom_call_target="tpu_custom_call" | custom-call | tf_op jit(solution)/shard_map/filter_blocks/pallas_call | solution.py:299
  7.0 5.1 %collective-permute-start.2 = (f32[88,128]{1,0:T(8,128)S(1)}, f32[88,128]{1,0:T(8,128)S(1)}, u32[]{:S(2)}, u32[]{:S(2)}) collective-permute-start(f32[88,128]{1,0:T(8,128)S(1)} %filter_blocks.1.refs_0_), channel_id=1, source_target_pairs={{0,6},{1,7},{2,4},{3,5},{4,2},{5,3},{6,0},{7,1},{8,14},{9,15},{10,... | collective-permute-start | bytes 135176 | tf_op jit(solution)/shard_map/ppermute | solution.py:283
  12.1 0.0 collective-permute-start.1
  12.1 0.6 %collective-permute-start = (f32[88,128]{1,0:T(8,128)S(1)}, f32[88,128]{1,0:T(8,128)S(1)}, u32[]{:S(2)}, u32[]{:S(2)}) collective-permute-start(f32[88,128]{1,0:T(8,128)S(1)} %filter_blocks.1.refs_0_), channel_id=1, source_target_pairs={{0,2},{1,3},{2,0},{3,1},{4,6},{5,7},{6,4},{7,5},{8,10},{9,11},{10,... | collective-permute-start | bytes 135176 | tf_op jit(solution)/shard_map/ppermute | solution.py:283
  12.8 1.4 %collective-permute-done.2.refs_3_ = f32[88,128]{1,0:T(8,128)S(1)} collective-permute-done((f32[88,128]{1,0:T(8,128)S(1)}, f32[88,128]{1,0:T(8,128)S(1)}, u32[]{:S(2)}, u32[]{:S(2)}) %collective-permute-start.2) | collective-permute-done | bytes 45088 | tf_op jit(solution)/shard_map/ppermute | solution.py:283
  14.2 2.9 %collective-permute-done.1.refs_2_ = f32[88,128]{1,0:T(8,128)S(1)} collective-permute-done((f32[88,128]{1,0:T(8,128)S(1)}, f32[88,128]{1,0:T(8,128)S(1)}, u32[]{:S(2)}, u32[]{:S(2)}) %collective-permute-start.1) | collective-permute-done | bytes 45088 | tf_op jit(solution)/shard_map/ppermute | solution.py:283
  17.1 0.0 collective-permute-done.refs_1_
  17.1 0.2 tile_rows.1
  17.3 0.0 copy-start.2
  17.3 1.6 %collective-permute-start.3 = (f32[232,128]{1,0:T(8,128)S(1)}, f32[232,128]{1,0:T(8,128)S(1)}, u32[]{:S(2)}, u32[]{:S(2)}) collective-permute-start(f32[232,128]{1,0:T(8,128)S(1)} %get-tuple-element.8.refs_1_), channel_id=1, source_target_pairs={{0,1},{1,0},{2,3},{3,2},{4,5},{5,4},{6,7},{7,6},{8,9},{9,8},{10,11... | collective-permute-start | bytes 356360 | tf_op jit(solution)/shard_map/ppermute | solution.py:283
  18.9 0.0 copy-done.2
  18.9 0.0 copy-start.1
  18.9 0.1 copy.10.refs_5_
  19.0 0.0 copy-start
  19.0 3.2 %collective-permute-done.3.refs_2_ = f32[232,128]{1,0:T(8,128)S(1)} collective-permute-done((f32[232,128]{1,0:T(8,128)S(1)}, f32[232,128]{1,0:T(8,128)S(1)}, u32[]{:S(2)}, u32[]{:S(2)}) %collective-permute-start.3) | collective-permute-done | bytes 118816 | tf_op jit(solution)/shard_map/ppermute | solution.py:283
  22.2 0.0 copy-done.1
  22.2 0.0 copy-done
  22.3 0.3 band_windows.1
  22.5 0.1 collective-permute-start.6
  22.6 1.6 %collective-permute-start.5 = (f32[1,72,128]{2,1,0:T(8,128)S(1)}, f32[1,72,128]{2,1,0:T(8,128)S(1)}, u32[]{:S(2)}, u32[]{:S(2)}) collective-permute-start(f32[1,72,128]{2,1,0:T(8,128)S(1)} %get-tuple-element.11), channel_id=1, source_target_pairs={{0,16},{8,24},{16,0},{24,8},{1,17},{9,25},{17,1},{25,9},{2,18},{10... | collective-permute-start | bytes 110600 | tf_op jit(solution)/shard_map/ppermute | solution.py:283
  24.2 0.3 collective-permute-start.4
  24.5 0.0 collective-permute-done.6.refs_1_
  24.5 0.6 %smooth_and_mix.3.refs_1_ = f32[4,1,32,128]{3,2,1,0:T(8,128)S(1)} custom-call(f32[1,72,128]{2,1,0:T(8,128)S(1)} %get-tuple-element.10.refs_0_, f32[1,72,128]{2,1,0:T(8,128)S(1)} %collective-permute-done.6.refs_1_), custom_call_target="tpu_custom_call" | custom-call | flops 1000000000 | bytes 1000000 | tf_op jit(solution)/shard_map/smooth_and_mix/pallas_call | solution.py:352
  25.1 1.6 %collective-permute-done.5.refs_0_ = f32[1,72,128]{2,1,0:T(8,128)S(1)} collective-permute-done((f32[1,72,128]{2,1,0:T(8,128)S(1)}, f32[1,72,128]{2,1,0:T(8,128)S(1)}, u32[]{:S(2)}, u32[]{:S(2)}) %collective-permute-start.5) | collective-permute-done | bytes 36896 | tf_op jit(solution)/shard_map/ppermute | solution.py:283
  26.6 0.4 %smooth_and_mix.4.refs_1_ = f32[4,1,32,128]{3,2,1,0:T(8,128)S(1)} custom-call(f32[1,72,128]{2,1,0:T(8,128)S(1)} %collective-permute-done.5.refs_0_, f32[4,1,32,128]{3,2,1,0:T(8,128)S(1)} %smooth_and_mix.3.refs_1_), custom_call_target="tpu_custom_call" | custom-call | flops 1000000000 | bytes 1000000 | tf_op jit(solution)/shard_map/smooth_and_mix/pallas_call | solution.py:352
  27.1 0.6 %collective-permute-done.4.refs_0_ = f32[1,72,128]{2,1,0:T(8,128)S(1)} collective-permute-done((f32[1,72,128]{2,1,0:T(8,128)S(1)}, f32[1,72,128]{2,1,0:T(8,128)S(1)}, u32[]{:S(2)}, u32[]{:S(2)}) %collective-permute-start.4) | collective-permute-done | bytes 36896 | tf_op jit(solution)/shard_map/ppermute | solution.py:283
  27.6 1.1 %smooth_and_mix.5 = f32[4,1,32,128]{3,2,1,0:T(8,128)} custom-call(f32[1,72,128]{2,1,0:T(8,128)S(1)} %collective-permute-done.4.refs_0_, f32[4,1,32,128]{3,2,1,0:T(8,128)S(1)} %smooth_and_mix.4.refs_1_), custom_call_target="tpu_custom_call" | custom-call | flops 1000000000 | bytes 1000000 | tf_op jit(solution)/shard_map/smooth_and_mix/pallas_call | solution.py:352
  (1 shorter events, 0.0 us)
Async XLA Ops:
  7.0 7.2 %collective-permute-start.2 = (f32[88,128]{1,0:T(8,128)S(1)}, f32[88,128]{1,0:T(8,128)S(1)}, u32[]{:S(2)}, u32[]{:S(2)}) collective-permute-start(f32[88,128]{1,0:T(8,128)S(1)} %filter_blocks.1.refs_0_), channel_id=1, source_target_pairs={{0,6},{1,7},{2,4},{3,5},{4,2},{5,3},{6,0},{7,1},{8,14},{9,15},{10,... | collective-permute-start | bytes 135176 | tf_op jit(solution)/shard_map/ppermute | solution.py:283
  12.1 4.9 %collective-permute-start.1 = (f32[88,128]{1,0:T(8,128)S(1)}, f32[88,128]{1,0:T(8,128)S(1)}, u32[]{:S(2)}, u32[]{:S(2)}) collective-permute-start(f32[88,128]{1,0:T(8,128)S(1)} %filter_blocks.1.refs_0_), channel_id=1, source_target_pairs={{0,4},{1,5},{2,6},{3,7},{4,0},{5,1},{6,2},{7,3},{8,12},{9,13},{10,... | collective-permute-start | bytes 135176 | tf_op jit(solution)/shard_map/ppermute | solution.py:283
  12.1 4.9 %collective-permute-start = (f32[88,128]{1,0:T(8,128)S(1)}, f32[88,128]{1,0:T(8,128)S(1)}, u32[]{:S(2)}, u32[]{:S(2)}) collective-permute-start(f32[88,128]{1,0:T(8,128)S(1)} %filter_blocks.1.refs_0_), channel_id=1, source_target_pairs={{0,2},{1,3},{2,0},{3,1},{4,6},{5,7},{6,4},{7,5},{8,10},{9,11},{10,... | collective-permute-start | bytes 135176 | tf_op jit(solution)/shard_map/ppermute | solution.py:283
  17.3 1.6 %copy-start.2 = (f32[4,1,2]{0,2,1:T(2,128)S(1)}, f32[4,1,2]{0,2,1:T(2,128)}, u32[]{:S(2)}) copy-start(f32[4,1,2]{0,2,1:T(2,128)} %param.17) | copy-start | bytes 100
  17.3 4.9 %collective-permute-start.3 = (f32[232,128]{1,0:T(8,128)S(1)}, f32[232,128]{1,0:T(8,128)S(1)}, u32[]{:S(2)}, u32[]{:S(2)}) collective-permute-start(f32[232,128]{1,0:T(8,128)S(1)} %get-tuple-element.8.refs_1_), channel_id=1, source_target_pairs={{0,1},{1,0},{2,3},{3,2},{4,5},{5,4},{6,7},{7,6},{8,9},{9,8},{10,11... | collective-permute-start | bytes 356360 | tf_op jit(solution)/shard_map/ppermute | solution.py:283
  18.9 3.3 %copy-start.1 = (f32[1,2,33]{2,1,0:T(2,128)S(1)}, f32[1,2,33]{2,1,0:T(2,128)}, u32[]{:S(2)}) copy-start(f32[1,2,33]{2,1,0:T(2,128)} %refs_4_.1) | copy-start | bytes 796
  19.0 3.3 %copy-start = (f32[1,2,33]{2,1,0:T(2,128)S(1)}, f32[1,2,33]{2,1,0:T(2,128)}, u32[]{:S(2)}) copy-start(f32[1,2,33]{2,1,0:T(2,128)} %refs_3_.1) | copy-start | bytes 796
  22.5 1.9 %collective-permute-start.6 = (f32[1,72,128]{2,1,0:T(8,128)S(1)}, f32[1,72,128]{2,1,0:T(8,128)S(1)}, u32[]{:S(2)}, u32[]{:S(2)}) collective-permute-start(f32[1,72,128]{2,1,0:T(8,128)S(1)} %get-tuple-element.9), channel_id=1, source_target_pairs={{0,8},{8,0},{16,24},{24,16},{1,9},{9,1},{17,25},{25,17},{2,10},{10... | collective-permute-start | bytes 110600 | tf_op jit(solution)/shard_map/ppermute | solution.py:283
  22.6 4.0 %collective-permute-start.5 = (f32[1,72,128]{2,1,0:T(8,128)S(1)}, f32[1,72,128]{2,1,0:T(8,128)S(1)}, u32[]{:S(2)}, u32[]{:S(2)}) collective-permute-start(f32[1,72,128]{2,1,0:T(8,128)S(1)} %get-tuple-element.11), channel_id=1, source_target_pairs={{0,16},{8,24},{16,0},{24,8},{1,17},{9,25},{17,1},{25,9},{2,18},{10... | collective-permute-start | bytes 110600 | tf_op jit(solution)/shard_map/ppermute | solution.py:283
  24.2 3.4 %collective-permute-start.4 = (f32[1,72,128]{2,1,0:T(8,128)S(1)}, f32[1,72,128]{2,1,0:T(8,128)S(1)}, u32[]{:S(2)}, u32[]{:S(2)}) collective-permute-start(f32[1,72,128]{2,1,0:T(8,128)S(1)} %get-tuple-element.12), channel_id=1, source_target_pairs={{0,24},{8,16},{16,8},{24,0},{1,25},{9,17},{17,9},{25,1},{2,26},{10... | collective-permute-start | bytes 110600 | tf_op jit(solution)/shard_map/ppermute | solution.py:283

commit v10 on v9

--- a/solution.py
+++ b/solution.py
@@ -239,9 +239,7 @@
     return lax.dot_general(left, right, (((ka,), (kb,)), ((), ())), preferred_element_type=F32)
 
 
-def beam_kernel(*refs, windows, share, reach, terms, comps, last):
-    if last:
-        refs, (stage, sems) = refs[:-2], refs[-2:]
+def beam_kernel(*refs, windows, share, reach, terms, comps):
     ins, sofar, out = refs[:windows], refs[windows:-1], refs[-1]
     wide = share + 2 * reach
     x = lax.broadcasted_iota(jnp.int32, (L, L), 0)
@@ -266,16 +264,8 @@
                     at, lane = wide + 2 * terms, c * terms + k
                     part = beamed * ref[h, at : at + 1, lane : lane + 1]
                     totals[c] = part if totals[c] is None else totals[c] + part
-    if not last:
-        for c in range(comps):
-            out[c, 0] = totals[c]
-        return
-    copies = [pltpu.make_async_copy(stage.at[c], out.at[c, 0], sems.at[c]) for c in range(comps)]
     for c in range(comps):
-        stage[c] = totals[c]
-        copies[c].start()
-    for copy in copies:
-        copy.wait()
+        out[c, 0] = totals[c]
 
 
 def flip(x, axis, bits):
@@ -348,13 +338,12 @@
     sent = {h: flip(windows[h : h + 1], "band", h) for h in list(range(half, bands)) + list(range(1, half))}
     smooth = functools.partial(beam_kernel, share=share, reach=reach, terms=terms, comps=comps)
 
-    def add_beams(windows, *sofar, last=False):
+    def add_beams(windows, *sofar):
         return pl.pallas_call(
-            functools.partial(smooth, windows=len(windows), last=last),
+            functools.partial(smooth, windows=len(windows)),
             out_shape=jax.ShapeDtypeStruct((comps, 1, share, L), F32),
             in_specs=[VMEM] * (len(windows) + len(sofar)),
-            out_specs=ANY if last else VMEM,
-            scratch_shapes=[pltpu.VMEM((comps, share, L), F32), pltpu.SemaphoreType.DMA((comps,))] if last else [],
+            out_specs=VMEM,
             compiler_params=SMALL,
             cost_estimate=pl.CostEstimate(flops=10**9, bytes_accessed=10**6, transcendentals=0),
             name="smooth_and_mix",
@@ -362,7 +351,7 @@
 
     result = add_beams([windows[0:1]] + [sent[h] for h in range(1, half)])
     result = add_beams([sent[half]], result)
-    return add_beams([sent[h] for h in range(half + 1, bands)], result, last=True)
+    return add_beams([sent[h] for h in range(half + 1, bands)], result)
 
 
 def solution(mesh):

time: 28.9 us -> 28.8 us (level)
  no operation moved by 1% of the time
where the time goes in v10:
time: 28.8 us; the launch traced here: 28.7 us
  waiting for transfers between devices  9.71 us (34%)
  starting transfers between devices  9.24 us (32%)
  Pallas kernels  8.9 us (31%)
  between operations  0.71 us (2%)
    ppermute x7, waiting for transfers between devices, flip(): return lax.ppermute(x, axis, [(i, i ^ bits) for i in range(count)])  9.71 us
    ppermute x7, starting transfers between devices, flip(): return lax.ppermute(x, axis, [(i, i ^ bits) for i in range(count)])  9.24 us
    pallas_call x1, Pallas kernels, on_device(): pl.pallas_call(functools.partial(filter_kernel, plan=plan), out_shape=jax...  6.36 us
    pallas_call x3, Pallas kernels, add_beams(): pl.pallas_call(functools.partial(smooth, windows=len(windows)), out_shape...  2.04 us
  transfers between devices with their start and end apart: 7, of which 5 were waited for; matrix products, arithmetic and copies ran while one was open for 0% of the time, Pallas kernels for 3%

profile of v10, /device:TPU:0, one launch (start us, length us, event | category | flops | bytes accessed | tf_op | source)
XLA Modules:
  0.0 28.7 jit_solution(11208377604056286107)
XLA Ops:
  0.7 6.4 %filter_blocks.1.refs_0_ = f32[88,128]{1,0:T(8,128)S(1)} custom-call(f32[1,64]{1,0:T(1,128)} %weights_in.1, bf16[1,64,8192]{2,1,0:T(8,128)(2,1)} %tod.1, bf16[1,64,2049]{2,1,0:T(8,128)(2,1)} %taps_in.1, s32[1,64]{1,0:T(1,128)} %bitcast.1, s32[1,64]{1,0:T(1,128)} %row_in.1, s32[1,1]{1,0:T(1,128)S(6)} %copy.11.counts_in), custom_call_target="tpu_custom_call" | custom-call | tf_op jit(solution)/shard_map/filter_blocks/pallas_call | solution.py:289
  7.0 5.1 %collective-permute-start.2 = (f32[88,128]{1,0:T(8,128)S(1)}, f32[88,128]{1,0:T(8,128)S(1)}, u32[]{:S(2)}, u32[]{:S(2)}) collective-permute-start(f32[88,128]{1,0:T(8,128)S(1)} %filter_blocks.1.refs_0_), channel_id=1, source_target_pairs={{0,6},{1,7},{2,4},{3,5},{4,2},{5,3},{6,0},{7,1},{8,14},{9,15},{10,... | collective-permute-start | bytes 135176 | tf_op jit(solution)/shard_map/ppermute | solution.py:273
  12.1 0.0 collective-permute-start.1
  12.1 0.6 %collective-permute-start = (f32[88,128]{1,0:T(8,128)S(1)}, f32[88,128]{1,0:T(8,128)S(1)}, u32[]{:S(2)}, u32[]{:S(2)}) collective-permute-start(f32[88,128]{1,0:T(8,128)S(1)} %filter_blocks.1.refs_0_), channel_id=1, source_target_pairs={{0,2},{1,3},{2,0},{3,1},{4,6},{5,7},{6,4},{7,5},{8,10},{9,11},{10,... | collective-permute-start | bytes 135176 | tf_op jit(solution)/shard_map/ppermute | solution.py:273
  12.8 1.4 %collective-permute-done.2.refs_3_ = f32[88,128]{1,0:T(8,128)S(1)} collective-permute-done((f32[88,128]{1,0:T(8,128)S(1)}, f32[88,128]{1,0:T(8,128)S(1)}, u32[]{:S(2)}, u32[]{:S(2)}) %collective-permute-start.2) | collective-permute-done | bytes 45088 | tf_op jit(solution)/shard_map/ppermute | solution.py:273
  14.2 2.9 %collective-permute-done.1.refs_2_ = f32[88,128]{1,0:T(8,128)S(1)} collective-permute-done((f32[88,128]{1,0:T(8,128)S(1)}, f32[88,128]{1,0:T(8,128)S(1)}, u32[]{:S(2)}, u32[]{:S(2)}) %collective-permute-start.1) | collective-permute-done | bytes 45088 | tf_op jit(solution)/shard_map/ppermute | solution.py:273
  17.1 0.0 collective-permute-done.refs_1_
  17.1 0.2 tile_rows.1
  17.3 0.0 copy-start.2
  17.3 1.6 %collective-permute-start.3 = (f32[232,128]{1,0:T(8,128)S(1)}, f32[232,128]{1,0:T(8,128)S(1)}, u32[]{:S(2)}, u32[]{:S(2)}) collective-permute-start(f32[232,128]{1,0:T(8,128)S(1)} %get-tuple-element.8.refs_1_), channel_id=1, source_target_pairs={{0,1},{1,0},{2,3},{3,2},{4,5},{5,4},{6,7},{7,6},{8,9},{9,8},{10,11... | collective-permute-start | bytes 356360 | tf_op jit(solution)/shard_map/ppermute | solution.py:273
  18.9 0.0 copy-done.2
  18.9 0.0 copy-start.1
  18.9 0.1 copy.10.refs_5_
  19.0 0.0 copy-start
  19.0 3.2 %collective-permute-done.3.refs_2_ = f32[232,128]{1,0:T(8,128)S(1)} collective-permute-done((f32[232,128]{1,0:T(8,128)S(1)}, f32[232,128]{1,0:T(8,128)S(1)}, u32[]{:S(2)}, u32[]{:S(2)}) %collective-permute-start.3) | collective-permute-done | bytes 118816 | tf_op jit(solution)/shard_map/ppermute | solution.py:273
  22.2 0.0 copy-done.1
  22.2 0.0 copy-done
  22.3 0.3 band_windows.1
  22.5 0.1 collective-permute-start.6
  22.6 1.6 %collective-permute-start.5 = (f32[1,72,128]{2,1,0:T(8,128)S(1)}, f32[1,72,128]{2,1,0:T(8,128)S(1)}, u32[]{:S(2)}, u32[]{:S(2)}) collective-permute-start(f32[1,72,128]{2,1,0:T(8,128)S(1)} %get-tuple-element.11), channel_id=1, source_target_pairs={{0,16},{8,24},{16,0},{24,8},{1,17},{9,25},{17,1},{25,9},{2,18},{10... | collective-permute-start | bytes 110600 | tf_op jit(solution)/shard_map/ppermute | solution.py:273
  24.2 0.3 collective-permute-start.4
  24.5 0.0 collective-permute-done.6.refs_1_
  24.5 0.6 %smooth_and_mix.3.refs_1_ = f32[4,1,32,128]{3,2,1,0:T(8,128)S(1)} custom-call(f32[1,72,128]{2,1,0:T(8,128)S(1)} %get-tuple-element.10.refs_0_, f32[1,72,128]{2,1,0:T(8,128)S(1)} %collective-permute-done.6.refs_1_), custom_call_target="tpu_custom_call" | custom-call | flops 1000000000 | bytes 1000000 | tf_op jit(solution)/shard_map/smooth_and_mix/pallas_call | solution.py:342
  25.1 1.6 %collective-permute-done.5.refs_0_ = f32[1,72,128]{2,1,0:T(8,128)S(1)} collective-permute-done((f32[1,72,128]{2,1,0:T(8,128)S(1)}, f32[1,72,128]{2,1,0:T(8,128)S(1)}, u32[]{:S(2)}, u32[]{:S(2)}) %collective-permute-start.5) | collective-permute-done | bytes 36896 | tf_op jit(solution)/shard_map/ppermute | solution.py:273
  26.6 0.4 %smooth_and_mix.4.refs_1_ = f32[4,1,32,128]{3,2,1,0:T(8,128)S(1)} custom-call(f32[1,72,128]{2,1,0:T(8,128)S(1)} %collective-permute-done.5.refs_0_, f32[4,1,32,128]{3,2,1,0:T(8,128)S(1)} %smooth_and_mix.3.refs_1_), custom_call_target="tpu_custom_call" | custom-call | flops 1000000000 | bytes 1000000 | tf_op jit(solution)/shard_map/smooth_and_mix/pallas_call | solution.py:342
  27.1 0.6 %collective-permute-done.4.refs_0_ = f32[1,72,128]{2,1,0:T(8,128)S(1)} collective-permute-done((f32[1,72,128]{2,1,0:T(8,128)S(1)}, f32[1,72,128]{2,1,0:T(8,128)S(1)}, u32[]{:S(2)}, u32[]{:S(2)}) %collective-permute-start.4) | collective-permute-done | bytes 36896 | tf_op jit(solution)/shard_map/ppermute | solution.py:273
  27.6 1.0 %smooth_and_mix.5 = f32[4,1,32,128]{3,2,1,0:T(8,128)} custom-call(f32[1,72,128]{2,1,0:T(8,128)S(1)} %collective-permute-done.4.refs_0_, f32[4,1,32,128]{3,2,1,0:T(8,128)S(1)} %smooth_and_mix.4.refs_1_), custom_call_target="tpu_custom_call" | custom-call | flops 1000000000 | bytes 1000000 | tf_op jit(solution)/shard_map/smooth_and_mix/pallas_call | solution.py:342
  (1 shorter events, 0.0 us)
Async XLA Ops:
  7.0 7.2 %collective-permute-start.2 = (f32[88,128]{1,0:T(8,128)S(1)}, f32[88,128]{1,0:T(8,128)S(1)}, u32[]{:S(2)}, u32[]{:S(2)}) collective-permute-start(f32[88,128]{1,0:T(8,128)S(1)} %filter_blocks.1.refs_0_), channel_id=1, source_target_pairs={{0,6},{1,7},{2,4},{3,5},{4,2},{5,3},{6,0},{7,1},{8,14},{9,15},{10,... | collective-permute-start | bytes 135176 | tf_op jit(solution)/shard_map/ppermute | solution.py:273
  12.1 4.9 %collective-permute-start.1 = (f32[88,128]{1,0:T(8,128)S(1)}, f32[88,128]{1,0:T(8,128)S(1)}, u32[]{:S(2)}, u32[]{:S(2)}) collective-permute-start(f32[88,128]{1,0:T(8,128)S(1)} %filter_blocks.1.refs_0_), channel_id=1, source_target_pairs={{0,4},{1,5},{2,6},{3,7},{4,0},{5,1},{6,2},{7,3},{8,12},{9,13},{10,... | collective-permute-start | bytes 135176 | tf_op jit(solution)/shard_map/ppermute | solution.py:273
  12.1 4.9 %collective-permute-start = (f32[88,128]{1,0:T(8,128)S(1)}, f32[88,128]{1,0:T(8,128)S(1)}, u32[]{:S(2)}, u32[]{:S(2)}) collective-permute-start(f32[88,128]{1,0:T(8,128)S(1)} %filter_blocks.1.refs_0_), channel_id=1, source_target_pairs={{0,2},{1,3},{2,0},{3,1},{4,6},{5,7},{6,4},{7,5},{8,10},{9,11},{10,... | collective-permute-start | bytes 135176 | tf_op jit(solution)/shard_map/ppermute | solution.py:273
  17.3 1.6 %copy-start.2 = (f32[4,1,2]{0,2,1:T(2,128)S(1)}, f32[4,1,2]{0,2,1:T(2,128)}, u32[]{:S(2)}) copy-start(f32[4,1,2]{0,2,1:T(2,128)} %param.17) | copy-start | bytes 100
  17.3 4.9 %collective-permute-start.3 = (f32[232,128]{1,0:T(8,128)S(1)}, f32[232,128]{1,0:T(8,128)S(1)}, u32[]{:S(2)}, u32[]{:S(2)}) collective-permute-start(f32[232,128]{1,0:T(8,128)S(1)} %get-tuple-element.8.refs_1_), channel_id=1, source_target_pairs={{0,1},{1,0},{2,3},{3,2},{4,5},{5,4},{6,7},{7,6},{8,9},{9,8},{10,11... | collective-permute-start | bytes 356360 | tf_op jit(solution)/shard_map/ppermute | solution.py:273
  18.9 3.3 %copy-start.1 = (f32[1,2,33]{2,1,0:T(2,128)S(1)}, f32[1,2,33]{2,1,0:T(2,128)}, u32[]{:S(2)}) copy-start(f32[1,2,33]{2,1,0:T(2,128)} %refs_4_.1) | copy-start | bytes 796
  19.0 3.3 %copy-start = (f32[1,2,33]{2,1,0:T(2,128)S(1)}, f32[1,2,33]{2,1,0:T(2,128)}, u32[]{:S(2)}) copy-start(f32[1,2,33]{2,1,0:T(2,128)} %refs_3_.1) | copy-start | bytes 796
  22.5 1.9 %collective-permute-start.6 = (f32[1,72,128]{2,1,0:T(8,128)S(1)}, f32[1,72,128]{2,1,0:T(8,128)S(1)}, u32[]{:S(2)}, u32[]{:S(2)}) collective-permute-start(f32[1,72,128]{2,1,0:T(8,128)S(1)} %get-tuple-element.9), channel_id=1, source_target_pairs={{0,8},{8,0},{16,24},{24,16},{1,9},{9,1},{17,25},{25,17},{2,10},{10... | collective-permute-start | bytes 110600 | tf_op jit(solution)/shard_map/ppermute | solution.py:273
  22.6 4.0 %collective-permute-start.5 = (f32[1,72,128]{2,1,0:T(8,128)S(1)}, f32[1,72,128]{2,1,0:T(8,128)S(1)}, u32[]{:S(2)}, u32[]{:S(2)}) collective-permute-start(f32[1,72,128]{2,1,0:T(8,128)S(1)} %get-tuple-element.11), channel_id=1, source_target_pairs={{0,16},{8,24},{16,0},{24,8},{1,17},{9,25},{17,1},{25,9},{2,18},{10... | collective-permute-start | bytes 110600 | tf_op jit(solution)/shard_map/ppermute | solution.py:273
  24.2 3.4 %collective-permute-start.4 = (f32[1,72,128]{2,1,0:T(8,128)S(1)}, f32[1,72,128]{2,1,0:T(8,128)S(1)}, u32[]{:S(2)}, u32[]{:S(2)}) collective-permute-start(f32[1,72,128]{2,1,0:T(8,128)S(1)} %get-tuple-element.12), channel_id=1, source_target_pairs={{0,24},{8,16},{16,8},{24,0},{1,25},{9,17},{17,9},{25,1},{2,26},{10... | collective-permute-start | bytes 110600 | tf_op jit(solution)/shard_map/ppermute | solution.py:273
